TPU v7x, 256 devices: a whole 4x4x8 slice. The times are simulated.
256 devices in a mesh: section: 4 (over x), ctx: 64 (over y, z, core).
Axes of the slice: x: 4, y: 4, z: 8, core: 2. Of those that a mesh axis runs over, the one named last changes fastest.
Arguments:
- queries: bfloat16 [32768, 4096], P(('section', 'ctx')), may hold values from -40 to 40
- keys: bfloat16 [32768, 512], P(('section', 'ctx')), may hold values from -6 to 6
- values: bfloat16 [32768, 512], P(('section', 'ctx')), may hold values from -6 to 6
- keep_index: int32 [256, 4, 8], P(('section', 'ctx')), may hold values from 0 to 127, as said below
Outputs:
- attended: bfloat16 [32768, 4096], P(('section', 'ctx'))
Inputs may be any that keep to these rules, and one draw needn't show every extreme that they name: `keep_index`: for each block and key and value head, 8 distinct positions in increasing order.
All inputs are finite; a program needn't handle non-finite values.
Results may differ from a plain program's by a relative error of at most 0.0085.
Values may be sent and summed in bfloat16 or wider, within the bound.
No kernel may reach another device: no remote copies, remote signals or barrier semaphores. Data moves between devices by JAX's collectives and lax.ppermute only.
A program may use at most 128 MiB of HBM per device.

v0:
```python
import math

import jax
import jax.numpy as jnp
from jax import lax
from jax.sharding import PartitionSpec as P

QH = 32
KVH = 4
HD = 128


very_negative = -1e30


def from_root(shard, axis, root):
    mine = lax.axis_index(axis) == root
    return lax.psum(jnp.where(mine, shard, jnp.zeros_like(shard)), axis)


def empty_state(rows_here, group_size):
    return (
        jnp.full((rows_here, KVH, group_size), very_negative, jnp.float32),
        jnp.zeros((rows_here, KVH, group_size), jnp.float32),
        jnp.zeros((rows_here, KVH, group_size, HD), jnp.float32),
    )


def absorb(running, scores, allowed, value_rows):
    highest, total, summed = running
    masked = jnp.where(allowed, scores, very_negative)
    new_highest = jnp.maximum(highest, jnp.max(masked, axis=-1))
    weights = jnp.where(allowed, jnp.exp(masked - new_highest[..., None]), 0.0)
    total = jnp.sum(weights, axis=-1)
    summed = jnp.einsum(
        "tkgs,skd->tkgd",
        weights.astype(jnp.bfloat16),
        value_rows,
        preferred_element_type=jnp.float32,
    )
    return (new_highest, total, summed)


def join(first, second):
    highest = jnp.maximum(first[0], second[0])
    first_scale = jnp.exp(first[0] - highest)
    second_scale = jnp.exp(second[0] - highest)
    total = first[1] * first_scale + second[1] * second_scale
    summed = first[2] * first_scale[..., None] + second[2] * second_scale[..., None]
    return (highest, total, summed)


def on_device(queries, keys, values, keep_index):
    rows_here = queries.shape[0]
    group_size = QH // KVH
    score_scale = 1.0 / math.sqrt(HD)
    host = lax.axis_index("section") * lax.axis_size("ctx") + lax.axis_index("ctx")
    query_heads = queries.reshape(rows_here, KVH, group_size, HD)
    key_heads = keys.reshape(rows_here, KVH, HD)
    value_heads = values.reshape(rows_here, KVH, HD)
    start_state = empty_state(rows_here, group_size)
    chosen = keep_index[0]
    kept_keys = jnp.take_along_axis(
        jnp.transpose(key_heads, (1, 0, 2)), chosen[:, :, None], axis=1
    )[None]
    kept_values = jnp.take_along_axis(
        jnp.transpose(value_heads, (1, 0, 2)), chosen[:, :, None], axis=1
    )[None]
    block_keys = lax.all_gather(kept_keys, ("section", "ctx"), axis=0, tiled=True)
    block_values = lax.all_gather(kept_values, ("section", "ctx"), axis=0, tiled=True)
    count = block_keys.shape[0]
    kept_count = block_keys.shape[2]
    host_ids = jnp.arange(count, dtype=jnp.int32)
    usable = (host_ids >= 1) & (host_ids < host)
    scores = (
        jnp.einsum("tkgd,nksd->tkgns", query_heads, block_keys, preferred_element_type=jnp.float32)
        * score_scale
    )
    scores = scores.reshape(rows_here, KVH, group_size, count * kept_count)
    allowed = jnp.repeat(usable, kept_count)[None, None, None, :]
    value_rows = jnp.transpose(block_values, (0, 2, 1, 3)).reshape(count * kept_count, KVH, HD)
    far_state = absorb(start_state, scores, allowed, value_rows)
    anchor_keys, anchor_values = (
        from_root(keys, ("section", "ctx"), 0),
        from_root(values, ("section", "ctx"), 0),
    )
    own_scores = (
        jnp.einsum("tkgd,skd->tkgs", query_heads, key_heads, preferred_element_type=jnp.float32)
        * score_scale
    )
    position = jnp.arange(rows_here)
    causal = (position[None, :] <= position[:, None])[:, None, None, :]
    own_state = absorb(start_state, own_scores, causal, value_heads)
    anchor_scores = (
        jnp.einsum(
            "tkgd,skd->tkgs",
            query_heads,
            anchor_keys.reshape(rows_here, KVH, HD),
            preferred_element_type=jnp.float32,
        )
        * score_scale
    )
    anchor_allowed = jnp.broadcast_to(host > 0, anchor_scores.shape)
    anchor_state = absorb(
        start_state, anchor_scores, anchor_allowed, anchor_values.reshape(rows_here, KVH, HD)
    )
    merged = join(join(own_state, anchor_state), far_state)
    result = merged[2] / merged[1][..., None]
    return result.reshape(rows_here, QH * HD).astype(jnp.bfloat16)


def solution(mesh):
    in_specs = (
        P(("section", "ctx"), None),
        P(("section", "ctx"), None),
        P(("section", "ctx"), None),
        P(("section", "ctx"), None, None),
    )
    out_specs = P(("section", "ctx"), None)
    return jax.shard_map(
        on_device, mesh=mesh, in_specs=in_specs, out_specs=out_specs, check_vma=False
    )
```

profile of v0, /device:TPU:7, one launch (start us, length us, event | category | flops | bytes accessed | tf_op | source)
XLA Modules:
  0.0 524.5 jit_solution(17256382779393609212)
XLA Ops:
  6.5 1.1 copy.32
  7.7 1.0 copy.35
  8.7 0.7 broadcast_select_fusion
  9.4 0.8 copy.38
  10.1 0.0 all-reduce.3.cloned.1.call-update
  10.2 0.0 all-gather.5.cloned.1.call-start
  10.2 0.7 shift-left_or_fusion
  10.9 0.7 and_bitcast_fusion
  11.6 0.1 copy.42
  11.7 0.1 reshape.121
  11.8 0.1 copy.45
  12.0 0.7 gather_fusion
  12.7 0.7 gather_fusion.1
  13.3 0.7 bitcast_select_fusion.2
  14.0 0.0 all-gather.7.cloned.1.call-start
  14.1 0.7 all-gather.7.cloned.1.call-update
  14.8 0.2 copy.69
  15.1 0.7 fusion.17
  15.8 0.6 fusion.22
  16.3 2.1 fusion.28
  18.4 0.1 broadcast_in_dim.96
  18.5 0.1 broadcast_in_dim.97
  18.7 246.3 %all-reduce.3.cloned.1.call-done = (bf16[128,4,128]{2,0,1:T(8,128)(2,1)}, bf16[128,4,128]{0,2,1:T(8,128)(2,1)}) async-done(((bf16[128,4,128]{2,0,1:T(8,128)(2,1)}, bf16[128,4,128]{0,2,1:T(8,128)(2,1)}), (bf16[128,4,128]{2,0,1:T(8,128)(2,1)}, bf16[128,4,128]{0,2,1:T(8,128)(2,1)})) %all-reduce.3.cloned.1.call-update) | async-done | bytes 262160 | tf_op jit(solution)/shard_map/psum | solution.py:18
  265.0 1.6 bitcast_reduce_fusion
  266.6 0.6 fusion.24
  267.2 0.7 fusion.26
  267.9 105.2 %all-gather.5.cloned.1.call-done = bf16[1024,8,128]{2,1,0:T(8,128)(2,1)} async-done(((bf16[4,8,128]{2,1,0:T(8,128)(2,1)}), bf16[1024,8,128]{2,1,0:T(8,128)(2,1)}) %all-gather.5.cloned.1.call-update) | async-done | bytes 2097168 | tf_op jit(solution)/shard_map/all_gather | solution.py:69
  373.1 16.2 %select_reduce_fusion.1 = (f32[128,4,8]{0,2,1:T(8,128)S(1)}, f32[128,4,8,256,8]{0,3,2,4,1:T(8,128)}) fusion(pred[256]{0:T(512)(128)(4,1)S(1)} %compare_and_fusion, bf16[128,4,8,128,1]{3,2,1,0,4:T(8,128)(2,1)S(1)} %bitcast.124, bf16[256,4,8,128,1]{3,2,1,0,4:T(8,128)(2,1)} %bitcast.125), kind=kOutput, calls=%fused_computation.9 | convolution fusion | flops 2172645376 | bytes 36716800 | tf_op jit(solution)/shard_map/tkgd,nksd->tkgns/dot_general | solution.py:76
  389.3 14.5 %select_reduce_fusion = f32[128,4,8]{0,2,1:T(8,128)S(1)} fusion(f32[128,4,8,256,8]{0,3,2,4,1:T(8,128)} %get-tuple-element.20, f32[128,4,8]{0,2,1:T(8,128)S(1)} %broadcast_maximum_fusion, pred[256]{0:T(512)(128)(4,1)S(1)} %compare_and_fusion), kind=kLoop, calls=%fused_computation.7 | loop fusion | flops 33550336 | bytes 33587456 | tf_op jit(solution)/shard_map/reduce_sum | solution.py:34
  403.9 76.0 %all-gather.7.cloned.1.call-done = bf16[1024,8,128]{2,1,0:T(8,128)(2,1)} async-done(((bf16[4,8,128]{2,1,0:T(8,128)(2,1)}), bf16[1024,8,128]{2,1,0:T(8,128)(2,1)}) %all-gather.7.cloned.1.call-update) | async-done | bytes 2097168 | tf_op jit(solution)/shard_map/all_gather | solution.py:70
  479.9 36.7 %fusion.10 = bf16[128,4,8,128]{0,3,2,1:T(8,128)(2,1)S(1)} fusion(f32[4,128,128,8]{2,1,3,0:T(8,128)S(1)} %fusion.26, f32[4,128,8,128]{1,3,2,0:T(8,128)} %fusion.28, f32[128,4,8,256,8]{0,3,2,4,1:T(8,128)} %get-tuple-element.20, f32[128,4,8]{0,2,1:T(8,128)S(1)} %broadcast_maximum_fusion, pred[2048]{0:T(1024)(128)(4,1)S(1)} %broadcast_in_dim.97, ...), kind=kOutput, calls=%fused_computation.16 | convolution fusion | flops 2185232384 | bytes 40994816 | tf_op jit(solution)/shard_map/tkgs,skd->tkgd/dot_general | solution.py:35
  516.6 1.3 copy.50
  (12 shorter events, 0.1 us)
Async XLA Ops:
  6.5 8.3 %copy-start = (bf16[128,4096]{1,0:T(8,128)(2,1)S(1)}, bf16[128,4096]{1,0:T(8,128)(2,1)}, u32[]{:S(2)}) copy-start(bf16[128,4096]{1,0:T(8,128)(2,1)} %param.6) | copy-start | bytes 3145732
  6.5 258.4 %all-reduce.3.cloned.1.call-start = ((), (), s32[]{:S(2)}) async-start(), calls=%async_computation.2 | async-start | bytes 524288 | tf_op jit(solution)/shard_map/psum | solution.py:18
  10.2 362.9 %all-gather.5.cloned.1.call-start = ((), (), s32[]{:S(2)}) async-start(), calls=%async_computation | async-start | bytes 2105344 | tf_op jit(solution)/shard_map/all_gather | solution.py:69
  14.0 465.9 %all-gather.7.cloned.1.call-start = ((), (), s32[]{:S(2)}) async-start(), calls=%async_computation.1 | async-start | bytes 2105344 | tf_op jit(solution)/shard_map/all_gather | solution.py:70
  265.0 2.2 copy-start.1
Sparse Core Ops, SparseCore 0:
  13.0 251.9 all-reduce.2
  268.7 104.3 all-gather.4
  376.8 103.0 all-gather.6
where the time goes:
time: 526 us; the launch traced here: 524 us
  waiting for transfers between devices  428 us (81%)
  matrix products  58 us (11%)
  other arithmetic  18.5 us (4%)
  between operations  13.3 us (3%)
  local copies, waits for them, and re-layouts  6.41 us (1%)
    psum x1, waiting for transfers between devices, from_root(): return lax.psum(jnp.where(mine, shard, jnp.zeros_like(shard)), axis)  246 us
    all_gather x1, waiting for transfers between devices, on_device(): lax.all_gather(kept_keys, ('section', 'ctx'), axis=0, tiled=True)  105 us
    all_gather x1, waiting for transfers between devices, on_device(): lax.all_gather(kept_values, ('section', 'ctx'), axis=0, tiled=True)  76 us
    dot_general x3, matrix products, absorb(): jnp.einsum('tkgs,skd->tkgd', weights.astype(jnp.bfloat16), value_rows, pr...  39.4 us
    dot_general x1, matrix products, on_device(): jnp.einsum('tkgd,nksd->tkgns', query_heads, block_keys, preferred_element...  16.2 us
    reduce_sum x3, other arithmetic, absorb(): total = jnp.sum(weights, axis=-1)  15.7 us
  transfers between devices with their start and end apart: 3, of which 3 were waited for; matrix products, arithmetic and copies ran while one was open for 8% of the time, Pallas kernels for 0%

commit v1 on v0

v1 whole, which is shorter than its diff:
```python
import functools
import math

import jax
import jax.numpy as jnp
from jax import lax
from jax.experimental import pallas as pl
from jax.experimental.pallas import tpu as pltpu
from jax.sharding import Mesh, PartitionSpec as P

QH = 32
KVH = 4
HD = 128
KEEP = 8
TOK = 128
GROUP = QH // KVH
NX, NY, NZ, NC = 4, 4, 8, 2
NXY = NX * NY
HALF = KVH // NC
AXES = ("x", "y", "z", "c")
PIECE = HALF * 2 * TOK // NXY
FAR = NXY * NZ * NC * KEEP
SLOT = HALF * 2 * TOK + PIECE
EXP2_SCALE = math.log2(math.e) / math.sqrt(HD)
VMEM_BYTES = 48 * 1024 * 1024

bf16 = jnp.bfloat16
f32 = jnp.float32


def pick_kernel(index_ref, keys_ref, values_ref, kept_ref, block_ref):
    rows = lax.broadcasted_iota(jnp.int32, (KEEP, TOK), 0)
    lanes = lax.broadcasted_iota(jnp.int32, (KEEP, TOK), 1)
    for j in range(KVH):
        chosen = jnp.zeros((KEEP, TOK), jnp.int32)
        for r in range(KEEP):
            chosen = jnp.where(rows == r, index_ref[0, j, r], chosen)
        onehot = (chosen == lanes).astype(f32).astype(bf16)
        columns = slice(j * HD, (j + 1) * HD)
        key_rows = jnp.dot(onehot, keys_ref[:, columns], preferred_element_type=f32)
        value_rows = jnp.dot(onehot, values_ref[:, columns], preferred_element_type=f32)
        kept_ref[j] = jnp.concatenate([key_rows, value_rows], axis=0).astype(bf16)
        block_ref[j, :TOK] = keys_ref[:, columns]
        block_ref[j, TOK:] = values_ref[:, columns]


def pick(keep_index, keys, values):
    return pl.pallas_call(
        pick_kernel,
        in_specs=[
            pl.BlockSpec(memory_space=pltpu.SMEM),
            pl.BlockSpec(memory_space=pltpu.VMEM),
            pl.BlockSpec(memory_space=pltpu.VMEM),
        ],
        out_shape=(
            jax.ShapeDtypeStruct((KVH, 2 * KEEP, HD), bf16),
            jax.ShapeDtypeStruct((KVH, 2 * TOK, HD), bf16),
        ),
    )(keep_index, keys, values)


def pair_kernel(core_ref, mine_ref, other_ref, pair_ref):
    first = core_ref[0] == 0
    for h in range(HALF):
        mine = mine_ref[h].astype(f32)
        other = other_ref[h].astype(f32)
        low = jnp.where(first, mine, other)
        high = jnp.where(first, other, mine)
        pair_ref[h, 0] = jnp.concatenate([low[:KEEP], high[:KEEP]], axis=0).astype(bf16)
        pair_ref[h, 1] = jnp.concatenate([low[KEEP:], high[KEEP:]], axis=0).astype(bf16)


def attend_kernel(place_ref, q_ref, k_ref, v_ref, far_ref, _, out_ref, key_rows, value_rows):
    block = place_ref[1]
    head = pl.program_id(0)
    first_key = k_ref[0:1, :].astype(f32)
    own_at, anchor_at = FAR + TOK, FAR
    lane_ones = jnp.ones((TOK, HD), f32)

    def put(at, keys, values, valid):
        keys = jnp.where(valid, keys.astype(f32), first_key)
        values = jnp.where(valid, values.astype(f32), 0.0)
        key_rows[pl.ds(at, TOK), :] = keys.astype(bf16)
        value_rows[pl.ds(at, TOK), :HD] = values.astype(bf16)
        value_rows[pl.ds(at, TOK), HD:] = jnp.where(valid, lane_ones, 0.0).astype(bf16)

    row_block = lax.broadcasted_iota(jnp.int32, (TOK, HD), 0) // KEEP

    at_head = pl.multiple_of(head * 2 * TOK, 2 * TOK)
    for s in range(NXY):
        owner = row_block + s * (TOK // KEEP)
        put(
            s * TOK,
            far_ref[s, pl.ds(at_head, TOK), :],
            far_ref[s, pl.ds(at_head + TOK, TOK), :],
            (owner >= 1) & (owner < block),
        )
    pieces = TOK // PIECE
    anchor_keys = [far_ref[head * 2 * pieces + i, HALF * 2 * TOK :, :] for i in range(pieces)]
    anchor_values = [
        far_ref[head * 2 * pieces + pieces + i, HALF * 2 * TOK :, :] for i in range(pieces)
    ]
    put(
        anchor_at,
        jnp.concatenate(anchor_keys, axis=0),
        jnp.concatenate(anchor_values, axis=0),
        row_block * 0 < block,
    )
    key_rows[own_at:, :] = k_ref[...]
    value_rows[own_at:, :HD] = v_ref[...]
    value_rows[own_at:, HD:] = lane_ones.astype(bf16)

    causal = lax.broadcasted_iota(jnp.int32, (TOK, TOK), 1) <= lax.broadcasted_iota(
        jnp.int32, (TOK, TOK), 0
    )
    for g in range(GROUP):
        columns = slice(g * HD, (g + 1) * HD)
        scores = lax.dot_general(
            q_ref[:, columns], key_rows[...], (((1,), (1,)), ((), ())), preferred_element_type=f32
        )
        scores = jnp.concatenate(
            [scores[:, :own_at], jnp.where(causal, scores[:, own_at:], -1e30)], axis=1
        )
        highest = jnp.max(scores, axis=1, keepdims=True)
        weights = jnp.exp2((scores - highest) * EXP2_SCALE).astype(bf16)
        summed = jnp.dot(weights, value_rows[...], preferred_element_type=f32)
        out_ref[:, columns] = (summed[:, :HD] / summed[:, HD:]).astype(bf16)


def attend(place, queries, keys, values, far, out, first):
    def heads(i, place_ref):
        return (0, place_ref[0 if first else 2] * HALF + i)

    whole = pl.BlockSpec((NXY, SLOT, HD), lambda i, place_ref: (0, 0, 0))
    grid_spec = pltpu.PrefetchScalarGridSpec(
        num_scalar_prefetch=1,
        grid=(HALF,),
        in_specs=[
            pl.BlockSpec((TOK, GROUP * HD), heads),
            pl.BlockSpec((TOK, HD), heads),
            pl.BlockSpec((TOK, HD), heads),
            whole,
            pl.BlockSpec(memory_space=pl.ANY),
        ],
        out_specs=pl.BlockSpec((TOK, GROUP * HD), heads),
        scratch_shapes=[
            pltpu.VMEM((FAR + 2 * TOK, HD), bf16),
            pltpu.VMEM((FAR + 2 * TOK, 2 * HD), bf16),
        ],
    )
    return pl.pallas_call(
        attend_kernel,
        grid_spec=grid_spec,
        out_shape=jax.ShapeDtypeStruct((TOK, QH * HD), bf16),
        input_output_aliases={5: 0},
        compiler_params=pltpu.CompilerParams(vmem_limit_bytes=VMEM_BYTES),
        cost_estimate=pl.CostEstimate(
            flops=2 * 2 * HALF * GROUP * TOK * (FAR + 2 * TOK) * HD,
            bytes_accessed=4 * 1024 * 1024,
            transcendentals=HALF * GROUP * TOK * (FAR + 2 * TOK),
        ),
    )(place, queries, keys, values, far, out)


def on_device(queries, keys, values, keep_index):
    core = lax.axis_index("c")
    xy = lax.axis_index("x") * NY + lax.axis_index("y")
    block = (xy * NZ + lax.axis_index("z")) * NC + core
    place = jnp.stack([core, block, 1 - core]).astype(jnp.int32)
    swap = [(0, 1), (1, 0)]
    to_all = functools.partial(lax.all_to_all, split_axis=0, concat_axis=0, tiled=True)

    kept, own = pick(keep_index, keys, values)
    half = lambda a, which: lax.dynamic_slice_in_dim(a, which * HALF, HALF, 0)
    sent = jnp.concatenate([half(kept, 1 - core), half(own, 1 - core)], axis=1)
    came = lax.ppermute(sent, "c", swap)
    pair = pl.pallas_call(
        pair_kernel,
        in_specs=[
            pl.BlockSpec(memory_space=pltpu.SMEM),
            pl.BlockSpec(memory_space=pltpu.VMEM),
            pl.BlockSpec(memory_space=pltpu.VMEM),
        ],
        out_shape=jax.ShapeDtypeStruct((HALF, 2, 2 * KEEP, HD), bf16),
    )(place, half(kept, core), came[:, : 2 * KEEP])

    anchor = jnp.where(core == 0, half(own, core), came[:, 2 * KEEP :])
    piece = to_all(anchor.reshape(NXY * PIECE, HD), ("x", "y"))[:PIECE]

    rows = HALF * 2 * 2 * KEEP
    along_z = to_all(
        jnp.tile(jnp.concatenate([pair.reshape(rows, HD), piece], axis=0)[None], (NZ, 1, 1)), "z"
    )
    retained = along_z[:, :rows].reshape(NZ, HALF, 2, 2 * KEEP, HD)
    retained = jnp.transpose(retained, (1, 2, 0, 3, 4)).reshape(HALF * 2 * TOK, HD)
    slot = jnp.concatenate([retained, along_z[0, rows:]], axis=0)
    far = to_all(jnp.tile(slot[None], (NXY, 1, 1)), ("x", "y"))
    far_other = lax.ppermute(far, "c", swap)

    out = jnp.zeros((TOK, QH * HD), bf16)
    out = attend(place, queries, keys, values, far, out, True)
    return attend(place, queries, keys, values, far_other, out, False)


def solution(mesh):
    fine = Mesh(mesh.devices.reshape(NX, NY, NZ, NC), AXES)
    return jax.shard_map(
        on_device,
        mesh=fine,
        in_specs=(P(AXES, None), P(AXES, None), P(AXES, None), P(AXES, None, None)),
        out_specs=P(AXES, None),
        check_vma=False,
    )
```

time: 526 us -> 91.6 us (0.17)
  the two profiles are of different devices: /device:TPU:7 before, /device:TPU:1 now
where the time goes in v1:
time: 91.6 us; the launch traced here: 91 us
  blocking collectives  46.5 us (51%)
  Pallas kernels  19.5 us (21%)
  starting transfers between devices  12.6 us (14%)
  waiting for transfers between devices  5.16 us (6%)
  local copies, waits for them, and re-layouts  4.27 us (5%)
  other arithmetic  2.89 us (3%)
    all_to_all x1, blocking collectives, on_device(): far = to_all(jnp.tile(slot[None], (NXY, 1, 1)), ('x', 'y'))  29.8 us
    all_to_all x1, blocking collectives, on_device(): to_all(jnp.tile(jnp.concatenate([pair.reshape(rows, HD), piece], axis=0)[...  16.7 us
    pallas_call x2, Pallas kernels, attend(): pl.pallas_call(attend_kernel, grid_spec=grid_spec, out_shape=jax.ShapeDty...  16.3 us
    all_to_all x1, starting transfers between devices, on_device(): piece = to_all(anchor.reshape(NXY * PIECE, HD), ('x', 'y'))[:PIECE]  5.02 us
    ppermute x1, starting transfers between devices, on_device(): far_other = lax.ppermute(far, 'c', swap)  4.29 us
    all_to_all x1, waiting for transfers between devices, on_device(): piece = to_all(anchor.reshape(NXY * PIECE, HD), ('x', 'y'))[:PIECE]  4.16 us
    ppermute x1, starting transfers between devices, on_device(): came = lax.ppermute(sent, 'c', swap)  3.33 us
    dynamic_slice x2, local copies, waits for them, and re-layouts, on_device(): half = lambda a, which: lax.dynamic_slice_in_dim(a, which * HALF, HALF, 0)  2.24 us
  transfers between devices with their start and end apart: 3, of which 2 were waited for; matrix products, arithmetic and copies ran while one was open for 2% of the time, Pallas kernels for 10%

profile of v1, /device:TPU:1, one launch (start us, length us, event | category | flops | bytes accessed | tf_op | source)
XLA Modules:
  0.0 91.0 jit_solution(8142979387629823228)
XLA Ops:
  0.0 1.8 %shard_map.46 = (bf16[4,16,128]{2,1,0:T(8,128)(2,1)}, bf16[4,256,128]{2,1,0:T(8,128)(2,1)}) custom-call(s32[1,4,8]{2,1,0:T(4,128)} %index_ref.1, bf16[128,512]{1,0:T(8,128)(2,1)} %k_ref.3, bf16[128,512]{1,0:T(8,128)(2,1)} %v_ref.3), custom_call_target="tpu_custom_call" | custom-call | tf_op jit(solution)/shard_map/pallas_call | solution.py:48
  1.8 0.9 %constant_dynamic-slice_fusion = bf16[2,256,128]{2,1,0:T(8,128)(2,1)S(1)} fusion(bf16[4,256,128]{2,1,0:T(8,128)(2,1)} %get-tuple-element.8, s32[]{:T(128)S(6)} %select_n.17), kind=kLoop, calls=%fused_computation.6 | loop fusion | bytes 262148 | tf_op jit(solution)/shard_map/dynamic_slice | solution.py:174
  2.7 1.3 %constant_dynamic-slice_fusion.2 = (bf16[2,16,128]{2,1,0:T(8,128)(2,1)}, bf16[2,16,128]{2,1,0:T(8,128)(2,1)S(1)}) fusion(bf16[4,16,128]{2,1,0:T(8,128)(2,1)} %get-tuple-element.7, s32[]{:T(128)S(6)} %select_n.16, s32[]{:T(128)S(6)} %select_n.17), kind=kLoop, calls=%fused_computation.8 | loop fusion | bytes 32776 | tf_op jit(solution)/shard_map/dynamic_slice | solution.py:174
  4.0 3.3 %collective-permute-start = (bf16[2,272,128]{2,1,0:T(8,128)(2,1)S(1)}, bf16[2,272,128]{2,1,0:T(8,128)(2,1)S(1)}, u32[]{:S(2)}, u32[]{:S(2)}) collective-permute-start(bf16[2,272,128]{2,1,0:T(8,128)(2,1)S(1)} %pad_maximum_fusion), channel_id=1, source_target_pairs={{0,1},{1,0},{2,3},{3,2},{4,5},{5,4},{6,7},{7,6},{8,9},{9,8},{10,11... | collective-permute-start | bytes 417800 | tf_op jit(solution)/shard_map/ppermute | solution.py:176
  7.4 1.0 %collective-permute-done = bf16[2,272,128]{2,1,0:T(8,128)(2,1)S(1)} collective-permute-done((bf16[2,272,128]{2,1,0:T(8,128)(2,1)S(1)}, bf16[2,272,128]{2,1,0:T(8,128)(2,1)S(1)}, u32[]{:S(2)}, u32[]{:S(2)}) %collective-permute-start) | collective-permute-done | bytes 139296 | tf_op jit(solution)/shard_map/ppermute | solution.py:176
  8.4 1.6 %slice_select_fusion = bf16[2,256,128]{2,1,0:T(8,128)(2,1)} fusion(bf16[2,272,128]{2,1,0:T(8,128)(2,1)S(1)} %collective-permute-done, bf16[4,256,128]{2,1,0:T(8,128)(2,1)} %get-tuple-element.8, s32[]{:T(128)S(6)} %select_n.16, pred[]{:T(512)S(6)} %eq.3), kind=kLoop, calls=%fused_computation.2 | loop fusion | flops 65536 | bytes 393221 | tf_op jit(solution)/shard_map/jit(_where)/select_n | solution.py:187
  9.9 5.0 %all-to-all-start = ((bf16[16,32,128]{2,1,0:T(8,128)(2,1)}), bf16[16,32,128]{2,1,0:T(8,128)(2,1)S(1)}, u32[]{:S(2)}, u32[]{:S(2)}) async-start(bf16[16,32,128]{2,1,0:T(8,128)(2,1)} %bitcast.4), calls=%async_computation | async-start | bytes 262144 | tf_op jit(solution)/shard_map/all_to_all | solution.py:188
  15.0 0.6 pad_add_fusion.core_ref.place_ref
  15.6 0.6 slice.24.other_ref
  16.1 1.3 %shard_map.47 = bf16[2,2,16,128]{3,2,1,0:T(8,128)(2,1)} custom-call(s32[3]{0:T(128)} %pad_add_fusion.core_ref.place_ref, bf16[2,16,128]{2,1,0:T(8,128)(2,1)} %get-tuple-element.9.mine_ref, bf16[2,16,128]{2,1,0:T(8,128)(2,1)} %slice.24.other_ref), custom_call_target="tpu_custom_call" | custom-call | tf_op jit(solution)/shard_map/pallas_call | solution.py:177
  17.5 4.2 %all-to-all-done = bf16[16,32,128]{2,1,0:T(8,128)(2,1)S(1)} async-done(((bf16[16,32,128]{2,1,0:T(8,128)(2,1)}), bf16[16,32,128]{2,1,0:T(8,128)(2,1)S(1)}, u32[]{:S(2)}, u32[]{:S(2)}) %all-to-all-start) | async-done | bytes 131104 | tf_op jit(solution)/shard_map/all_to_all | solution.py:188
  21.6 0.7 pad_maximum_fusion.2
  22.4 16.7 %all_to_all.19 = bf16[8,96,128]{2,1,0:T(8,128)(2,1)S(1)} all-to-all(bf16[8,96,128]{2,1,0:T(8,128)(2,1)S(1)} %tile.4), channel_id=1, replica_groups=mesh['x'=4,'y'=4,'z'=8,'c'=2] {'z'}, dimensions={0} | all-to-all | bytes 393216 | tf_op jit(solution)/shard_map/all_to_all | solution.py:191
  39.1 0.3 tile.5
  39.4 0.0 copy-start
  39.4 0.0 copy-start.1
  39.4 0.0 copy-start.2
  39.5 0.0 copy-start.3
  39.5 29.8 %all_to_all.20.far_ref = bf16[16,544,128]{2,1,0:T(8,128)(2,1)S(1)} all-to-all(bf16[16,544,128]{2,1,0:T(8,128)(2,1)S(1)} %tile.5), channel_id=1, replica_groups=mesh['x'=4,'y'=4,'z'=8,'c'=2] {'x','y'}, dimensions={0} | all-to-all | bytes 4456448 | tf_op jit(solution)/shard_map/all_to_all | solution.py:197
  69.3 4.3 %collective-permute-start.1 = (bf16[16,544,128]{2,1,0:T(8,128)(2,1)S(1)}, bf16[16,544,128]{2,1,0:T(8,128)(2,1)S(1)}, u32[]{:S(2)}, u32[]{:S(2)}) collective-permute-start(bf16[16,544,128]{2,1,0:T(8,128)(2,1)S(1)} %all_to_all.20.far_ref), channel_id=1, source_target_pairs={{0,1},{1,0},{2,3},{3,2},{4,5},{5,4},{6,7},{7,6},{8,9},{9,8},{10,11... | collective-permute-start | bytes 6684680 | tf_op jit(solution)/shard_map/ppermute | solution.py:198
  73.6 1.1 %broadcast_in_dim.3._ = bf16[128,4096]{1,0:T(8,128)(2,1)} broadcast(bf16[]{:T(256)} %constant.29.clone.1), dimensions={} | broadcast | bytes 1048578 | tf_op jit(solution)/shard_map/broadcast_in_dim | solution.py:200
  74.6 0.0 copy-done
  74.6 0.0 copy-done.1
  74.6 0.0 copy-done.2
  74.6 0.0 copy-done.3
  74.6 8.2 %shard_map.48._ = bf16[128,4096]{1,0:T(8,128)(2,1)} custom-call(s32[3]{0:T(128)S(1)} %copy-done.2, bf16[128,4096]{1,0:T(8,128)(2,1)S(1)} %copy-done.3, bf16[128,512]{1,0:T(8,128)(2,1)S(1)} %copy-done, bf16[128,512]{1,0:T(8,128)(2,1)S(1)} %copy-done.1, bf16[16,544,128]{2,1,0:T(8,128)(2,1)S(1)} %all_to_all.20.far_ref, ...), custom_call_target="tpu_custom_call", output_to_operand_aliasing={{}: (5, {})} | custom-call | flops 2415919104 | bytes 4194304 | tf_op jit(solution)/shard_map/pallas_call | solution.py:151
  82.8 0.0 collective-permute-done.1.far_ref
  82.8 8.2 %shard_map.49 = bf16[128,4096]{1,0:T(8,128)(2,1)} custom-call(s32[3]{0:T(128)S(1)} %copy-done.2, bf16[128,4096]{1,0:T(8,128)(2,1)S(1)} %copy-done.3, bf16[128,512]{1,0:T(8,128)(2,1)S(1)} %copy-done, bf16[128,512]{1,0:T(8,128)(2,1)S(1)} %copy-done.1, bf16[16,544,128]{2,1,0:T(8,128)(2,1)S(1)} %collective-permute-done.1.far_ref, ...), custom_call_target="tpu_custom_call", output_to_operand_aliasing={{}: (5, {})} | custom-call | flops 2415919104 | bytes 4194304 | tf_op jit(solution)/shard_map/pallas_call | solution.py:151
  (7 shorter events, 0.1 us)
Async XLA Ops:
  4.0 4.3 %collective-permute-start = (bf16[2,272,128]{2,1,0:T(8,128)(2,1)S(1)}, bf16[2,272,128]{2,1,0:T(8,128)(2,1)S(1)}, u32[]{:S(2)}, u32[]{:S(2)}) collective-permute-start(bf16[2,272,128]{2,1,0:T(8,128)(2,1)S(1)} %pad_maximum_fusion), channel_id=1, source_target_pairs={{0,1},{1,0},{2,3},{3,2},{4,5},{5,4},{6,7},{7,6},{8,9},{9,8},{10,11... | collective-permute-start | bytes 417800 | tf_op jit(solution)/shard_map/ppermute | solution.py:176
  9.9 11.7 %all-to-all-start = ((bf16[16,32,128]{2,1,0:T(8,128)(2,1)}), bf16[16,32,128]{2,1,0:T(8,128)(2,1)S(1)}, u32[]{:S(2)}, u32[]{:S(2)}) async-start(bf16[16,32,128]{2,1,0:T(8,128)(2,1)} %bitcast.4), calls=%async_computation | async-start | bytes 262144 | tf_op jit(solution)/shard_map/all_to_all | solution.py:188
  39.4 35.2 %copy-start = (bf16[128,512]{1,0:T(8,128)(2,1)S(1)}, bf16[128,512]{1,0:T(8,128)(2,1)}, u32[]{:S(2)}) copy-start(bf16[128,512]{1,0:T(8,128)(2,1)} %k_ref.3) | copy-start | bytes 393220
  39.4 35.2 %copy-start.1 = (bf16[128,512]{1,0:T(8,128)(2,1)S(1)}, bf16[128,512]{1,0:T(8,128)(2,1)}, u32[]{:S(2)}) copy-start(bf16[128,512]{1,0:T(8,128)(2,1)} %v_ref.3) | copy-start | bytes 393220
  39.4 35.2 %copy-start.2 = (s32[3]{0:T(128)S(1)}, s32[3]{0:T(128)}, u32[]{:S(2)}) copy-start(s32[3]{0:T(128)} %pad_add_fusion.core_ref.place_ref) | copy-start | bytes 40
  39.5 35.2 %copy-start.3 = (bf16[128,4096]{1,0:T(8,128)(2,1)S(1)}, bf16[128,4096]{1,0:T(8,128)(2,1)}, u32[]{:S(2)}) copy-start(bf16[128,4096]{1,0:T(8,128)(2,1)} %q_ref.3) | copy-start | bytes 3145732
  69.3 13.6 %collective-permute-start.1 = (bf16[16,544,128]{2,1,0:T(8,128)(2,1)S(1)}, bf16[16,544,128]{2,1,0:T(8,128)(2,1)S(1)}, u32[]{:S(2)}, u32[]{:S(2)}) collective-permute-start(bf16[16,544,128]{2,1,0:T(8,128)(2,1)S(1)} %all_to_all.20.far_ref), channel_id=1, source_target_pairs={{0,1},{1,0},{2,3},{3,2},{4,5},{5,4},{6,7},{7,6},{8,9},{9,8},{10,11... | collective-permute-start | bytes 6684680 | tf_op jit(solution)/shard_map/ppermute | solution.py:198

commit v2 on v0

v2 whole, which is shorter than its diff:
```python
import functools
import math

import jax
import jax.numpy as jnp
from jax import lax
from jax.experimental import pallas as pl
from jax.experimental.pallas import tpu as pltpu
from jax.sharding import Mesh, PartitionSpec as P

QH = 32
KVH = 4
HD = 128
KEEP = 8
TOK = 128
GROUP = QH // KVH
NX, NY, NZ, NC = 4, 4, 8, 2
DEVICES = NX * NY * NZ * NC
HALF = KVH // NC
FIRST = 16
SECOND = 8
PAIR = NC * KEEP
KEPT_ROWS = HALF * 2 * PAIR
PIECE = HALF * 2 * TOK // FIRST
CHUNK = FIRST * PAIR
FAR = SECOND * CHUNK
SLOT = HALF * 2 * CHUNK + PIECE
EXP2_SCALE = math.log2(math.e) / math.sqrt(HD)
VMEM_BYTES = 48 * 1024 * 1024

bf16 = jnp.bfloat16
f32 = jnp.float32
in_smem = pl.BlockSpec(memory_space=pltpu.SMEM)
in_vmem = pl.BlockSpec(memory_space=pltpu.VMEM)


def device(core, a, u, zh, zl):
    x, y = (a, u) if core == 0 else (u, a)
    z = (2 * zh + zl) % NZ if core == 0 else (2 * zh - zl) % NZ
    return ((x * NY + y) * NZ + z) * NC + core


def first_groups():
    return [
        [device(c, a, u, zh, zl) for u in range(4) for zh in range(4)]
        for c in range(2)
        for a in range(4)
        for zl in range(2)
    ]


def second_groups():
    return [
        [device(c, a, u, zh, zl) for a in range(4) for zl in range(2)]
        for c in range(2)
        for u in range(4)
        for zh in range(4)
    ]


def pick_kernel(block_ref, index_ref, keys_ref, values_ref, mine_ref, sent_ref):
    core = block_ref[0] % NC
    rows = lax.broadcasted_iota(jnp.int32, (KEEP, TOK), 0)
    lanes = lax.broadcasted_iota(jnp.int32, (KEEP, TOK), 1)
    for out_ref, owner in ((sent_ref, 1 - core), (mine_ref, core)):
        for h in range(HALF):
            j = owner * HALF + h
            chosen = jnp.zeros((KEEP, TOK), jnp.int32)
            for r in range(KEEP):
                chosen = jnp.where(rows == r, index_ref[0, j, r], chosen)
            onehot = (chosen == lanes).astype(f32).astype(bf16)
            columns = pl.ds(pl.multiple_of(j * HD, HD), HD)
            keys = keys_ref[:, columns]
            values = values_ref[:, columns]
            key_rows = jnp.dot(onehot, keys, preferred_element_type=f32)
            value_rows = jnp.dot(onehot, values, preferred_element_type=f32)
            out_ref[h, :PAIR] = jnp.concatenate([key_rows, value_rows], axis=0).astype(bf16)
            out_ref[h, PAIR : PAIR + TOK] = keys
            out_ref[h, PAIR + TOK :] = values


def pick(block, keep_index, keys, values):
    shape = jax.ShapeDtypeStruct((HALF, PAIR + 2 * TOK, HD), bf16)
    return pl.pallas_call(
        pick_kernel,
        in_specs=[in_smem, in_smem, in_vmem, in_vmem],
        out_specs=(in_vmem, in_vmem),
        out_shape=(shape, shape),
    )(block, keep_index, keys, values)


def first_kernel(block_ref, mine_ref, came_ref, out_ref):
    core = block_ref[0] % NC
    for h in range(HALF):
        mine = mine_ref[h, :PAIR].astype(f32)
        came = came_ref[h, :PAIR].astype(f32)
        low = jnp.where(core == 0, mine, came)
        high = jnp.where(core == 0, came, mine)
        keys = jnp.concatenate([low[:KEEP], high[:KEEP]], axis=0).astype(bf16)
        values = jnp.concatenate([low[KEEP:], high[KEEP:]], axis=0).astype(bf16)
        for k in range(FIRST):
            out_ref[k, 2 * h * PAIR : (2 * h + 1) * PAIR] = keys
            out_ref[k, (2 * h + 1) * PAIR : (2 * h + 2) * PAIR] = values

    def pieces(ref):
        each = FIRST // HALF
        for k in range(FIRST):
            at = PAIR + (k % each) * PIECE
            out_ref[k, KEPT_ROWS:] = ref[k // each, at : at + PIECE]

    pl.when(core == 0)(lambda: pieces(mine_ref))
    pl.when(core != 0)(lambda: pieces(came_ref))


def second_kernel(in_ref, out_ref):
    for s in range(SECOND):
        for m in range(FIRST):
            for part in range(HALF * 2):
                at = part * CHUNK + m * PAIR
                out_ref[s, at : at + PAIR] = in_ref[m, part * PAIR : (part + 1) * PAIR]
        out_ref[s, HALF * 2 * CHUNK :] = in_ref[0, KEPT_ROWS:]


def attend_kernel(with_far, with_anchor, with_prior, with_own, other, *refs):
    refs = list(refs)
    take = lambda on: refs.pop(0) if on else None
    block_ref, q_ref, k_ref, v_ref = (take(True) for _ in range(4))
    far_ref, anchor_ref = take(with_far), take(with_anchor)
    prior_ref, prior_state_ref = take(with_prior), take(with_prior)
    if with_anchor and with_far:
        take(True)
    partial = not with_anchor
    out_ref, state_ref = take(True), take(partial)
    key_rows, value_rows, scratch = refs
    block = block_ref[0]
    head = pl.program_id(0)
    source = 1 - block % NC if other else block % NC
    first_key = k_ref[0:1, :]
    anchor_at = FAR if with_far else 0
    own_at = anchor_at + (TOK if with_anchor else 0)
    total_keys = own_at + (TOK if with_own else 0)

    @pl.when(head == 0)
    def _():
        if with_far:
            rows = lax.broadcasted_iota(jnp.int32, (CHUNK, HD), 0)
            u, zh, half = rows // (4 * PAIR), (rows // PAIR) % 4, (rows // KEEP) % NC
            step_u = jnp.where(source == 0, NZ * NC, NY * NZ * NC)
            step_a = jnp.where(source == 0, NY * NZ * NC, NZ * NC)
            sign = jnp.where(source == 0, 1, -1)
            for zl in range(2):
                base = u * step_u + ((2 * zh + sign * zl) % NZ) * NC + half
                for a in range(4):
                    owner = base + a * step_a
                    valid = ((owner >= 1) & (owner < block)).astype(f32).astype(bf16)
                    at = (a * 2 + zl) * CHUNK
                    value_rows[at : at + CHUNK, HD:] = valid
        if with_anchor:
            valid = jnp.where(block > 0, jnp.ones((TOK, HD), f32), 0.0).astype(bf16)
            value_rows[anchor_at : anchor_at + TOK, HD:] = valid
        if with_own:
            value_rows[own_at:total_keys, HD:] = jnp.ones((TOK, HD), bf16)

    def put(at, count, keys, values):
        valid = value_rows[at : at + count, HD:]
        spare = jnp.ones((count, HD), bf16) - valid
        key_rows[at : at + count, :] = keys * valid + first_key * spare
        value_rows[at : at + count, :HD] = values * valid

    if with_far:
        at_head = pl.multiple_of(head * 2 * CHUNK, 2 * CHUNK)
        for s in range(SECOND):
            put(
                s * CHUNK,
                CHUNK,
                far_ref[s, pl.ds(at_head, CHUNK), :],
                far_ref[s, pl.ds(at_head + CHUNK, CHUNK), :],
            )
    if with_anchor:
        pieces = TOK // PIECE
        for i in range(pieces):
            put(
                anchor_at + i * PIECE,
                PIECE,
                anchor_ref[head * 2 * pieces + i],
                anchor_ref[head * 2 * pieces + pieces + i],
            )
    if with_own:
        key_rows[own_at:total_keys, :] = k_ref[...]
        value_rows[own_at:total_keys, :HD] = v_ref[...]
        causal = lax.broadcasted_iota(jnp.int32, (TOK, TOK), 1) <= lax.broadcasted_iota(
            jnp.int32, (TOK, TOK), 0
        )

    def scores(g):
        found = lax.dot_general(
            q_ref[:, g * HD : (g + 1) * HD],
            key_rows[:total_keys, :],
            (((1,), (1,)), ((), ())),
            preferred_element_type=f32,
        )
        if with_own:
            scratch[g % 2, :, :own_at] = found[:, :own_at]
            scratch[g % 2, :, own_at:total_keys] = jnp.where(causal, found[:, own_at:], -1e30)
        else:
            scratch[g % 2, :, :total_keys] = found

    low_lanes = lax.broadcasted_iota(jnp.int32, (TOK, HD), 1) < HD // 2
    scores(0)
    for g in range(GROUP):
        if g + 1 < GROUP:
            scores(g + 1)
        columns = slice(g * HD, (g + 1) * HD)
        found = scratch[g % 2, :, :total_keys]
        highest = jnp.max(found, axis=1, keepdims=True)
        if with_prior:
            state = prior_state_ref[:, columns]
            prior_highest, prior_total = state[:, :1], state[:, HD - 1 :]
            highest = jnp.maximum(highest, prior_highest)
        weights = jnp.exp2((found - highest) * EXP2_SCALE).astype(bf16)
        summed = jnp.dot(weights, value_rows[:total_keys, :], preferred_element_type=f32)
        top, total = summed[:, :HD], summed[:, HD:]
        if with_prior:
            shrink = jnp.exp2((prior_highest - highest) * EXP2_SCALE)
            top = top + prior_ref[:, columns] * shrink
            total = total + prior_total * shrink
        if partial:
            out_ref[:, columns] = top
            state_ref[:, columns] = jnp.where(low_lanes, highest, total)
        else:
            out_ref[:, columns] = (top / total).astype(bf16)


def attend(block, queries, keys, values, far, anchor, prior, out, other):
    with_far, with_anchor, with_prior = far is not None, anchor is not None, prior is not None
    with_own = with_far

    def heads(i, block_ref):
        core = block_ref[0] % NC
        return (0, (1 - core if other else core) * HALF + i)

    wide = pl.BlockSpec((TOK, GROUP * HD), heads)
    local = pl.BlockSpec((TOK, GROUP * HD), lambda i, block_ref: (0, i))
    narrow = pl.BlockSpec((TOK, HD), heads)
    operands, in_specs, aliases = [queries, keys, values], [wide, narrow, narrow], {}
    if with_far:
        operands.append(far)
        in_specs.append(in_vmem)
    if with_anchor:
        operands.append(anchor)
        in_specs.append(in_vmem)
    if with_prior:
        operands += prior
        in_specs += [local, local]
    if out is not None:
        operands.append(out)
        in_specs.append(pl.BlockSpec(memory_space=pl.ANY))
        aliases = {len(operands): 0}
    if with_anchor:
        out_shape = jax.ShapeDtypeStruct((TOK, QH * HD), bf16)
        out_specs = wide
    else:
        out_shape = (jax.ShapeDtypeStruct((TOK, HALF * GROUP * HD), f32),) * 2
        out_specs = (local, local)
    rows = (FAR + TOK if with_far else 0) + (TOK if with_anchor else 0)
    work = HALF * GROUP * TOK * rows
    return pl.pallas_call(
        functools.partial(attend_kernel, with_far, with_anchor, with_prior, with_own, other),
        grid_spec=pltpu.PrefetchScalarGridSpec(
            num_scalar_prefetch=1,
            grid=(HALF,),
            in_specs=in_specs,
            out_specs=out_specs,
            scratch_shapes=[
                pltpu.VMEM((rows, HD), bf16),
                pltpu.VMEM((rows, 2 * HD), bf16),
                pltpu.VMEM((2, TOK, rows), f32),
            ],
        ),
        out_shape=out_shape,
        input_output_aliases=aliases,
        compiler_params=pltpu.CompilerParams(vmem_limit_bytes=VMEM_BYTES),
        cost_estimate=pl.CostEstimate(
            flops=4 * work * HD, bytes_accessed=4 * 1024 * 1024, transcendentals=work
        ),
    )(block, *operands)


def on_device(queries, keys, values, keep_index):
    block = lax.axis_index("d").astype(jnp.int32).reshape(1)
    swap = functools.partial(
        lax.ppermute, axis_name="d", perm=[(i, i ^ 1) for i in range(DEVICES)]
    )

    def gather(slots, groups):
        return lax.all_to_all(slots, "d", 0, 0, tiled=True, axis_index_groups=groups)

    mine, sent = pick(block, keep_index, keys, values)
    came = swap(sent)
    slots = pl.pallas_call(
        first_kernel,
        in_specs=[in_smem, in_vmem, in_vmem],
        out_specs=in_vmem,
        out_shape=jax.ShapeDtypeStruct((FIRST, KEPT_ROWS + PIECE, HD), bf16),
    )(block, mine, came)
    near = gather(slots, first_groups())
    slots = pl.pallas_call(
        second_kernel,
        in_specs=[in_vmem],
        out_specs=in_vmem,
        out_shape=jax.ShapeDtypeStruct((SECOND, SLOT, HD), bf16),
    )(near)
    far = gather(slots, second_groups())
    far_other = swap(far)
    piece = far[:1, HALF * 2 * CHUNK :]
    anchor = gather(jnp.tile(piece, (FIRST, 1, 1)), first_groups())
    anchor_other = swap(anchor)

    arrays = (block, queries, keys, values)
    prior = attend(*arrays, far, None, None, None, False)
    out = attend(*arrays, None, anchor, prior, None, False)
    return attend(*arrays, far_other, anchor_other, None, out, True)


def solution(mesh):
    line = Mesh(mesh.devices.reshape(DEVICES), ("d",))
    return jax.shard_map(
        on_device,
        mesh=line,
        in_specs=(P("d", None), P("d", None), P("d", None), P("d", None, None)),
        out_specs=P("d", None),
        check_vma=False,
    )
```

time: 526 us -> 92.8 us (0.18)
  the two profiles are of different devices: /device:TPU:7 before, /device:TPU:1 now
where the time goes in v2:
time: 92.8 us; the launch traced here: 92.4 us
  blocking collectives  59.7 us (64%)
  Pallas kernels  24.9 us (27%)
  starting transfers between devices  5.92 us (6%)
  waiting for transfers between devices  1.21 us (1%)
    all_to_all x3, blocking collectives, gather(): lax.all_to_all(slots, 'd', 0, 0, tiled=True, axis_index_groups=groups)  59.7 us
    pallas_call x3, Pallas kernels, attend(): pl.pallas_call(functools.partial(attend_kernel, with_far, with_anchor, wi...  18.7 us
    ppermute x1, starting transfers between devices, on_device(): came = swap(sent)  3.24 us
    pallas_call x1, Pallas kernels, on_device(): pl.pallas_call(second_kernel, in_specs=[in_vmem], out_specs=in_vmem, out_...  2.62 us
    ppermute x1, starting transfers between devices, on_device(): far_other = swap(far)  2.27 us
  transfers between devices with their start and end apart: 3, of which 1 were waited for; matrix products, arithmetic and copies ran while one was open for 0% of the time, Pallas kernels for 12%

profile of v2, /device:TPU:1, one launch (start us, length us, event | category | flops | bytes accessed | tf_op | source)
XLA Modules:
  0.0 92.4 jit_solution(13998043357225626298)
XLA Ops:
  0.0 1.8 %shard_map.46 = (bf16[2,272,128]{2,1,0:T(8,128)(2,1)}, bf16[2,272,128]{2,1,0:T(8,128)(2,1)}) custom-call(s32[1]{0:T(128)} %bitcast.block_ref.refs_0_, s32[1,4,8]{2,1,0:T(4,128)} %index_ref.1, bf16[128,512]{1,0:T(8,128)(2,1)} %refs_2_.5, bf16[128,512]{1,0:T(8,128)(2,1)} %refs_3_.5), custom_call_target="tpu_custom_call" | custom-call | tf_op jit(solution)/shard_map/pallas_call | solution.py:84
  1.8 3.2 %collective-permute-start = (bf16[2,272,128]{2,1,0:T(8,128)(2,1)}, bf16[2,272,128]{2,1,0:T(8,128)(2,1)S(1)}, u32[]{:S(2)}, u32[]{:S(2)}) collective-permute-start(bf16[2,272,128]{2,1,0:T(8,128)(2,1)} %get-tuple-element.10), channel_id=1, source_target_pairs={{0,1},{1,0},{2,3},{3,2},{4,5},{5,4},{6,7},{7,6},{8,9},{9,8},{10,11... | collective-permute-start | bytes 417800 | tf_op jit(solution)/shard_map/ppermute | solution.py:299
  5.1 1.2 %collective-permute-done.came_ref = bf16[2,272,128]{2,1,0:T(8,128)(2,1)S(1)} collective-permute-done((bf16[2,272,128]{2,1,0:T(8,128)(2,1)}, bf16[2,272,128]{2,1,0:T(8,128)(2,1)S(1)}, u32[]{:S(2)}, u32[]{:S(2)}) %collective-permute-start) | collective-permute-done | bytes 139296 | tf_op jit(solution)/shard_map/ppermute | solution.py:299
  6.3 0.0 copy-start.3
  6.3 0.7 copy-done.3
  7.0 1.7 %shard_map.47 = bf16[16,96,128]{2,1,0:T(8,128)(2,1)} custom-call(s32[1]{0:T(128)} %bitcast.block_ref.refs_0_, bf16[2,272,128]{2,1,0:T(8,128)(2,1)} %get-tuple-element.9.mine_ref, bf16[2,272,128]{2,1,0:T(8,128)(2,1)} %copy-done.3), custom_call_target="tpu_custom_call" | custom-call | tf_op jit(solution)/shard_map/pallas_call | solution.py:300
  8.7 23.5 %all_to_all.15.in_ref = bf16[16,96,128]{2,1,0:T(8,128)(2,1)} all-to-all(bf16[16,96,128]{2,1,0:T(8,128)(2,1)} %shard_map.47), channel_id=1, replica_groups={{0,4,8,12,16,20,24,28,32,36,40,44,48,52,56,60},{2,6,10,14,18,22,26,30,3..., dimensions={0} | all-to-all | bytes 786432 | tf_op jit(solution)/shard_map/all_to_all | solution.py:296
  32.2 2.6 %shard_map.48 = bf16[8,1056,128]{2,1,0:T(8,128)(2,1)} custom-call(bf16[16,96,128]{2,1,0:T(8,128)(2,1)} %all_to_all.15.in_ref), custom_call_target="tpu_custom_call" | custom-call | tf_op jit(solution)/shard_map/pallas_call | solution.py:307
  34.8 0.0 copy-start
  34.8 0.0 copy-start.1
  34.8 0.0 copy-start.2
  34.8 22.6 %all_to_all.16.refs_4_ = bf16[8,1056,128]{2,1,0:T(8,128)(2,1)S(1)} all-to-all(bf16[8,1056,128]{2,1,0:T(8,128)(2,1)} %shard_map.48), channel_id=1, replica_groups={{0,2,64,66,128,130,192,194},{4,6,68,70,132,134,196,198},{8,10,72,74,136..., dimensions={0} | all-to-all | bytes 4325376 | tf_op jit(solution)/shard_map/all_to_all | solution.py:296
  57.4 2.3 %collective-permute-start.1 = (bf16[8,1056,128]{2,1,0:T(8,128)(2,1)S(1)}, bf16[8,1056,128]{2,1,0:T(8,128)(2,1)S(1)}, u32[]{:S(2)}, u32[]{:S(2)}) collective-permute-start(bf16[8,1056,128]{2,1,0:T(8,128)(2,1)S(1)} %all_to_all.16.refs_4_), channel_id=1, source_target_pairs={{0,1},{1,0},{2,3},{3,2},{4,5},{5,4},{6,7},{7,6},{8,9},{9,8},{10,11... | collective-permute-start | bytes 6488072 | tf_op jit(solution)/shard_map/ppermute | solution.py:314
  59.7 13.6 %all_to_all.17.refs_4_ = bf16[16,32,128]{2,1,0:T(8,128)(2,1)S(1)} all-to-all(bf16[16,32,128]{2,1,0:T(8,128)(2,1)S(1)} %tile.10), channel_id=1, replica_groups={{0,4,8,12,16,20,24,28,32,36,40,44,48,52,56,60},{2,6,10,14,18,22,26,30,3..., dimensions={0} | all-to-all | bytes 262144 | tf_op jit(solution)/shard_map/all_to_all | solution.py:296
  73.3 0.4 collective-permute-start.2
  73.7 0.0 copy-done
  73.7 0.0 copy-done.1
  73.7 0.0 copy-done.2
  73.7 7.3 %shard_map.49 = (f32[128,2048]{1,0:T(8,128)S(1)}, f32[128,2048]{1,0:T(8,128)S(1)}) custom-call(s32[1]{0:T(128)} %bitcast.block_ref.refs_0_, bf16[128,4096]{1,0:T(8,128)(2,1)S(1)} %copy-done, bf16[128,512]{1,0:T(8,128)(2,1)S(1)} %copy-done.1, bf16[128,512]{1,0:T(8,128)(2,1)S(1)} %copy-done.2, bf16[8,1056,128]{2,1,0:T(8,128)(2,1)S(1)} %all_to_all.16.refs_4_), custom_call_target="tpu_custom_call" | custom-call | flops 2281701376 | bytes 4194304 | tf_op jit(solution)/shard_map/pallas_call | solution.py:267
  81.0 3.6 %shard_map.50.refs_6_ = bf16[128,4096]{1,0:T(8,128)(2,1)} custom-call(s32[1]{0:T(128)} %bitcast.block_ref.refs_0_, bf16[128,4096]{1,0:T(8,128)(2,1)S(1)} %copy-done, bf16[128,512]{1,0:T(8,128)(2,1)S(1)} %copy-done.1, bf16[128,512]{1,0:T(8,128)(2,1)S(1)} %copy-done.2, bf16[16,32,128]{2,1,0:T(8,128)(2,1)S(1)} %all_to_all.17.refs_4_, ...), custom_call_target="tpu_custom_call" | custom-call | flops 134217728 | bytes 4194304 | tf_op jit(solution)/shard_map/pallas_call | solution.py:267
  84.6 0.0 collective-permute-done.2.refs_5_
  84.6 0.0 collective-permute-done.1.refs_4_
  84.6 7.8 %shard_map.51 = bf16[128,4096]{1,0:T(8,128)(2,1)} custom-call(s32[1]{0:T(128)} %bitcast.block_ref.refs_0_, bf16[128,4096]{1,0:T(8,128)(2,1)S(1)} %copy-done, bf16[128,512]{1,0:T(8,128)(2,1)S(1)} %copy-done.1, bf16[128,512]{1,0:T(8,128)(2,1)S(1)} %copy-done.2, ...), custom_call_target="tpu_custom_call", output_to_operand_aliasing={{}: (6, {})} | custom-call | flops 2415919104 | bytes 4194304 | tf_op jit(solution)/shard_map/pallas_call | solution.py:267
  (2 shorter events, 0.0 us)
Async XLA Ops:
  1.8 4.4 %collective-permute-start = (bf16[2,272,128]{2,1,0:T(8,128)(2,1)}, bf16[2,272,128]{2,1,0:T(8,128)(2,1)S(1)}, u32[]{:S(2)}, u32[]{:S(2)}) collective-permute-start(bf16[2,272,128]{2,1,0:T(8,128)(2,1)} %get-tuple-element.10), channel_id=1, source_target_pairs={{0,1},{1,0},{2,3},{3,2},{4,5},{5,4},{6,7},{7,6},{8,9},{9,8},{10,11... | collective-permute-start | bytes 417800 | tf_op jit(solution)/shard_map/ppermute | solution.py:299
  6.3 0.7 copy-start.3
  34.8 38.9 %copy-start = (bf16[128,4096]{1,0:T(8,128)(2,1)S(1)}, bf16[128,4096]{1,0:T(8,128)(2,1)}, u32[]{:S(2)}) copy-start(bf16[128,4096]{1,0:T(8,128)(2,1)} %refs_1_.5) | copy-start | bytes 3145732
  34.8 38.9 %copy-start.1 = (bf16[128,512]{1,0:T(8,128)(2,1)S(1)}, bf16[128,512]{1,0:T(8,128)(2,1)}, u32[]{:S(2)}) copy-start(bf16[128,512]{1,0:T(8,128)(2,1)} %refs_2_.5) | copy-start | bytes 393220
  34.8 38.9 %copy-start.2 = (bf16[128,512]{1,0:T(8,128)(2,1)S(1)}, bf16[128,512]{1,0:T(8,128)(2,1)}, u32[]{:S(2)}) copy-start(bf16[128,512]{1,0:T(8,128)(2,1)} %refs_3_.5) | copy-start | bytes 393220
  57.4 27.2 %collective-permute-start.1 = (bf16[8,1056,128]{2,1,0:T(8,128)(2,1)S(1)}, bf16[8,1056,128]{2,1,0:T(8,128)(2,1)S(1)}, u32[]{:S(2)}, u32[]{:S(2)}) collective-permute-start(bf16[8,1056,128]{2,1,0:T(8,128)(2,1)S(1)} %all_to_all.16.refs_4_), channel_id=1, source_target_pairs={{0,1},{1,0},{2,3},{3,2},{4,5},{5,4},{6,7},{7,6},{8,9},{9,8},{10,11... | collective-permute-start | bytes 6488072 | tf_op jit(solution)/shard_map/ppermute | solution.py:314
  73.3 11.3 %collective-permute-start.2 = (bf16[16,32,128]{2,1,0:T(8,128)(2,1)S(1)}, bf16[16,32,128]{2,1,0:T(8,128)(2,1)S(1)}, u32[]{:S(2)}, u32[]{:S(2)}) collective-permute-start(bf16[16,32,128]{2,1,0:T(8,128)(2,1)S(1)} %all_to_all.17.refs_4_), channel_id=1, source_target_pairs={{0,1},{1,0},{2,3},{3,2},{4,5},{5,4},{6,7},{7,6},{8,9},{9,8},{10,11... | collective-permute-start | bytes 393224 | tf_op jit(solution)/shard_map/ppermute | solution.py:317

commit v3 on v2

v3 whole, which is shorter than its diff:
```python
import functools
import math

import jax
import jax.numpy as jnp
from jax import lax
from jax.experimental import pallas as pl
from jax.experimental.pallas import tpu as pltpu
from jax.sharding import Mesh, PartitionSpec as P

QH = 32
KVH = 4
HD = 128
KEEP = 8
TOK = 128
GROUP = QH // KVH
NX, NY, NZ, NC = 4, 4, 8, 2
DEVICES = NX * NY * NZ * NC
HALF = KVH // NC
FIRST = 16
SECOND = 8
PAIR = NC * KEEP
KEPT_ROWS = HALF * 2 * PAIR
CHUNK = FIRST * PAIR
PIECE = HALF * 2 * TOK // SECOND
SLOT = HALF * 2 * CHUNK + PIECE
PLANE = NY * NZ * NC * KEEP
PART = 4 * PAIR
EXP2_SCALE = math.log2(math.e) / math.sqrt(HD)
MIB = 1024 * 1024

bf16 = jnp.bfloat16
f32 = jnp.float32
in_smem = pl.BlockSpec(memory_space=pltpu.SMEM)
in_vmem = pl.BlockSpec(memory_space=pltpu.VMEM)


def at(x, y, z, core):
    return ((x * NY + y) * NZ + z) * NC + core


def device(core, a, u, zh, zl):
    x, y = (a, u) if core == 0 else (u, a)
    z = (2 * zh + zl) % NZ if core == 0 else (2 * zh - zl) % NZ
    return at(x, y, z, core)


def first_groups():
    return [
        [device(c, a, u, zh, zl) for u in range(4) for zh in range(4)]
        for c in range(2)
        for a in range(4)
        for zl in range(2)
    ]


def second_groups():
    return [
        [device(c, a, u, zh, zl) for a in range(4) for zl in range(2)]
        for c in range(2)
        for u in range(4)
        for zh in range(4)
    ]


def pick_kernel(block_ref, index_ref, keys_ref, values_ref, mine_ref, sent_ref, held_ref, lent_ref):
    core = block_ref[0] % NC
    rows = lax.broadcasted_iota(jnp.int32, (KEEP, TOK), 0)
    lanes = lax.broadcasted_iota(jnp.int32, (KEEP, TOK), 1)
    for out_ref, block_out_ref, owner in (
        (sent_ref, lent_ref, 1 - core),
        (mine_ref, held_ref, core),
    ):
        for h in range(HALF):
            j = owner * HALF + h
            chosen = jnp.zeros((KEEP, TOK), jnp.int32)
            for r in range(KEEP):
                chosen = jnp.where(rows == r, index_ref[0, j, r], chosen)
            onehot = (chosen == lanes).astype(f32).astype(bf16)
            columns = pl.ds(pl.multiple_of(j * HD, HD), HD)
            keys, values = keys_ref[:, columns], values_ref[:, columns]
            key_rows = jnp.dot(onehot, keys, preferred_element_type=f32)
            value_rows = jnp.dot(onehot, values, preferred_element_type=f32)
            out_ref[h] = jnp.concatenate([key_rows, value_rows], axis=0).astype(bf16)
            block_out_ref[2 * h * TOK : (2 * h + 1) * TOK] = keys
            block_out_ref[(2 * h + 1) * TOK : (2 * h + 2) * TOK] = values


def first_kernel(block_ref, mine_ref, came_ref, piece_ref, out_ref):
    core = block_ref[0] % NC
    for h in range(HALF):
        mine = mine_ref[h].astype(f32)
        came = came_ref[h].astype(f32)
        low = jnp.where(core == 0, mine, came)
        high = jnp.where(core == 0, came, mine)
        keys = jnp.concatenate([low[:KEEP], high[:KEEP]], axis=0).astype(bf16)
        values = jnp.concatenate([low[KEEP:], high[KEEP:]], axis=0).astype(bf16)
        for k in range(FIRST):
            out_ref[k, 2 * h * PAIR : (2 * h + 1) * PAIR] = keys
            out_ref[k, (2 * h + 1) * PAIR : (2 * h + 2) * PAIR] = values
    for k in range(FIRST):
        out_ref[k, KEPT_ROWS:] = piece_ref[0]


def second_kernel(in_ref, out_ref):
    for m in range(FIRST):
        for part in range(HALF * 2):
            rows = in_ref[m, part * PAIR : (part + 1) * PAIR]
            put = part * CHUNK + m * PAIR
            for s in range(SECOND):
                out_ref[s, put : put + PAIR] = rows
    for s in range(SECOND):
        out_ref[s, HALF * 2 * CHUNK :] = in_ref[0, KEPT_ROWS:]


def small_call(kernel, operands, in_specs, shapes, limit):
    return pl.pallas_call(
        kernel,
        in_specs=in_specs,
        out_specs=tuple(in_vmem for _ in shapes),
        out_shape=tuple(jax.ShapeDtypeStruct(s, bf16) for s in shapes),
        compiler_params=pltpu.CompilerParams(vmem_limit_bytes=limit * MIB),
    )(*operands)


def attend_kernel(other, block_ref, q_ref, k_ref, v_ref, far_ref, *refs):
    out_ref, key_rows, value_rows, even, odd = refs[-5:]
    block = block_ref[0]
    core = block % NC
    source = 1 - core if other else core
    first_head = source * HALF

    def columns_of(j, width):
        return pl.ds(pl.multiple_of(j * width, width), width)

    def run(planes):
        far = planes * PLANE
        keys = far + 2 * TOK

        def put(h, start, count, new_keys, new_values, valid):
            if valid is None:
                key_rows[h, start : start + count, :] = new_keys
                value_rows[h, start : start + count, :HD] = new_values
                value_rows[h, start : start + count, HD:] = jnp.ones((count, HD), bf16)
            else:
                first_key = k_ref[0:1, columns_of(first_head + h, HD)]
                spare = jnp.ones((count, HD), bf16) - valid
                key_rows[h, start : start + count, :] = new_keys * valid + first_key * spare
                value_rows[h, start : start + count, :HD] = new_values * valid
                value_rows[h, start : start + count, HD:] = valid

        def gather_rows(h):
            rows = lax.broadcasted_iota(jnp.int32, (PART, HD), 0)
            zh, half = rows // PAIR, (rows // KEEP) % NC
            for x in range(planes):
                for i in range(PLANE // PART):
                    slot = jnp.where(source == 0, 2 * x + i // 4, i)
                    row = jnp.where(source == 0, (i % 4) * PART, x * PART) + h * 2 * CHUNK
                    row = pl.multiple_of(row, PART)
                    valid = None
                    if x >= planes - 2 or (x == 0 and i == 0):
                        y = jnp.where(source == 0, i % 4, i // 2)
                        shift = jnp.where(source == 0, i // 4, NZ - i % 2)
                        owner = at(x, y, (2 * zh + shift) % NZ, half)
                        valid = ((owner >= 1) & (owner < block)).astype(f32).astype(bf16)
                    put(
                        h,
                        x * PLANE + i * PART,
                        PART,
                        far_ref[slot, pl.ds(row, PART), :],
                        far_ref[slot, pl.ds(pl.multiple_of(row + CHUNK, PART), PART), :],
                        valid,
                    )
            j = first_head + h
            valid = None
            if planes == 2:
                valid = jnp.where(block > 0, jnp.ones((PIECE, HD), f32), 0.0).astype(bf16)
            for i in range(TOK // PIECE):
                put(
                    h,
                    far + i * PIECE,
                    PIECE,
                    far_ref[h * 4 + i, HALF * 2 * CHUNK :, :],
                    far_ref[h * 4 + 2 + i, HALF * 2 * CHUNK :, :],
                    valid,
                )
            put(
                h,
                far + TOK,
                TOK,
                k_ref[:, columns_of(j, HD)],
                v_ref[:, columns_of(j, HD)],
                None,
            )

        causal = lax.broadcasted_iota(jnp.int32, (TOK, TOK), 1) <= lax.broadcasted_iota(
            jnp.int32, (TOK, TOK), 0
        )

        def scores(unit, held):
            found = lax.dot_general(
                q_ref[:, columns_of(first_head * GROUP + unit, HD)],
                key_rows[unit // GROUP, :keys, :],
                (((1,), (1,)), ((), ())),
                preferred_element_type=f32,
            )
            held[:, : keys - TOK] = found[:, : keys - TOK]
            held[:, keys - TOK : keys] = jnp.where(causal, found[:, keys - TOK :], -1e30)

        def finish(unit, held):
            found = held[:, :keys]
            highest = jnp.max(found, axis=1, keepdims=True)
            weights = jnp.exp2((found - highest) * EXP2_SCALE).astype(bf16)
            summed = jnp.dot(
                weights, value_rows[unit // GROUP, :keys, :], preferred_element_type=f32
            )
            out_ref[:, columns_of(unit, HD)] = (summed[:, :HD] / summed[:, HD:]).astype(bf16)

        units = HALF * GROUP
        gather_rows(0)
        scores(0, even)
        for unit in range(units):
            if unit == GROUP // 2:
                gather_rows(1)
            if unit + 1 < units:
                scores(unit + 1, even if unit % 2 else odd)
            finish(unit, odd if unit % 2 else even)

    near = block // (NY * NZ * NC) < NX // 2
    pl.when(near)(functools.partial(run, NX // 2))
    pl.when(jnp.logical_not(near))(functools.partial(run, NX))


def attend(block, queries, keys, values, far, out, other):
    def half(i, block_ref):
        core = block_ref[0] % NC
        return (0, 1 - core if other else core)

    operands = [queries, keys, values, far]
    in_specs = [in_vmem] * len(operands)
    aliases = {}
    if out is not None:
        operands.append(out)
        in_specs.append(pl.BlockSpec(memory_space=pl.ANY))
        aliases = {len(operands): 0}
    rows = NX * PLANE + 2 * TOK
    work = HALF * GROUP * TOK * rows
    return pl.pallas_call(
        functools.partial(attend_kernel, other),
        grid_spec=pltpu.PrefetchScalarGridSpec(
            num_scalar_prefetch=1,
            grid=(1,),
            in_specs=in_specs,
            out_specs=pl.BlockSpec((TOK, HALF * GROUP * HD), half),
            scratch_shapes=[
                pltpu.VMEM((HALF, rows, HD), bf16),
                pltpu.VMEM((HALF, rows, 2 * HD), bf16),
                pltpu.VMEM((TOK, rows), f32),
                pltpu.VMEM((TOK, rows), f32),
            ],
        ),
        out_shape=jax.ShapeDtypeStruct((TOK, QH * HD), bf16),
        input_output_aliases=aliases,
        compiler_params=pltpu.CompilerParams(vmem_limit_bytes=32 * MIB),
        cost_estimate=pl.CostEstimate(
            flops=4 * work * HD, bytes_accessed=4 * MIB, transcendentals=work
        ),
    )(block, *operands)


def on_device(queries, keys, values, keep_index):
    me = lax.axis_index("d")
    block = me.astype(jnp.int32).reshape(1)
    swap = functools.partial(
        lax.ppermute, axis_name="d", perm=[(i, i ^ 1) for i in range(DEVICES)]
    )

    def gather(slots, groups):
        return lax.all_to_all(slots, "d", 0, 0, tiled=True, axis_index_groups=groups)

    kept, own = (HALF, PAIR, HD), (HALF * 2 * TOK, HD)
    mine, sent, held, lent = small_call(
        pick_kernel,
        (block, keep_index, keys, values),
        [in_smem, in_smem, in_vmem, in_vmem],
        (kept, kept, own, own),
        60,
    )
    lent = lax.ppermute(lent, "d", [(0, 1)])
    anchor = jnp.where(me % NC == 0, held, lent)
    pieces = gather(anchor.reshape(SECOND, PIECE, HD), second_groups())
    (slots,) = small_call(
        first_kernel,
        (block, mine, swap(sent), pieces),
        [in_smem, in_vmem, in_vmem, in_vmem],
        ((FIRST, KEPT_ROWS + PIECE, HD),),
        4,
    )
    near = gather(slots, first_groups())
    (slots,) = small_call(second_kernel, (near,), [in_vmem], ((SECOND, SLOT, HD),), 8)
    far = gather(slots, second_groups())
    far_other = swap(far)

    out = attend(block, queries, keys, values, far, None, False)
    return attend(block, queries, keys, values, far_other, out, True)


def solution(mesh):
    line = Mesh(mesh.devices.reshape(DEVICES), ("d",))
    return jax.shard_map(
        on_device,
        mesh=line,
        in_specs=(P("d", None), P("d", None), P("d", None), P("d", None, None)),
        out_specs=P("d", None),
        check_vma=False,
    )
```

time: 92.8 us -> 78.4 us (0.84)
  the two profiles are of different devices: /device:TPU:1 before, /device:TPU:7 now
where the time goes in v3:
time: 78.4 us; the launch traced here: 77.9 us
  blocking collectives  42.7 us (54%)
  Pallas kernels  16.5 us (21%)
  starting transfers between devices  10.5 us (13%)
  waiting for transfers between devices  6.75 us (9%)
    all_to_all x2, blocking collectives, gather(): lax.all_to_all(slots, 'd', 0, 0, tiled=True, axis_index_groups=groups)  42.7 us
    pallas_call x2, Pallas kernels, attend(): pl.pallas_call(functools.partial(attend_kernel, other), grid_spec=pltpu.P...  14.3 us
    all_to_all x1, starting transfers between devices, gather(): lax.all_to_all(slots, 'd', 0, 0, tiled=True, axis_index_groups=groups)  9.48 us
    all_to_all x1, waiting for transfers between devices, gather(): lax.all_to_all(slots, 'd', 0, 0, tiled=True, axis_index_groups=groups)  5.37 us
    pallas_call x3, Pallas kernels, small_call(): pl.pallas_call(kernel, in_specs=in_specs, out_specs=tuple((in_vmem for _...  2.2 us
  transfers between devices with their start and end apart: 4, of which 2 were waited for; matrix products, arithmetic and copies ran while one was open for 0% of the time, Pallas kernels for 9%

profile of v3, /device:TPU:7, one launch (start us, length us, event | category | flops | bytes accessed | tf_op | source)
XLA Modules:
  0.0 77.9 jit_solution(14180500916184209879)
XLA Ops:
  0.0 1.8 %shard_map.46 = (bf16[2,16,128]{2,1,0:T(8,128)(2,1)}, bf16[2,16,128]{2,1,0:T(8,128)(2,1)}, bf16[512,128]{1,0:T(8,128)(2,1)}, bf16[512,128]{1,0:T(8,128)(2,1)}) custom-call(s32[1]{0:T(128)} %bitcast.block_ref, s32[1,4,8]{2,1,0:T(4,128)} %index_ref.1, bf16[128,512]{1,0:T(8,128)(2,1)} %k_ref.3, bf16[128,512]{1,0:T(8,128)(2,1)} %v_ref.3), custom_call_target="tpu_custom_call" | custom-call | tf_op jit(solution)/shard_map/pallas_call | solution.py:117
  1.8 0.7 collective-permute-start.1
  2.5 0.0 collective-permute-done.1
  2.5 0.7 broadcast_select_fusion
  3.2 9.5 %all-to-all-start = ((bf16[8,64,128]{2,1,0:T(8,128)(2,1)}), bf16[8,64,128]{2,1,0:T(8,128)(2,1)S(1)}, u32[]{:S(2)}, u32[]{:S(2)}) async-start(bf16[8,64,128]{2,1,0:T(8,128)(2,1)} %bitcast.1), calls=%async_computation | async-start | bytes 262144 | tf_op jit(solution)/shard_map/all_to_all | solution.py:279
  12.7 0.0 collective-permute-start
  12.7 1.4 %collective-permute-done.came_ref = bf16[2,16,128]{2,1,0:T(8,128)(2,1)S(1)} collective-permute-done((bf16[2,16,128]{2,1,0:T(8,128)(2,1)}, bf16[2,16,128]{2,1,0:T(8,128)(2,1)S(1)}, u32[]{:S(2)}, u32[]{:S(2)}) %collective-permute-start) | collective-permute-done | bytes 8224 | tf_op jit(solution)/shard_map/ppermute | solution.py:294
  14.0 5.4 %all-to-all-done.piece_ref = bf16[8,64,128]{2,1,0:T(8,128)(2,1)S(1)} async-done(((bf16[8,64,128]{2,1,0:T(8,128)(2,1)}), bf16[8,64,128]{2,1,0:T(8,128)(2,1)S(1)}, u32[]{:S(2)}, u32[]{:S(2)}) %all-to-all-start) | async-done | bytes 131104 | tf_op jit(solution)/shard_map/all_to_all | solution.py:279
  19.4 0.0 copy-start.2
  19.4 0.7 copy-done.2
  20.1 0.1 shard_map.47
  20.2 22.1 %all_to_all.15.in_ref = bf16[16,128,128]{2,1,0:T(8,128)(2,1)S(1)} all-to-all(bf16[16,128,128]{2,1,0:T(8,128)(2,1)S(1)} %shard_map.47), channel_id=1, replica_groups={{0,4,8,12,16,20,24,28,32,36,40,44,48,52,56,60},{2,6,10,14,18,22,26,30,3..., dimensions={0} | all-to-all | bytes 1048576 | tf_op jit(solution)/shard_map/all_to_all | solution.py:279
  42.3 0.4 shard_map.48
  42.6 0.0 copy-start
  42.6 0.0 copy-start.1
  42.7 0.0 copy-start.3
  42.7 20.6 %all_to_all.16.far_ref = bf16[8,1088,128]{2,1,0:T(8,128)(2,1)S(1)} all-to-all(bf16[8,1088,128]{2,1,0:T(8,128)(2,1)S(1)} %shard_map.48), channel_id=1, replica_groups={{0,2,64,66,128,130,192,194},{4,6,68,70,132,134,196,198},{8,10,72,74,136..., dimensions={0} | all-to-all | bytes 4456448 | tf_op jit(solution)/shard_map/all_to_all | solution.py:279
  63.2 0.4 collective-permute-start.2
  63.6 0.0 copy-done
  63.6 0.0 copy-done.1
  63.6 0.0 copy-done.3
  63.6 7.2 %shard_map.49.refs_0_ = bf16[128,4096]{1,0:T(8,128)(2,1)} custom-call(s32[1]{0:T(128)} %bitcast.block_ref, bf16[128,4096]{1,0:T(8,128)(2,1)S(1)} %copy-done.3, bf16[128,512]{1,0:T(8,128)(2,1)S(1)} %copy-done, bf16[128,512]{1,0:T(8,128)(2,1)S(1)} %copy-done.1, bf16[8,1088,128]{2,1,0:T(8,128)(2,1)S(1)} %all_to_all.16.far_ref), custom_call_target="tpu_custom_call" | custom-call | flops 2415919104 | bytes 4194304 | tf_op jit(solution)/shard_map/pallas_call | solution.py:248
  70.8 0.0 collective-permute-done.2.far_ref
  70.9 7.0 %shard_map.50 = bf16[128,4096]{1,0:T(8,128)(2,1)} custom-call(s32[1]{0:T(128)} %bitcast.block_ref, bf16[128,4096]{1,0:T(8,128)(2,1)S(1)} %copy-done.3, bf16[128,512]{1,0:T(8,128)(2,1)S(1)} %copy-done, bf16[128,512]{1,0:T(8,128)(2,1)S(1)} %copy-done.1, bf16[8,1088,128]{2,1,0:T(8,128)(2,1)S(1)} %collective-permute-done.2.far_ref, ...), custom_call_target="tpu_custom_call", output_to_operand_aliasing={{}: (5, {})} | custom-call | flops 2415919104 | bytes 4194304 | tf_op jit(solution)/shard_map/pallas_call | solution.py:248
Async XLA Ops:
  1.8 0.7 collective-permute-start.1
  3.2 16.2 %all-to-all-start = ((bf16[8,64,128]{2,1,0:T(8,128)(2,1)}), bf16[8,64,128]{2,1,0:T(8,128)(2,1)S(1)}, u32[]{:S(2)}, u32[]{:S(2)}) async-start(bf16[8,64,128]{2,1,0:T(8,128)(2,1)} %bitcast.1), calls=%async_computation | async-start | bytes 262144 | tf_op jit(solution)/shard_map/all_to_all | solution.py:279
  12.7 1.4 %collective-permute-start = (bf16[2,16,128]{2,1,0:T(8,128)(2,1)}, bf16[2,16,128]{2,1,0:T(8,128)(2,1)S(1)}, u32[]{:S(2)}, u32[]{:S(2)}) collective-permute-start(bf16[2,16,128]{2,1,0:T(8,128)(2,1)} %get-tuple-element.10), channel_id=1, source_target_pairs={{0,1},{1,0},{2,3},{3,2},{4,5},{5,4},{6,7},{7,6},{8,9},{9,8},{10,11... | collective-permute-start | bytes 24584 | tf_op jit(solution)/shard_map/ppermute | solution.py:294
  19.4 0.7 copy-start.2
  42.6 21.0 %copy-start = (bf16[128,512]{1,0:T(8,128)(2,1)S(1)}, bf16[128,512]{1,0:T(8,128)(2,1)}, u32[]{:S(2)}) copy-start(bf16[128,512]{1,0:T(8,128)(2,1)} %k_ref.3) | copy-start | bytes 393220
  42.6 21.0 %copy-start.1 = (bf16[128,512]{1,0:T(8,128)(2,1)S(1)}, bf16[128,512]{1,0:T(8,128)(2,1)}, u32[]{:S(2)}) copy-start(bf16[128,512]{1,0:T(8,128)(2,1)} %v_ref.3) | copy-start | bytes 393220
  42.7 21.0 %copy-start.3 = (bf16[128,4096]{1,0:T(8,128)(2,1)S(1)}, bf16[128,4096]{1,0:T(8,128)(2,1)}, u32[]{:S(2)}) copy-start(bf16[128,4096]{1,0:T(8,128)(2,1)} %q_ref.3) | copy-start | bytes 3145732
  63.2 7.6 %collective-permute-start.2 = (bf16[8,1088,128]{2,1,0:T(8,128)(2,1)S(1)}, bf16[8,1088,128]{2,1,0:T(8,128)(2,1)S(1)}, u32[]{:S(2)}, u32[]{:S(2)}) collective-permute-start(bf16[8,1088,128]{2,1,0:T(8,128)(2,1)S(1)} %all_to_all.16.far_ref), channel_id=1, source_target_pairs={{0,1},{1,0},{2,3},{3,2},{4,5},{5,4},{6,7},{7,6},{8,9},{9,8},{10,11... | collective-permute-start | bytes 6684680 | tf_op jit(solution)/shard_map/ppermute | solution.py:302

commit v4 on v3

--- a/solution.py
+++ b/solution.py
@@ -20,6 +20,7 @@
 FIRST = 16
 SECOND = 8
 PAIR = NC * KEEP
+KEPT = HALF * PAIR
 KEPT_ROWS = HALF * 2 * PAIR
 CHUNK = FIRST * PAIR
 PIECE = HALF * 2 * TOK // SECOND
@@ -63,14 +64,24 @@
     ]
 
 
-def pick_kernel(block_ref, index_ref, keys_ref, values_ref, mine_ref, sent_ref, held_ref, lent_ref):
-    core = block_ref[0] % NC
+def pick_kernel(
+    block_ref, index_hbm, keys_hbm, values_hbm, mine_ref, sent_ref, index_ref, keys_ref, values_ref, done
+):
+    copies = [
+        pltpu.make_async_copy(source, target, done.at[i])
+        for i, (source, target) in enumerate(
+            ((index_hbm, index_ref), (keys_hbm, keys_ref), (values_hbm, values_ref))
+        )
+    ]
+    for copy in copies:
+        copy.start()
+    for copy in copies:
+        copy.wait()
+    block = block_ref[0]
+    core = block % NC
     rows = lax.broadcasted_iota(jnp.int32, (KEEP, TOK), 0)
     lanes = lax.broadcasted_iota(jnp.int32, (KEEP, TOK), 1)
-    for out_ref, block_out_ref, owner in (
-        (sent_ref, lent_ref, 1 - core),
-        (mine_ref, held_ref, core),
-    ):
+    for out_ref, owner in ((sent_ref, 1 - core), (mine_ref, core)):
         for h in range(HALF):
             j = owner * HALF + h
             chosen = jnp.zeros((KEEP, TOK), jnp.int32)
@@ -81,16 +92,18 @@
             keys, values = keys_ref[:, columns], values_ref[:, columns]
             key_rows = jnp.dot(onehot, keys, preferred_element_type=f32)
             value_rows = jnp.dot(onehot, values, preferred_element_type=f32)
-            out_ref[h] = jnp.concatenate([key_rows, value_rows], axis=0).astype(bf16)
-            block_out_ref[2 * h * TOK : (2 * h + 1) * TOK] = keys
-            block_out_ref[(2 * h + 1) * TOK : (2 * h + 2) * TOK] = values
-
-
-def first_kernel(block_ref, mine_ref, came_ref, piece_ref, out_ref):
+            found = jnp.concatenate([key_rows, value_rows], axis=0).astype(bf16)
+            out_ref[h * PAIR : (h + 1) * PAIR] = found
+            whole = jnp.concatenate([keys, values], axis=0)
+            put = KEPT + 2 * h * TOK
+            out_ref[put : put + 2 * TOK] = jnp.where(block == 0, whole, jnp.zeros_like(whole))
+
+
+def first_kernel(block_ref, mine_ref, came_ref, out_ref):
     core = block_ref[0] % NC
     for h in range(HALF):
-        mine = mine_ref[h].astype(f32)
-        came = came_ref[h].astype(f32)
+        mine = mine_ref[h * PAIR : (h + 1) * PAIR].astype(f32)
+        came = came_ref[h * PAIR : (h + 1) * PAIR].astype(f32)
         low = jnp.where(core == 0, mine, came)
         high = jnp.where(core == 0, came, mine)
         keys = jnp.concatenate([low[:KEEP], high[:KEEP]], axis=0).astype(bf16)
@@ -98,11 +111,9 @@
         for k in range(FIRST):
             out_ref[k, 2 * h * PAIR : (2 * h + 1) * PAIR] = keys
             out_ref[k, (2 * h + 1) * PAIR : (2 * h + 2) * PAIR] = values
-    for k in range(FIRST):
-        out_ref[k, KEPT_ROWS:] = piece_ref[0]
-
-
-def second_kernel(in_ref, out_ref):
+
+
+def second_kernel(in_ref, piece_ref, out_ref):
     for m in range(FIRST):
         for part in range(HALF * 2):
             rows = in_ref[m, part * PAIR : (part + 1) * PAIR]
@@ -110,15 +121,16 @@
             for s in range(SECOND):
                 out_ref[s, put : put + PAIR] = rows
     for s in range(SECOND):
-        out_ref[s, HALF * 2 * CHUNK :] = in_ref[0, KEPT_ROWS:]
-
-
-def small_call(kernel, operands, in_specs, shapes, limit):
+        out_ref[s, HALF * 2 * CHUNK :] = piece_ref[...]
+
+
+def small_call(kernel, operands, in_specs, shapes, limit, scratch=()):
     return pl.pallas_call(
         kernel,
         in_specs=in_specs,
         out_specs=tuple(in_vmem for _ in shapes),
         out_shape=tuple(jax.ShapeDtypeStruct(s, bf16) for s in shapes),
+        scratch_shapes=scratch,
         compiler_params=pltpu.CompilerParams(vmem_limit_bytes=limit * MIB),
     )(*operands)
 
@@ -133,7 +145,7 @@
     def columns_of(j, width):
         return pl.ds(pl.multiple_of(j * width, width), width)
 
-    def run(planes):
+    def run(full, planes):
         far = planes * PLANE
         keys = far + 2 * TOK
 
@@ -158,7 +170,7 @@
                     row = jnp.where(source == 0, (i % 4) * PART, x * PART) + h * 2 * CHUNK
                     row = pl.multiple_of(row, PART)
                     valid = None
-                    if x >= planes - 2 or (x == 0 and i == 0):
+                    if x >= full or (x == 0 and i == 0):
                         y = jnp.where(source == 0, i % 4, i // 2)
                         shift = jnp.where(source == 0, i // 4, NZ - i % 2)
                         owner = at(x, y, (2 * zh + shift) % NZ, half)
@@ -173,7 +185,7 @@
                     )
             j = first_head + h
             valid = None
-            if planes == 2:
+            if full == 0:
                 valid = jnp.where(block > 0, jnp.ones((PIECE, HD), f32), 0.0).astype(bf16)
             for i in range(TOK // PIECE):
                 put(
@@ -226,9 +238,10 @@
                 scores(unit + 1, even if unit % 2 else odd)
             finish(unit, odd if unit % 2 else even)
 
-    near = block // (NY * NZ * NC) < NX // 2
-    pl.when(near)(functools.partial(run, NX // 2))
-    pl.when(jnp.logical_not(near))(functools.partial(run, NX))
+    own_plane = block // (NY * NZ * NC)
+    for low, high in ((0, 1), (1, 2), (2, 4)):
+        here = (own_plane >= low) & (own_plane < high)
+        pl.when(here)(functools.partial(run, low, high))
 
 
 def attend(block, queries, keys, values, far, out, other):
@@ -268,6 +281,35 @@
     )(block, *operands)
 
 
+def send(rows, pairs):
+    return lax.ppermute(rows, "d", pairs)
+
+
+def anchor_at_base(held):
+    pieces = held[: 2 * PIECE]
+    for a in range(1, 4):
+        pairs = [(device(c, 0, 0, 0, 0), device(c, a, 0, 0, 0)) for c in range(NC)]
+        pieces = pieces + send(held[2 * a * PIECE : 2 * (a + 1) * PIECE], pairs)
+    steps = (
+        [(device(c, a, 0, 0, 0), device(c, a, u, 0, 0)) for c in range(NC) for a in range(4)]
+        for u in range(1, 4)
+    )
+    return sum((send(pieces, pairs) for pairs in steps), pieces)
+
+
+def anchor_along_z(pieces):
+    lines = [(c, a, u) for c in range(NC) for a in range(4) for u in range(4)]
+    other = send(
+        pieces[PIECE:], [(device(*line, 0, 0), device(*line, 0, 1)) for line in lines]
+    )
+    piece = pieces[:PIECE] + other
+    steps = (
+        [(device(*line, 0, zl), device(*line, zh, zl)) for line in lines for zl in range(2)]
+        for zh in range(1, 4)
+    )
+    return sum((send(piece, pairs) for pairs in steps), piece)
+
+
 def on_device(queries, keys, values, keep_index):
     me = lax.axis_index("d")
     block = me.astype(jnp.int32).reshape(1)
@@ -278,26 +320,31 @@
     def gather(slots, groups):
         return lax.all_to_all(slots, "d", 0, 0, tiled=True, axis_index_groups=groups)
 
-    kept, own = (HALF, PAIR, HD), (HALF * 2 * TOK, HD)
-    mine, sent, held, lent = small_call(
+    given = (KEPT + HALF * 2 * TOK, HD)
+    mine, sent = small_call(
         pick_kernel,
         (block, keep_index, keys, values),
-        [in_smem, in_smem, in_vmem, in_vmem],
-        (kept, kept, own, own),
-        60,
-    )
-    lent = lax.ppermute(lent, "d", [(0, 1)])
-    anchor = jnp.where(me % NC == 0, held, lent)
-    pieces = gather(anchor.reshape(SECOND, PIECE, HD), second_groups())
+        [in_smem] + [pl.BlockSpec(memory_space=pl.ANY)] * 3,
+        (given, given),
+        4,
+        (
+            pltpu.SMEM(keep_index.shape, jnp.int32),
+            pltpu.VMEM(keys.shape, bf16),
+            pltpu.VMEM(values.shape, bf16),
+            pltpu.SemaphoreType.DMA((3,)),
+        ),
+    )
+    came = swap(sent)
+    base = anchor_at_base(mine[KEPT:] + came[KEPT:])
     (slots,) = small_call(
         first_kernel,
-        (block, mine, swap(sent), pieces),
-        [in_smem, in_vmem, in_vmem, in_vmem],
-        ((FIRST, KEPT_ROWS + PIECE, HD),),
+        (block, mine, came),
+        [in_smem, in_vmem, in_vmem],
+        ((FIRST, KEPT_ROWS, HD),),
         4,
     )
     near = gather(slots, first_groups())
-    (slots,) = small_call(second_kernel, (near,), [in_vmem], ((SECOND, SLOT, HD),), 8)
+    (slots,) = small_call(second_kernel, (near, anchor_along_z(base)), [in_vmem, in_vmem], ((SECOND, SLOT, HD),), 8)
     far = gather(slots, second_groups())
     far_other = swap(far)
 

time: 78.4 us -> 72.5 us (0.925)
  blocking collectives: 42.7 us -> 25.3 us
  starting transfers between devices: 10.5 us -> 21.2 us
  local copies, waits for them, and re-layouts: 0.72 us -> 2.52 us
    all_to_all x2 -> x1, blocking collectives: 42.7 us -> 25.3 us  [gather(): lax.all_to_all(slots, 'd', 0, 0, tiled=True, axis_index_groups=groups)]
    ppermute x2 -> x11, starting transfers between devices: 0.66 us -> 10.6 us  [the longest x10 9.84 us: send(): return lax.ppermute(rows, 'd', pairs)]
    all_to_all x1, waiting for transfers between devices: 5.37 us -> 0.01 us  [gather(): lax.all_to_all(slots, 'd', 0, 0, tiled=True, axis_index_groups=groups)]
    ppermute x2 -> x11, waiting for transfers between devices: 1.38 us -> 6.6 us  [the longest x10 5.6 us: send(): return lax.ppermute(rows, 'd', pairs)]
    unnamed x8 -> x12, local copies, waits for them, and re-layouts: 0.72 us -> 2.51 us
    all_to_all x1, starting transfers between devices: 9.48 us -> 10.6 us  [gather(): lax.all_to_all(slots, 'd', 0, 0, tiled=True, axis_index_groups=groups)]
  transfers between devices with their start and end apart: 4 -> 13, of which waited for: 2 -> 3; matrix products, arithmetic and copies ran while one was open for 0% -> 0% of each run, Pallas kernels for 9% -> 11%
where the time goes in v4:
time: 72.5 us; the launch traced here: 72.1 us
  blocking collectives  25.3 us (35%)
  starting transfers between devices  21.2 us (29%)
  Pallas kernels  16.2 us (22%)
  waiting for transfers between devices  6.6 us (9%)
  local copies, waits for them, and re-layouts  2.52 us (3%)
    all_to_all x1, blocking collectives, gather(): lax.all_to_all(slots, 'd', 0, 0, tiled=True, axis_index_groups=groups)  25.3 us
    pallas_call x2, Pallas kernels, attend(): pl.pallas_call(functools.partial(attend_kernel, other), grid_spec=pltpu.P...  14.3 us
    all_to_all x1, starting transfers between devices, gather(): lax.all_to_all(slots, 'd', 0, 0, tiled=True, axis_index_groups=groups)  10.6 us
    ppermute x10, starting transfers between devices, send(): return lax.ppermute(rows, 'd', pairs)  9.84 us
    ppermute x10, waiting for transfers between devices, send(): return lax.ppermute(rows, 'd', pairs)  5.6 us
    unnamed x12, local copies, waits for them, and re-layouts  2.51 us
    pallas_call x3, Pallas kernels, small_call(): pl.pallas_call(kernel, in_specs=in_specs, out_specs=tuple((in_vmem for _...  1.88 us
  transfers between devices with their start and end apart: 13, of which 3 were waited for; matrix products, arithmetic and copies ran while one was open for 0% of the time, Pallas kernels for 11%

profile of v4, /device:TPU:7, one launch (start us, length us, event | category | flops | bytes accessed | tf_op | source)
XLA Modules:
  0.0 72.1 jit_solution(2540116841203428016)
XLA Ops:
  0.0 0.9 %copy-done = bf16[128,512]{1,0:T(8,128)(2,1)S(1)} copy-done((bf16[128,512]{1,0:T(8,128)(2,1)S(1)}, bf16[128,512]{1,0:T(8,128)(2,1)}, u32[]{:S(2)}) %copy-start) | copy-done | bytes 131096
  0.9 0.9 %copy-done.2 = bf16[128,512]{1,0:T(8,128)(2,1)S(1)} copy-done((bf16[128,512]{1,0:T(8,128)(2,1)S(1)}, bf16[128,512]{1,0:T(8,128)(2,1)}, u32[]{:S(2)}) %copy-start.2) | copy-done | bytes 131096
  1.8 0.7 copy-done.4
  2.5 0.8 %shard_map.46 = (bf16[544,128]{1,0:T(8,128)(2,1)S(1)}, bf16[544,128]{1,0:T(8,128)(2,1)S(1)}) custom-call(s32[1]{0:T(128)} %bitcast.block_ref, s32[1,4,8]{2,1,0:T(4,128)S(1)} %copy-done.4, bf16[128,512]{1,0:T(8,128)(2,1)S(1)} %copy-done, bf16[128,512]{1,0:T(8,128)(2,1)S(1)} %copy-done.2), custom_call_target="tpu_custom_call" | custom-call | tf_op jit(solution)/shard_map/pallas_call | solution.py:128
  3.3 0.8 %collective-permute-start = (bf16[544,128]{1,0:T(8,128)(2,1)S(1)}, bf16[544,128]{1,0:T(8,128)(2,1)S(1)}, u32[]{:S(2)}, u32[]{:S(2)}) collective-permute-start(bf16[544,128]{1,0:T(8,128)(2,1)S(1)} %get-tuple-element.8), channel_id=1, source_target_pairs={{0,1},{1,0},{2,3},{3,2},{4,5},{5,4},{6,7},{7,6},{8,9},{9,8},{10,11... | collective-permute-start | bytes 417800 | tf_op jit(solution)/shard_map/ppermute | solution.py:337
  4.0 1.0 %collective-permute-done.came_ref = bf16[544,128]{1,0:T(8,128)(2,1)S(1)} collective-permute-done((bf16[544,128]{1,0:T(8,128)(2,1)S(1)}, bf16[544,128]{1,0:T(8,128)(2,1)S(1)}, u32[]{:S(2)}, u32[]{:S(2)}) %collective-permute-start) | collective-permute-done | bytes 139296 | tf_op jit(solution)/shard_map/ppermute | solution.py:337
  5.1 0.7 collective-permute-start.1
  5.8 0.7 collective-permute-start.2
  6.4 0.7 collective-permute-start.3
  7.1 0.0 collective-permute-done.1
  7.1 0.0 collective-permute-done.3
  7.1 0.7 collective-permute-start.4
  7.8 0.7 collective-permute-start.5
  8.5 1.3 %collective-permute-start.6 = (bf16[128,128]{1,0:T(8,128)(2,1)S(1)}, bf16[128,128]{1,0:T(8,128)(2,1)S(1)}, u32[]{:S(2)}, u32[]{:S(2)}) collective-permute-start(bf16[128,128]{1,0:T(8,128)(2,1)S(1)} %fusion.1), channel_id=1, source_target_pairs={{0,48},{64,112},{128,176},{192,240},{1,193},{17,209},{33,225},{49,... | collective-permute-start | bytes 98312 | tf_op jit(solution)/shard_map/ppermute | solution.py:285
  9.8 0.7 %shard_map.47 = bf16[16,64,128]{2,1,0:T(8,128)(2,1)} custom-call(s32[1]{0:T(128)} %bitcast.block_ref, bf16[544,128]{1,0:T(8,128)(2,1)S(1)} %get-tuple-element.7.mine_ref, bf16[544,128]{1,0:T(8,128)(2,1)S(1)} %collective-permute-done.came_ref), custom_call_target="tpu_custom_call" | custom-call | tf_op jit(solution)/shard_map/pallas_call | solution.py:128
  10.5 10.6 %all-to-all-start = ((bf16[16,64,128]{2,1,0:T(8,128)(2,1)}), bf16[16,64,128]{2,1,0:T(8,128)(2,1)S(1)}, u32[]{:S(2)}, u32[]{:S(2)}) async-start(bf16[16,64,128]{2,1,0:T(8,128)(2,1)} %shard_map.47), calls=%async_computation | async-start | bytes 524288 | tf_op jit(solution)/shard_map/all_to_all | solution.py:321
  21.1 0.0 collective-permute-done.5
  21.2 1.4 %collective-permute-start.7 = (bf16[64,128]{1,0:T(8,128)(2,1)S(1)}, bf16[64,128]{1,0:T(8,128)(2,1)S(1)}, u32[]{:S(2)}, u32[]{:S(2)}) collective-permute-start(bf16[64,128]{1,0:T(8,128)(2,1)S(1)} %slice.38), channel_id=1, source_target_pairs={{0,2},{16,18},{32,34},{48,50},{64,66},{80,82},{96,98},{112,114},{1... | collective-permute-start | bytes 49160 | tf_op jit(solution)/shard_map/ppermute | solution.py:285
  22.6 4.7 %collective-permute-done.7 = bf16[64,128]{1,0:T(8,128)(2,1)S(1)} collective-permute-done((bf16[64,128]{1,0:T(8,128)(2,1)S(1)}, bf16[64,128]{1,0:T(8,128)(2,1)S(1)}, u32[]{:S(2)}, u32[]{:S(2)}) %collective-permute-start.7) | collective-permute-done | bytes 16416 | tf_op jit(solution)/shard_map/ppermute | solution.py:285
  27.3 1.3 %collective-permute-start.10 = (bf16[64,128]{1,0:T(8,128)(2,1)S(1)}, bf16[64,128]{1,0:T(8,128)(2,1)S(1)}, u32[]{:S(2)}, u32[]{:S(2)}) collective-permute-start(bf16[64,128]{1,0:T(8,128)(2,1)S(1)} %slice_add_fusion.2), channel_id=1, source_target_pairs={{0,12},{2,14},{16,28},{18,30},{32,44},{34,46},{48,60},{50,62},{64,... | collective-permute-start | bytes 49160 | tf_op jit(solution)/shard_map/ppermute | solution.py:285
  28.6 1.3 %collective-permute-start.8 = (bf16[64,128]{1,0:T(8,128)(2,1)S(1)}, bf16[64,128]{1,0:T(8,128)(2,1)S(1)}, u32[]{:S(2)}, u32[]{:S(2)}) collective-permute-start(bf16[64,128]{1,0:T(8,128)(2,1)S(1)} %slice_add_fusion.2), channel_id=1, source_target_pairs={{0,4},{2,6},{16,20},{18,22},{32,36},{34,38},{48,52},{50,54},{64,68... | collective-permute-start | bytes 49160 | tf_op jit(solution)/shard_map/ppermute | solution.py:285
  29.9 1.3 %collective-permute-start.9 = (bf16[64,128]{1,0:T(8,128)(2,1)S(1)}, bf16[64,128]{1,0:T(8,128)(2,1)S(1)}, u32[]{:S(2)}, u32[]{:S(2)}) collective-permute-start(bf16[64,128]{1,0:T(8,128)(2,1)S(1)} %slice_add_fusion.2), channel_id=1, source_target_pairs={{0,8},{2,10},{16,24},{18,26},{32,40},{34,42},{48,56},{50,58},{64,7... | collective-permute-start | bytes 49160 | tf_op jit(solution)/shard_map/ppermute | solution.py:285
  31.2 0.0 collective-permute-done.8
  31.2 0.8 %collective-permute-done.9 = bf16[64,128]{1,0:T(8,128)(2,1)S(1)} collective-permute-done((bf16[64,128]{1,0:T(8,128)(2,1)S(1)}, bf16[64,128]{1,0:T(8,128)(2,1)S(1)}, u32[]{:S(2)}, u32[]{:S(2)}) %collective-permute-start.9) | collective-permute-done | bytes 16416 | tf_op jit(solution)/shard_map/ppermute | solution.py:285
  32.1 0.4 shard_map.48
  32.4 0.0 copy-start.1
  32.4 0.0 copy-start.3
  32.5 0.0 copy-start.5
  32.5 25.3 %all_to_all.10.far_ref = bf16[8,1088,128]{2,1,0:T(8,128)(2,1)S(1)} all-to-all(bf16[8,1088,128]{2,1,0:T(8,128)(2,1)S(1)} %shard_map.48), channel_id=1, replica_groups={{0,2,64,66,128,130,192,194},{4,6,68,70,132,134,196,198},{8,10,72,74,136..., dimensions={0} | all-to-all | bytes 4456448 | tf_op jit(solution)/shard_map/all_to_all | solution.py:321
  57.8 0.0 collective-permute-start.11
  57.8 7.2 %shard_map.49.refs_0_ = bf16[128,4096]{1,0:T(8,128)(2,1)} custom-call(s32[1]{0:T(128)} %bitcast.block_ref, bf16[128,4096]{1,0:T(8,128)(2,1)S(1)} %copy-done.5, bf16[128,512]{1,0:T(8,128)(2,1)S(1)} %copy-done.1, bf16[128,512]{1,0:T(8,128)(2,1)S(1)} %copy-done.3, bf16[8,1088,128]{2,1,0:T(8,128)(2,1)S(1)} %all_to_all.10.far_ref), custom_call_target="tpu_custom_call" | custom-call | flops 2415919104 | bytes 4194304 | tf_op jit(solution)/shard_map/pallas_call | solution.py:261
  65.0 7.0 %shard_map.50 = bf16[128,4096]{1,0:T(8,128)(2,1)} custom-call(s32[1]{0:T(128)} %bitcast.block_ref, bf16[128,4096]{1,0:T(8,128)(2,1)S(1)} %copy-done.5, bf16[128,512]{1,0:T(8,128)(2,1)S(1)} %copy-done.1, bf16[128,512]{1,0:T(8,128)(2,1)S(1)} %copy-done.3, bf16[8,1088,128]{2,1,0:T(8,128)(2,1)S(1)} %collective-permute-done.11.far_ref, ...), custom_call_target="tpu_custom_call", output_to_operand_aliasing={{}: (5, {})} | custom-call | flops 2415919104 | bytes 4194304 | tf_op jit(solution)/shard_map/pallas_call | solution.py:261
  (19 shorter events, 0.1 us)
Async XLA Ops:
  0.0 0.9 %copy-start = (bf16[128,512]{1,0:T(8,128)(2,1)S(1)}, bf16[128,512]{1,0:T(8,128)(2,1)}, u32[]{:S(2)}) copy-start(bf16[128,512]{1,0:T(8,128)(2,1)} %k_ref.3) | copy-start | bytes 393220
  0.9 0.9 %copy-start.2 = (bf16[128,512]{1,0:T(8,128)(2,1)S(1)}, bf16[128,512]{1,0:T(8,128)(2,1)}, u32[]{:S(2)}) copy-start(bf16[128,512]{1,0:T(8,128)(2,1)} %v_ref.3) | copy-start | bytes 393220
  1.8 0.7 copy-start.4
  3.3 1.8 %collective-permute-start = (bf16[544,128]{1,0:T(8,128)(2,1)S(1)}, bf16[544,128]{1,0:T(8,128)(2,1)S(1)}, u32[]{:S(2)}, u32[]{:S(2)}) collective-permute-start(bf16[544,128]{1,0:T(8,128)(2,1)S(1)} %get-tuple-element.8), channel_id=1, source_target_pairs={{0,1},{1,0},{2,3},{3,2},{4,5},{5,4},{6,7},{7,6},{8,9},{9,8},{10,11... | collective-permute-start | bytes 417800 | tf_op jit(solution)/shard_map/ppermute | solution.py:337
  5.1 2.0 %collective-permute-start.1 = (bf16[128,128]{1,0:T(8,128)(2,1)S(1)}, bf16[128,128]{1,0:T(8,128)(2,1)S(1)}, u32[]{:S(2)}, u32[]{:S(2)}) collective-permute-start(bf16[128,128]{1,0:T(8,128)(2,1)S(1)} %get-tuple-element.9), channel_id=1, source_target_pairs={{0,64},{1,17}} | collective-permute-start | bytes 98312 | tf_op jit(solution)/shard_map/ppermute | solution.py:285
  5.8 1.4 %collective-permute-start.2 = (bf16[128,128]{1,0:T(8,128)(2,1)S(1)}, bf16[128,128]{1,0:T(8,128)(2,1)S(1)}, u32[]{:S(2)}, u32[]{:S(2)}) collective-permute-start(bf16[128,128]{1,0:T(8,128)(2,1)S(1)} %get-tuple-element.11), channel_id=1, source_target_pairs={{0,128},{1,33}} | collective-permute-start | bytes 98312 | tf_op jit(solution)/shard_map/ppermute | solution.py:285
  6.4 0.7 collective-permute-start.3
  7.1 14.0 %collective-permute-start.4 = (bf16[128,128]{1,0:T(8,128)(2,1)S(1)}, bf16[128,128]{1,0:T(8,128)(2,1)S(1)}, u32[]{:S(2)}, u32[]{:S(2)}) collective-permute-start(bf16[128,128]{1,0:T(8,128)(2,1)S(1)} %fusion.1), channel_id=1, source_target_pairs={{0,16},{64,80},{128,144},{192,208},{1,65},{17,81},{33,97},{49,113}} | collective-permute-start | bytes 98312 | tf_op jit(solution)/shard_map/ppermute | solution.py:285
  7.8 13.3 %collective-permute-start.5 = (bf16[128,128]{1,0:T(8,128)(2,1)S(1)}, bf16[128,128]{1,0:T(8,128)(2,1)S(1)}, u32[]{:S(2)}, u32[]{:S(2)}) collective-permute-start(bf16[128,128]{1,0:T(8,128)(2,1)S(1)} %fusion.1), channel_id=1, source_target_pairs={{0,32},{64,96},{128,160},{192,224},{1,129},{17,145},{33,161},{49,1... | collective-permute-start | bytes 98312 | tf_op jit(solution)/shard_map/ppermute | solution.py:285
  8.5 12.7 %collective-permute-start.6 = (bf16[128,128]{1,0:T(8,128)(2,1)S(1)}, bf16[128,128]{1,0:T(8,128)(2,1)S(1)}, u32[]{:S(2)}, u32[]{:S(2)}) collective-permute-start(bf16[128,128]{1,0:T(8,128)(2,1)S(1)} %fusion.1), channel_id=1, source_target_pairs={{0,48},{64,112},{128,176},{192,240},{1,193},{17,209},{33,225},{49,... | collective-permute-start | bytes 98312 | tf_op jit(solution)/shard_map/ppermute | solution.py:285
  10.5 21.5 %all-to-all-start = ((bf16[16,64,128]{2,1,0:T(8,128)(2,1)}), bf16[16,64,128]{2,1,0:T(8,128)(2,1)S(1)}, u32[]{:S(2)}, u32[]{:S(2)}) async-start(bf16[16,64,128]{2,1,0:T(8,128)(2,1)} %shard_map.47), calls=%async_computation | async-start | bytes 524288 | tf_op jit(solution)/shard_map/all_to_all | solution.py:321
  21.2 6.1 %collective-permute-start.7 = (bf16[64,128]{1,0:T(8,128)(2,1)S(1)}, bf16[64,128]{1,0:T(8,128)(2,1)S(1)}, u32[]{:S(2)}, u32[]{:S(2)}) collective-permute-start(bf16[64,128]{1,0:T(8,128)(2,1)S(1)} %slice.38), channel_id=1, source_target_pairs={{0,2},{16,18},{32,34},{48,50},{64,66},{80,82},{96,98},{112,114},{1... | collective-permute-start | bytes 49160 | tf_op jit(solution)/shard_map/ppermute | solution.py:285
  27.3 3.9 %collective-permute-start.10 = (bf16[64,128]{1,0:T(8,128)(2,1)S(1)}, bf16[64,128]{1,0:T(8,128)(2,1)S(1)}, u32[]{:S(2)}, u32[]{:S(2)}) collective-permute-start(bf16[64,128]{1,0:T(8,128)(2,1)S(1)} %slice_add_fusion.2), channel_id=1, source_target_pairs={{0,12},{2,14},{16,28},{18,30},{32,44},{34,46},{48,60},{50,62},{64,... | collective-permute-start | bytes 49160 | tf_op jit(solution)/shard_map/ppermute | solution.py:285
  28.6 2.6 %collective-permute-start.8 = (bf16[64,128]{1,0:T(8,128)(2,1)S(1)}, bf16[64,128]{1,0:T(8,128)(2,1)S(1)}, u32[]{:S(2)}, u32[]{:S(2)}) collective-permute-start(bf16[64,128]{1,0:T(8,128)(2,1)S(1)} %slice_add_fusion.2), channel_id=1, source_target_pairs={{0,4},{2,6},{16,20},{18,22},{32,36},{34,38},{48,52},{50,54},{64,68... | collective-permute-start | bytes 49160 | tf_op jit(solution)/shard_map/ppermute | solution.py:285
  29.9 2.1 %collective-permute-start.9 = (bf16[64,128]{1,0:T(8,128)(2,1)S(1)}, bf16[64,128]{1,0:T(8,128)(2,1)S(1)}, u32[]{:S(2)}, u32[]{:S(2)}) collective-permute-start(bf16[64,128]{1,0:T(8,128)(2,1)S(1)} %slice_add_fusion.2), channel_id=1, source_target_pairs={{0,8},{2,10},{16,24},{18,26},{32,40},{34,42},{48,56},{50,58},{64,7... | collective-permute-start | bytes 49160 | tf_op jit(solution)/shard_map/ppermute | solution.py:285
  32.4 25.3 %copy-start.1 = (bf16[128,512]{1,0:T(8,128)(2,1)S(1)}, bf16[128,512]{1,0:T(8,128)(2,1)}, u32[]{:S(2)}) copy-start(bf16[128,512]{1,0:T(8,128)(2,1)} %k_ref.3) | copy-start | bytes 393220
  32.4 25.3 %copy-start.3 = (bf16[128,512]{1,0:T(8,128)(2,1)S(1)}, bf16[128,512]{1,0:T(8,128)(2,1)}, u32[]{:S(2)}) copy-start(bf16[128,512]{1,0:T(8,128)(2,1)} %v_ref.3) | copy-start | bytes 393220
  32.5 25.3 %copy-start.5 = (bf16[128,4096]{1,0:T(8,128)(2,1)S(1)}, bf16[128,4096]{1,0:T(8,128)(2,1)}, u32[]{:S(2)}) copy-start(bf16[128,4096]{1,0:T(8,128)(2,1)} %q_ref.3) | copy-start | bytes 3145732
  57.8 7.3 %collective-permute-start.11 = (bf16[8,1088,128]{2,1,0:T(8,128)(2,1)S(1)}, bf16[8,1088,128]{2,1,0:T(8,128)(2,1)S(1)}, u32[]{:S(2)}, u32[]{:S(2)}) collective-permute-start(bf16[8,1088,128]{2,1,0:T(8,128)(2,1)S(1)} %all_to_all.10.far_ref), channel_id=1, source_target_pairs={{0,1},{1,0},{2,3},{3,2},{4,5},{5,4},{6,7},{7,6},{8,9},{9,8},{10,11... | collective-permute-start | bytes 6684680 | tf_op jit(solution)/shard_map/ppermute | solution.py:349

commit v5 on v4

--- a/solution.py
+++ b/solution.py
@@ -64,19 +64,7 @@
     ]
 
 
-def pick_kernel(
-    block_ref, index_hbm, keys_hbm, values_hbm, mine_ref, sent_ref, index_ref, keys_ref, values_ref, done
-):
-    copies = [
-        pltpu.make_async_copy(source, target, done.at[i])
-        for i, (source, target) in enumerate(
-            ((index_hbm, index_ref), (keys_hbm, keys_ref), (values_hbm, values_ref))
-        )
-    ]
-    for copy in copies:
-        copy.start()
-    for copy in copies:
-        copy.wait()
+def pick_kernel(block_ref, index_ref, both_ref, mine_ref, sent_ref):
     block = block_ref[0]
     core = block % NC
     rows = lax.broadcasted_iota(jnp.int32, (KEEP, TOK), 0)
@@ -88,8 +76,8 @@
             for r in range(KEEP):
                 chosen = jnp.where(rows == r, index_ref[0, j, r], chosen)
             onehot = (chosen == lanes).astype(f32).astype(bf16)
-            columns = pl.ds(pl.multiple_of(j * HD, HD), HD)
-            keys, values = keys_ref[:, columns], values_ref[:, columns]
+            keys = both_ref[:, pl.ds(pl.multiple_of(j * HD, HD), HD)]
+            values = both_ref[:, pl.ds(pl.multiple_of((KVH + j) * HD, HD), HD)]
             key_rows = jnp.dot(onehot, keys, preferred_element_type=f32)
             value_rows = jnp.dot(onehot, values, preferred_element_type=f32)
             found = jnp.concatenate([key_rows, value_rows], axis=0).astype(bf16)
@@ -124,19 +112,18 @@
         out_ref[s, HALF * 2 * CHUNK :] = piece_ref[...]
 
 
-def small_call(kernel, operands, in_specs, shapes, limit, scratch=()):
+def small_call(kernel, operands, in_specs, shapes, limit):
     return pl.pallas_call(
         kernel,
         in_specs=in_specs,
         out_specs=tuple(in_vmem for _ in shapes),
         out_shape=tuple(jax.ShapeDtypeStruct(s, bf16) for s in shapes),
-        scratch_shapes=scratch,
         compiler_params=pltpu.CompilerParams(vmem_limit_bytes=limit * MIB),
     )(*operands)
 
 
 def attend_kernel(other, block_ref, q_ref, k_ref, v_ref, far_ref, *refs):
-    out_ref, key_rows, value_rows, even, odd = refs[-5:]
+    out_ref, key_rows, value_rows, even, odd, third = refs[-6:]
     block = block_ref[0]
     core = block % NC
     source = 1 - core if other else core
@@ -192,8 +179,8 @@
                     h,
                     far + i * PIECE,
                     PIECE,
-                    far_ref[h * 4 + i, HALF * 2 * CHUNK :, :],
-                    far_ref[h * 4 + 2 + i, HALF * 2 * CHUNK :, :],
+                    far_ref[2 * i + h, HALF * 2 * CHUNK :, :],
+                    far_ref[2 * (i + 2) + h, HALF * 2 * CHUNK :, :],
                     valid,
                 )
             put(
@@ -230,13 +217,15 @@
 
         units = HALF * GROUP
         gather_rows(0)
+        buffers = (even, odd, third)
         scores(0, even)
+        scores(1, odd)
         for unit in range(units):
             if unit == GROUP // 2:
                 gather_rows(1)
-            if unit + 1 < units:
-                scores(unit + 1, even if unit % 2 else odd)
-            finish(unit, odd if unit % 2 else even)
+            if unit + 2 < units:
+                scores(unit + 2, buffers[(unit + 2) % 3])
+            finish(unit, buffers[unit % 3])
 
     own_plane = block // (NY * NZ * NC)
     for low, high in ((0, 1), (1, 2), (2, 4)):
@@ -270,6 +259,7 @@
                 pltpu.VMEM((HALF, rows, 2 * HD), bf16),
                 pltpu.VMEM((TOK, rows), f32),
                 pltpu.VMEM((TOK, rows), f32),
+                pltpu.VMEM((TOK, rows), f32),
             ],
         ),
         out_shape=jax.ShapeDtypeStruct((TOK, QH * HD), bf16),
@@ -285,26 +275,28 @@
     return lax.ppermute(rows, "d", pairs)
 
 
-def anchor_at_base(held):
-    pieces = held[: 2 * PIECE]
-    for a in range(1, 4):
-        pairs = [(device(c, 0, 0, 0, 0), device(c, a, 0, 0, 0)) for c in range(NC)]
-        pieces = pieces + send(held[2 * a * PIECE : 2 * (a + 1) * PIECE], pairs)
+def anchor_over_second(held):
+    half = HALF * TOK
+    rows = held[:half] + send(
+        held[half:], [(device(c, 0, 0, 0, 0), device(c, 0, 0, 0, 1)) for c in range(NC)]
+    )
     steps = (
-        [(device(c, a, 0, 0, 0), device(c, a, u, 0, 0)) for c in range(NC) for a in range(4)]
+        [(device(c, 0, 0, 0, zl), device(c, a, 0, 0, zl)) for c in range(NC) for zl in range(2)]
+        for a in range(1, 4)
+    )
+    pieces = (rows[a * PIECE : (a + 1) * PIECE] for a in range(1, 4))
+    return sum((send(piece, pairs) for piece, pairs in zip(pieces, steps)), rows[:PIECE])
+
+
+def anchor_over_first(piece):
+    lines = [(c, a, zl) for c in range(NC) for a in range(4) for zl in range(2)]
+    steps = (
+        [(device(c, a, 0, 0, zl), device(c, a, u, 0, zl)) for c, a, zl in lines]
         for u in range(1, 4)
     )
-    return sum((send(pieces, pairs) for pairs in steps), pieces)
-
-
-def anchor_along_z(pieces):
-    lines = [(c, a, u) for c in range(NC) for a in range(4) for u in range(4)]
-    other = send(
-        pieces[PIECE:], [(device(*line, 0, 0), device(*line, 0, 1)) for line in lines]
-    )
-    piece = pieces[:PIECE] + other
+    piece = sum((send(piece, pairs) for pairs in steps), piece)
     steps = (
-        [(device(*line, 0, zl), device(*line, zh, zl)) for line in lines for zl in range(2)]
+        [(device(c, a, u, 0, zl), device(c, a, u, zh, zl)) for c, a, zl in lines for u in range(4)]
         for zh in range(1, 4)
     )
     return sum((send(piece, pairs) for pairs in steps), piece)
@@ -323,19 +315,13 @@
     given = (KEPT + HALF * 2 * TOK, HD)
     mine, sent = small_call(
         pick_kernel,
-        (block, keep_index, keys, values),
-        [in_smem] + [pl.BlockSpec(memory_space=pl.ANY)] * 3,
+        (block, keep_index, jnp.concatenate([keys, values], axis=1)),
+        [in_smem, in_smem, in_vmem],
         (given, given),
         4,
-        (
-            pltpu.SMEM(keep_index.shape, jnp.int32),
-            pltpu.VMEM(keys.shape, bf16),
-            pltpu.VMEM(values.shape, bf16),
-            pltpu.SemaphoreType.DMA((3,)),
-        ),
     )
     came = swap(sent)
-    base = anchor_at_base(mine[KEPT:] + came[KEPT:])
+    base = anchor_over_second(mine[KEPT:] + came[KEPT:])
     (slots,) = small_call(
         first_kernel,
         (block, mine, came),
@@ -344,7 +330,7 @@
         4,
     )
     near = gather(slots, first_groups())
-    (slots,) = small_call(second_kernel, (near, anchor_along_z(base)), [in_vmem, in_vmem], ((SECOND, SLOT, HD),), 8)
+    (slots,) = small_call(second_kernel, (near, anchor_over_first(base)), [in_vmem, in_vmem], ((SECOND, SLOT, HD),), 8)
     far = gather(slots, second_groups())
     far_other = swap(far)
 

time: 72.5 us -> 71.2 us (0.982)
  blocking collectives: 25.3 us -> 21.9 us
  starting transfers between devices: 21.2 us -> 23.5 us
  local copies, waits for them, and re-layouts: 2.52 us -> 0.71 us
  other arithmetic: 0.05 us -> 1.04 us
  waiting for transfers between devices: 6.6 us -> 7.42 us
    all_to_all x1, blocking collectives: 25.3 us -> 21.9 us  [gather(): lax.all_to_all(slots, 'd', 0, 0, tiled=True, axis_index_groups=groups)]
    all_to_all x1, starting transfers between devices: 10.6 us -> 13.6 us  [gather(): lax.all_to_all(slots, 'd', 0, 0, tiled=True, axis_index_groups=groups)]
    unnamed x12 -> x8, local copies, waits for them, and re-layouts: 2.51 us -> 0.7 us
    concatenate x0 -> x1, other arithmetic: none -> 0.99 us  [on_device(): jnp.concatenate([keys, values], axis=1)]
    ppermute x10, waiting for transfers between devices: 5.6 us -> 6.41 us  [send(): return lax.ppermute(rows, 'd', pairs)]
where the time goes in v5:
time: 71.2 us; the launch traced here: 70.7 us
  starting transfers between devices  23.5 us (33%)
  blocking collectives  21.9 us (31%)
  Pallas kernels  16 us (22%)
  waiting for transfers between devices  7.42 us (10%)
  other arithmetic  1.04 us (1%)
    all_to_all x1, blocking collectives, gather(): lax.all_to_all(slots, 'd', 0, 0, tiled=True, axis_index_groups=groups)  21.9 us
    pallas_call x2, Pallas kernels, attend(): pl.pallas_call(functools.partial(attend_kernel, other), grid_spec=pltpu.P...  14.1 us
    all_to_all x1, starting transfers between devices, gather(): lax.all_to_all(slots, 'd', 0, 0, tiled=True, axis_index_groups=groups)  13.6 us
    ppermute x10, starting transfers between devices, send(): return lax.ppermute(rows, 'd', pairs)  9.13 us
    ppermute x10, waiting for transfers between devices, send(): return lax.ppermute(rows, 'd', pairs)  6.41 us
    pallas_call x3, Pallas kernels, small_call(): pl.pallas_call(kernel, in_specs=in_specs, out_specs=tuple((in_vmem for _...  1.85 us
  transfers between devices with their start and end apart: 13, of which 3 were waited for; matrix products, arithmetic and copies ran while one was open for 0% of the time, Pallas kernels for 11%

profile of v5, /device:TPU:7, one launch (start us, length us, event | category | flops | bytes accessed | tf_op | source)
XLA Modules:
  0.0 70.7 jit_solution(1991575041146866163)
XLA Ops:
  0.0 1.0 %pad_maximum_fusion.both_ref = bf16[128,1024]{1,0:T(8,128)(2,1)S(1)} fusion(bf16[128,512]{1,0:T(8,128)(2,1)} %v_ref.3, bf16[128,512]{1,0:T(8,128)(2,1)} %k_ref.3), kind=kLoop, calls=%fused_computation | loop fusion | flops 524288 | bytes 524288 | tf_op jit(solution)/shard_map/concatenate | solution.py:318
  1.0 0.0 copy-start.2
  1.0 0.7 copy-done.2
  1.7 0.8 %shard_map.46 = (bf16[544,128]{1,0:T(8,128)(2,1)S(1)}, bf16[544,128]{1,0:T(8,128)(2,1)S(1)}) custom-call(s32[1]{0:T(128)} %bitcast.block_ref, s32[1,4,8]{2,1,0:T(4,128)S(1)} %copy-done.2, bf16[128,1024]{1,0:T(8,128)(2,1)S(1)} %pad_maximum_fusion.both_ref), custom_call_target="tpu_custom_call" | custom-call | tf_op jit(solution)/shard_map/pallas_call | solution.py:116
  2.4 0.7 %collective-permute-start = (bf16[544,128]{1,0:T(8,128)(2,1)S(1)}, bf16[544,128]{1,0:T(8,128)(2,1)S(1)}, u32[]{:S(2)}, u32[]{:S(2)}) collective-permute-start(bf16[544,128]{1,0:T(8,128)(2,1)S(1)} %get-tuple-element.8), channel_id=1, source_target_pairs={{0,1},{1,0},{2,3},{3,2},{4,5},{5,4},{6,7},{7,6},{8,9},{9,8},{10,11... | collective-permute-start | bytes 417800 | tf_op jit(solution)/shard_map/ppermute | solution.py:323
  3.2 1.0 %collective-permute-done.came_ref = bf16[544,128]{1,0:T(8,128)(2,1)S(1)} collective-permute-done((bf16[544,128]{1,0:T(8,128)(2,1)S(1)}, bf16[544,128]{1,0:T(8,128)(2,1)S(1)}, u32[]{:S(2)}, u32[]{:S(2)}) %collective-permute-start) | collective-permute-done | bytes 139296 | tf_op jit(solution)/shard_map/ppermute | solution.py:323
  4.2 0.7 collective-permute-start.1
  4.9 0.0 collective-permute-done.1
  4.9 0.7 collective-permute-start.2
  5.6 0.7 collective-permute-start.3
  6.2 0.7 collective-permute-start.4
  6.9 0.7 %shard_map.47 = bf16[16,64,128]{2,1,0:T(8,128)(2,1)} custom-call(s32[1]{0:T(128)} %bitcast.block_ref, bf16[544,128]{1,0:T(8,128)(2,1)S(1)} %get-tuple-element.7.mine_ref, bf16[544,128]{1,0:T(8,128)(2,1)S(1)} %collective-permute-done.came_ref), custom_call_target="tpu_custom_call" | custom-call | tf_op jit(solution)/shard_map/pallas_call | solution.py:116
  7.7 13.6 %all-to-all-start = ((bf16[16,64,128]{2,1,0:T(8,128)(2,1)}), bf16[16,64,128]{2,1,0:T(8,128)(2,1)S(1)}, u32[]{:S(2)}, u32[]{:S(2)}) async-start(bf16[16,64,128]{2,1,0:T(8,128)(2,1)} %shard_map.47), calls=%async_computation | async-start | bytes 524288 | tf_op jit(solution)/shard_map/all_to_all | solution.py:313
  21.3 0.0 collective-permute-done.3
  21.3 0.7 collective-permute-start.5
  22.0 0.7 collective-permute-start.6
  22.6 1.3 %collective-permute-start.7 = (bf16[64,128]{1,0:T(8,128)(2,1)S(1)}, bf16[64,128]{1,0:T(8,128)(2,1)S(1)}, u32[]{:S(2)}, u32[]{:S(2)}) collective-permute-start(bf16[64,128]{1,0:T(8,128)(2,1)S(1)} %fusion.1), channel_id=1, source_target_pairs={{0,48},{2,50},{64,112},{66,114},{128,176},{130,178},{192,240},{194... | collective-permute-start | bytes 49160 | tf_op jit(solution)/shard_map/ppermute | solution.py:275
  23.9 0.0 collective-permute-done.5
  23.9 0.0 collective-permute-done.6
  24.0 5.6 %collective-permute-done.7 = bf16[64,128]{1,0:T(8,128)(2,1)S(1)} collective-permute-done((bf16[64,128]{1,0:T(8,128)(2,1)S(1)}, bf16[64,128]{1,0:T(8,128)(2,1)S(1)}, u32[]{:S(2)}, u32[]{:S(2)}) %collective-permute-start.7) | collective-permute-done | bytes 16416 | tf_op jit(solution)/shard_map/ppermute | solution.py:275
  29.5 1.3 %collective-permute-start.10 = (bf16[64,128]{1,0:T(8,128)(2,1)S(1)}, bf16[64,128]{1,0:T(8,128)(2,1)S(1)}, u32[]{:S(2)}, u32[]{:S(2)}) collective-permute-start(bf16[64,128]{1,0:T(8,128)(2,1)S(1)} %add_add_fusion.1), channel_id=1, source_target_pairs={{0,12},{16,28},{32,44},{48,60},{2,14},{18,30},{34,46},{50,62},{64,... | collective-permute-start | bytes 49160 | tf_op jit(solution)/shard_map/ppermute | solution.py:275
  30.8 1.3 %collective-permute-start.8 = (bf16[64,128]{1,0:T(8,128)(2,1)S(1)}, bf16[64,128]{1,0:T(8,128)(2,1)S(1)}, u32[]{:S(2)}, u32[]{:S(2)}) collective-permute-start(bf16[64,128]{1,0:T(8,128)(2,1)S(1)} %add_add_fusion.1), channel_id=1, source_target_pairs={{0,4},{16,20},{32,36},{48,52},{2,6},{18,22},{34,38},{50,54},{64,68... | collective-permute-start | bytes 49160 | tf_op jit(solution)/shard_map/ppermute | solution.py:275
  32.1 1.3 %collective-permute-start.9 = (bf16[64,128]{1,0:T(8,128)(2,1)S(1)}, bf16[64,128]{1,0:T(8,128)(2,1)S(1)}, u32[]{:S(2)}, u32[]{:S(2)}) collective-permute-start(bf16[64,128]{1,0:T(8,128)(2,1)S(1)} %add_add_fusion.1), channel_id=1, source_target_pairs={{0,8},{16,24},{32,40},{48,56},{2,10},{18,26},{34,42},{50,58},{64,7... | collective-permute-start | bytes 49160 | tf_op jit(solution)/shard_map/ppermute | solution.py:275
  33.4 0.0 collective-permute-done.10
  33.4 0.8 %collective-permute-done.9 = bf16[64,128]{1,0:T(8,128)(2,1)S(1)} collective-permute-done((bf16[64,128]{1,0:T(8,128)(2,1)S(1)}, bf16[64,128]{1,0:T(8,128)(2,1)S(1)}, u32[]{:S(2)}, u32[]{:S(2)}) %collective-permute-start.9) | collective-permute-done | bytes 16416 | tf_op jit(solution)/shard_map/ppermute | solution.py:275
  34.3 0.4 shard_map.48
  34.6 0.0 copy-start
  34.7 0.0 copy-start.1
  34.7 0.0 copy-start.3
  34.7 21.9 %all_to_all.10.far_ref = bf16[8,1088,128]{2,1,0:T(8,128)(2,1)S(1)} all-to-all(bf16[8,1088,128]{2,1,0:T(8,128)(2,1)S(1)} %shard_map.48), channel_id=1, replica_groups={{0,2,64,66,128,130,192,194},{4,6,68,70,132,134,196,198},{8,10,72,74,136..., dimensions={0} | all-to-all | bytes 4456448 | tf_op jit(solution)/shard_map/all_to_all | solution.py:313
  56.6 7.2 %shard_map.49.refs_0_ = bf16[128,4096]{1,0:T(8,128)(2,1)} custom-call(s32[1]{0:T(128)} %bitcast.block_ref, bf16[128,4096]{1,0:T(8,128)(2,1)S(1)} %copy-done.3, bf16[128,512]{1,0:T(8,128)(2,1)S(1)} %copy-done, bf16[128,512]{1,0:T(8,128)(2,1)S(1)} %copy-done.1, bf16[8,1088,128]{2,1,0:T(8,128)(2,1)S(1)} %all_to_all.10.far_ref), custom_call_target="tpu_custom_call" | custom-call | flops 2415919104 | bytes 4194304 | tf_op jit(solution)/shard_map/pallas_call | solution.py:250
  63.8 7.0 %shard_map.50 = bf16[128,4096]{1,0:T(8,128)(2,1)} custom-call(s32[1]{0:T(128)} %bitcast.block_ref, bf16[128,4096]{1,0:T(8,128)(2,1)S(1)} %copy-done.3, bf16[128,512]{1,0:T(8,128)(2,1)S(1)} %copy-done, bf16[128,512]{1,0:T(8,128)(2,1)S(1)} %copy-done.1, bf16[8,1088,128]{2,1,0:T(8,128)(2,1)S(1)} %collective-permute-done.11.far_ref, ...), custom_call_target="tpu_custom_call", output_to_operand_aliasing={{}: (5, {})} | custom-call | flops 2415919104 | bytes 4194304 | tf_op jit(solution)/shard_map/pallas_call | solution.py:250
  (16 shorter events, 0.1 us)
Async XLA Ops:
  1.0 0.7 copy-start.2
  2.4 1.7 %collective-permute-start = (bf16[544,128]{1,0:T(8,128)(2,1)S(1)}, bf16[544,128]{1,0:T(8,128)(2,1)S(1)}, u32[]{:S(2)}, u32[]{:S(2)}) collective-permute-start(bf16[544,128]{1,0:T(8,128)(2,1)S(1)} %get-tuple-element.8), channel_id=1, source_target_pairs={{0,1},{1,0},{2,3},{3,2},{4,5},{5,4},{6,7},{7,6},{8,9},{9,8},{10,11... | collective-permute-start | bytes 417800 | tf_op jit(solution)/shard_map/ppermute | solution.py:323
  4.2 0.7 collective-permute-start.1
  4.9 16.3 %collective-permute-start.2 = (bf16[64,128]{1,0:T(8,128)(2,1)S(1)}, bf16[64,128]{1,0:T(8,128)(2,1)S(1)}, u32[]{:S(2)}, u32[]{:S(2)}) collective-permute-start(bf16[64,128]{1,0:T(8,128)(2,1)S(1)} %get-tuple-element.9), channel_id=1, source_target_pairs={{0,64},{2,66},{1,17},{15,31}} | collective-permute-start | bytes 49160 | tf_op jit(solution)/shard_map/ppermute | solution.py:275
  5.6 15.7 %collective-permute-start.3 = (bf16[64,128]{1,0:T(8,128)(2,1)S(1)}, bf16[64,128]{1,0:T(8,128)(2,1)S(1)}, u32[]{:S(2)}, u32[]{:S(2)}) collective-permute-start(bf16[64,128]{1,0:T(8,128)(2,1)S(1)} %get-tuple-element.11), channel_id=1, source_target_pairs={{0,128},{2,130},{1,33},{15,47}} | collective-permute-start | bytes 49160 | tf_op jit(solution)/shard_map/ppermute | solution.py:275
  6.2 15.0 %collective-permute-start.4 = (bf16[64,128]{1,0:T(8,128)(2,1)S(1)}, bf16[64,128]{1,0:T(8,128)(2,1)S(1)}, u32[]{:S(2)}, u32[]{:S(2)}) collective-permute-start(bf16[64,128]{1,0:T(8,128)(2,1)S(1)} %get-tuple-element.10), channel_id=1, source_target_pairs={{0,192},{2,194},{1,49},{15,63}} | collective-permute-start | bytes 49160 | tf_op jit(solution)/shard_map/ppermute | solution.py:275
  7.7 26.6 %all-to-all-start = ((bf16[16,64,128]{2,1,0:T(8,128)(2,1)}), bf16[16,64,128]{2,1,0:T(8,128)(2,1)S(1)}, u32[]{:S(2)}, u32[]{:S(2)}) async-start(bf16[16,64,128]{2,1,0:T(8,128)(2,1)} %shard_map.47), calls=%async_computation | async-start | bytes 524288 | tf_op jit(solution)/shard_map/all_to_all | solution.py:313
  21.3 2.6 %collective-permute-start.5 = (bf16[64,128]{1,0:T(8,128)(2,1)S(1)}, bf16[64,128]{1,0:T(8,128)(2,1)S(1)}, u32[]{:S(2)}, u32[]{:S(2)}) collective-permute-start(bf16[64,128]{1,0:T(8,128)(2,1)S(1)} %fusion.1), channel_id=1, source_target_pairs={{0,16},{2,18},{64,80},{66,82},{128,144},{130,146},{192,208},{194,2... | collective-permute-start | bytes 49160 | tf_op jit(solution)/shard_map/ppermute | solution.py:275
  22.0 2.0 %collective-permute-start.6 = (bf16[64,128]{1,0:T(8,128)(2,1)S(1)}, bf16[64,128]{1,0:T(8,128)(2,1)S(1)}, u32[]{:S(2)}, u32[]{:S(2)}) collective-permute-start(bf16[64,128]{1,0:T(8,128)(2,1)S(1)} %fusion.1), channel_id=1, source_target_pairs={{0,32},{2,34},{64,96},{66,98},{128,160},{130,162},{192,224},{194,2... | collective-permute-start | bytes 49160 | tf_op jit(solution)/shard_map/ppermute | solution.py:275
  22.6 6.9 %collective-permute-start.7 = (bf16[64,128]{1,0:T(8,128)(2,1)S(1)}, bf16[64,128]{1,0:T(8,128)(2,1)S(1)}, u32[]{:S(2)}, u32[]{:S(2)}) collective-permute-start(bf16[64,128]{1,0:T(8,128)(2,1)S(1)} %fusion.1), channel_id=1, source_target_pairs={{0,48},{2,50},{64,112},{66,114},{128,176},{130,178},{192,240},{194... | collective-permute-start | bytes 49160 | tf_op jit(solution)/shard_map/ppermute | solution.py:275
  29.5 3.9 %collective-permute-start.10 = (bf16[64,128]{1,0:T(8,128)(2,1)S(1)}, bf16[64,128]{1,0:T(8,128)(2,1)S(1)}, u32[]{:S(2)}, u32[]{:S(2)}) collective-permute-start(bf16[64,128]{1,0:T(8,128)(2,1)S(1)} %add_add_fusion.1), channel_id=1, source_target_pairs={{0,12},{16,28},{32,44},{48,60},{2,14},{18,30},{34,46},{50,62},{64,... | collective-permute-start | bytes 49160 | tf_op jit(solution)/shard_map/ppermute | solution.py:275
  30.8 2.6 %collective-permute-start.8 = (bf16[64,128]{1,0:T(8,128)(2,1)S(1)}, bf16[64,128]{1,0:T(8,128)(2,1)S(1)}, u32[]{:S(2)}, u32[]{:S(2)}) collective-permute-start(bf16[64,128]{1,0:T(8,128)(2,1)S(1)} %add_add_fusion.1), channel_id=1, source_target_pairs={{0,4},{16,20},{32,36},{48,52},{2,6},{18,22},{34,38},{50,54},{64,68... | collective-permute-start | bytes 49160 | tf_op jit(solution)/shard_map/ppermute | solution.py:275
  32.1 2.1 %collective-permute-start.9 = (bf16[64,128]{1,0:T(8,128)(2,1)S(1)}, bf16[64,128]{1,0:T(8,128)(2,1)S(1)}, u32[]{:S(2)}, u32[]{:S(2)}) collective-permute-start(bf16[64,128]{1,0:T(8,128)(2,1)S(1)} %add_add_fusion.1), channel_id=1, source_target_pairs={{0,8},{16,24},{32,40},{48,56},{2,10},{18,26},{34,42},{50,58},{64,7... | collective-permute-start | bytes 49160 | tf_op jit(solution)/shard_map/ppermute | solution.py:275
  34.6 22.0 %copy-start = (bf16[128,512]{1,0:T(8,128)(2,1)S(1)}, bf16[128,512]{1,0:T(8,128)(2,1)}, u32[]{:S(2)}) copy-start(bf16[128,512]{1,0:T(8,128)(2,1)} %k_ref.3) | copy-start | bytes 393220
  34.7 21.9 %copy-start.1 = (bf16[128,512]{1,0:T(8,128)(2,1)S(1)}, bf16[128,512]{1,0:T(8,128)(2,1)}, u32[]{:S(2)}) copy-start(bf16[128,512]{1,0:T(8,128)(2,1)} %v_ref.3) | copy-start | bytes 393220
  34.7 21.9 %copy-start.3 = (bf16[128,4096]{1,0:T(8,128)(2,1)S(1)}, bf16[128,4096]{1,0:T(8,128)(2,1)}, u32[]{:S(2)}) copy-start(bf16[128,4096]{1,0:T(8,128)(2,1)} %q_ref.3) | copy-start | bytes 3145732
  56.6 7.2 %collective-permute-start.11 = (bf16[8,1088,128]{2,1,0:T(8,128)(2,1)S(1)}, bf16[8,1088,128]{2,1,0:T(8,128)(2,1)S(1)}, u32[]{:S(2)}, u32[]{:S(2)}) collective-permute-start(bf16[8,1088,128]{2,1,0:T(8,128)(2,1)S(1)} %all_to_all.10.far_ref), channel_id=1, source_target_pairs={{0,1},{1,0},{2,3},{3,2},{4,5},{5,4},{6,7},{7,6},{8,9},{9,8},{10,11... | collective-permute-start | bytes 6684680 | tf_op jit(solution)/shard_map/ppermute | solution.py:335

commit v6 on v5

--- a/solution.py
+++ b/solution.py
@@ -179,8 +179,8 @@
                     h,
                     far + i * PIECE,
                     PIECE,
-                    far_ref[2 * i + h, HALF * 2 * CHUNK :, :],
-                    far_ref[2 * (i + 2) + h, HALF * 2 * CHUNK :, :],
+                    far_ref[h * 4 + i, HALF * 2 * CHUNK :, :],
+                    far_ref[h * 4 + 2 + i, HALF * 2 * CHUNK :, :],
                     valid,
                 )
             put(
@@ -276,16 +276,12 @@
 
 
 def anchor_over_second(held):
-    half = HALF * TOK
-    rows = held[:half] + send(
-        held[half:], [(device(c, 0, 0, 0, 0), device(c, 0, 0, 0, 1)) for c in range(NC)]
-    )
-    steps = (
-        [(device(c, 0, 0, 0, zl), device(c, a, 0, 0, zl)) for c in range(NC) for zl in range(2)]
-        for a in range(1, 4)
-    )
-    pieces = (rows[a * PIECE : (a + 1) * PIECE] for a in range(1, 4))
-    return sum((send(piece, pairs) for piece, pairs in zip(pieces, steps)), rows[:PIECE])
+    pieces = held[: 2 * PIECE]
+    for a in range(1, 4):
+        pairs = [(device(c, 0, 0, 0, 0), device(c, a, 0, 0, 0)) for c in range(NC)]
+        pieces = pieces + send(held[2 * a * PIECE : 2 * (a + 1) * PIECE], pairs)
+    pairs = [(device(c, a, 0, 0, 0), device(c, a, 0, 0, 1)) for c in range(NC) for a in range(4)]
+    return pieces[:PIECE] + send(pieces[PIECE:], pairs)
 
 
 def anchor_over_first(piece):

time: 71.2 us -> 69.7 us (0.979)
  starting transfers between devices: 23.5 us -> 21.2 us
    all_to_all x1, starting transfers between devices: 13.6 us -> 10.9 us  [gather(): lax.all_to_all(slots, 'd', 0, 0, tiled=True, axis_index_groups=groups)]
  transfers between devices with their start and end apart: 13 -> 13, of which waited for: 3 -> 3; matrix products, arithmetic and copies ran while one was open for 0% -> 0% of each run, Pallas kernels for 11% -> 12%
where the time goes in v6:
time: 69.7 us; the launch traced here: 68.7 us
  blocking collectives  22.1 us (32%)
  starting transfers between devices  21.2 us (30%)
  Pallas kernels  16 us (23%)
  waiting for transfers between devices  7.45 us (11%)
  other arithmetic  1.04 us (1%)
  local copies, waits for them, and re-layouts  0.71 us (1%)
    all_to_all x1, blocking collectives, gather(): lax.all_to_all(slots, 'd', 0, 0, tiled=True, axis_index_groups=groups)  22.1 us
    pallas_call x2, Pallas kernels, attend(): pl.pallas_call(functools.partial(attend_kernel, other), grid_spec=pltpu.P...  14.1 us
    all_to_all x1, starting transfers between devices, gather(): lax.all_to_all(slots, 'd', 0, 0, tiled=True, axis_index_groups=groups)  10.9 us
    ppermute x10, starting transfers between devices, send(): return lax.ppermute(rows, 'd', pairs)  9.13 us
    ppermute x10, waiting for transfers between devices, send(): return lax.ppermute(rows, 'd', pairs)  6.44 us
    pallas_call x3, Pallas kernels, small_call(): pl.pallas_call(kernel, in_specs=in_specs, out_specs=tuple((in_vmem for _...  1.85 us
  transfers between devices with their start and end apart: 13, of which 3 were waited for; matrix products, arithmetic and copies ran while one was open for 0% of the time, Pallas kernels for 12%

profile of v6, /device:TPU:7, one launch (start us, length us, event | category | flops | bytes accessed | tf_op | source)
XLA Modules:
  0.0 68.7 jit_solution(6604072384960206874)
XLA Ops:
  0.0 1.0 %pad_maximum_fusion.both_ref = bf16[128,1024]{1,0:T(8,128)(2,1)S(1)} fusion(bf16[128,512]{1,0:T(8,128)(2,1)} %v_ref.3, bf16[128,512]{1,0:T(8,128)(2,1)} %k_ref.3), kind=kLoop, calls=%fused_computation | loop fusion | flops 524288 | bytes 524288 | tf_op jit(solution)/shard_map/concatenate | solution.py:314
  1.0 0.0 copy-start.2
  1.0 0.7 copy-done.2
  1.7 0.8 %shard_map.46 = (bf16[544,128]{1,0:T(8,128)(2,1)S(1)}, bf16[544,128]{1,0:T(8,128)(2,1)S(1)}) custom-call(s32[1]{0:T(128)} %bitcast.block_ref, s32[1,4,8]{2,1,0:T(4,128)S(1)} %copy-done.2, bf16[128,1024]{1,0:T(8,128)(2,1)S(1)} %pad_maximum_fusion.both_ref), custom_call_target="tpu_custom_call" | custom-call | tf_op jit(solution)/shard_map/pallas_call | solution.py:116
  2.4 0.7 %collective-permute-start = (bf16[544,128]{1,0:T(8,128)(2,1)S(1)}, bf16[544,128]{1,0:T(8,128)(2,1)S(1)}, u32[]{:S(2)}, u32[]{:S(2)}) collective-permute-start(bf16[544,128]{1,0:T(8,128)(2,1)S(1)} %get-tuple-element.8), channel_id=1, source_target_pairs={{0,1},{1,0},{2,3},{3,2},{4,5},{5,4},{6,7},{7,6},{8,9},{9,8},{10,11... | collective-permute-start | bytes 417800 | tf_op jit(solution)/shard_map/ppermute | solution.py:319
  3.2 1.0 %collective-permute-done.came_ref = bf16[544,128]{1,0:T(8,128)(2,1)S(1)} collective-permute-done((bf16[544,128]{1,0:T(8,128)(2,1)S(1)}, bf16[544,128]{1,0:T(8,128)(2,1)S(1)}, u32[]{:S(2)}, u32[]{:S(2)}) %collective-permute-start) | collective-permute-done | bytes 139296 | tf_op jit(solution)/shard_map/ppermute | solution.py:319
  4.2 0.7 collective-permute-start.1
  4.9 0.7 collective-permute-start.2
  5.5 0.7 collective-permute-start.3
  6.2 0.0 collective-permute-done.2
  6.2 0.0 collective-permute-done.3
  6.3 0.7 collective-permute-start.4
  6.9 0.7 %shard_map.47 = bf16[16,64,128]{2,1,0:T(8,128)(2,1)} custom-call(s32[1]{0:T(128)} %bitcast.block_ref, bf16[544,128]{1,0:T(8,128)(2,1)S(1)} %get-tuple-element.7.mine_ref, bf16[544,128]{1,0:T(8,128)(2,1)S(1)} %collective-permute-done.came_ref), custom_call_target="tpu_custom_call" | custom-call | tf_op jit(solution)/shard_map/pallas_call | solution.py:116
  7.7 10.9 %all-to-all-start = ((bf16[16,64,128]{2,1,0:T(8,128)(2,1)}), bf16[16,64,128]{2,1,0:T(8,128)(2,1)S(1)}, u32[]{:S(2)}, u32[]{:S(2)}) async-start(bf16[16,64,128]{2,1,0:T(8,128)(2,1)} %shard_map.47), calls=%async_computation | async-start | bytes 524288 | tf_op jit(solution)/shard_map/all_to_all | solution.py:309
  18.6 0.7 collective-permute-start.5
  19.2 0.7 collective-permute-start.6
  19.9 1.3 %collective-permute-start.7 = (bf16[64,128]{1,0:T(8,128)(2,1)S(1)}, bf16[64,128]{1,0:T(8,128)(2,1)S(1)}, u32[]{:S(2)}, u32[]{:S(2)}) collective-permute-start(bf16[64,128]{1,0:T(8,128)(2,1)S(1)} %slice_add_fusion.2), channel_id=1, source_target_pairs={{0,48},{2,50},{64,112},{66,114},{128,176},{130,178},{192,240},{194... | collective-permute-start | bytes 49160 | tf_op jit(solution)/shard_map/ppermute | solution.py:275
  21.2 0.0 collective-permute-done.5
  21.2 5.6 %collective-permute-done.7 = bf16[64,128]{1,0:T(8,128)(2,1)S(1)} collective-permute-done((bf16[64,128]{1,0:T(8,128)(2,1)S(1)}, bf16[64,128]{1,0:T(8,128)(2,1)S(1)}, u32[]{:S(2)}, u32[]{:S(2)}) %collective-permute-start.7) | collective-permute-done | bytes 16416 | tf_op jit(solution)/shard_map/ppermute | solution.py:275
  26.8 1.3 %collective-permute-start.10 = (bf16[64,128]{1,0:T(8,128)(2,1)S(1)}, bf16[64,128]{1,0:T(8,128)(2,1)S(1)}, u32[]{:S(2)}, u32[]{:S(2)}) collective-permute-start(bf16[64,128]{1,0:T(8,128)(2,1)S(1)} %add_add_fusion.1), channel_id=1, source_target_pairs={{0,12},{16,28},{32,44},{48,60},{2,14},{18,30},{34,46},{50,62},{64,... | collective-permute-start | bytes 49160 | tf_op jit(solution)/shard_map/ppermute | solution.py:275
  28.1 1.3 %collective-permute-start.8 = (bf16[64,128]{1,0:T(8,128)(2,1)S(1)}, bf16[64,128]{1,0:T(8,128)(2,1)S(1)}, u32[]{:S(2)}, u32[]{:S(2)}) collective-permute-start(bf16[64,128]{1,0:T(8,128)(2,1)S(1)} %add_add_fusion.1), channel_id=1, source_target_pairs={{0,4},{16,20},{32,36},{48,52},{2,6},{18,22},{34,38},{50,54},{64,68... | collective-permute-start | bytes 49160 | tf_op jit(solution)/shard_map/ppermute | solution.py:275
  29.4 1.3 %collective-permute-start.9 = (bf16[64,128]{1,0:T(8,128)(2,1)S(1)}, bf16[64,128]{1,0:T(8,128)(2,1)S(1)}, u32[]{:S(2)}, u32[]{:S(2)}) collective-permute-start(bf16[64,128]{1,0:T(8,128)(2,1)S(1)} %add_add_fusion.1), channel_id=1, source_target_pairs={{0,8},{16,24},{32,40},{48,56},{2,10},{18,26},{34,42},{50,58},{64,7... | collective-permute-start | bytes 49160 | tf_op jit(solution)/shard_map/ppermute | solution.py:275
  30.7 0.0 collective-permute-done.10
  30.7 0.8 %collective-permute-done.9 = bf16[64,128]{1,0:T(8,128)(2,1)S(1)} collective-permute-done((bf16[64,128]{1,0:T(8,128)(2,1)S(1)}, bf16[64,128]{1,0:T(8,128)(2,1)S(1)}, u32[]{:S(2)}, u32[]{:S(2)}) %collective-permute-start.9) | collective-permute-done | bytes 16416 | tf_op jit(solution)/shard_map/ppermute | solution.py:275
  31.6 0.4 shard_map.48
  31.9 0.0 copy-start
  31.9 0.0 copy-start.1
  32.0 0.0 copy-start.3
  32.0 22.1 %all_to_all.10.far_ref = bf16[8,1088,128]{2,1,0:T(8,128)(2,1)S(1)} all-to-all(bf16[8,1088,128]{2,1,0:T(8,128)(2,1)S(1)} %shard_map.48), channel_id=1, replica_groups={{0,2,64,66,128,130,192,194},{4,6,68,70,132,134,196,198},{8,10,72,74,136..., dimensions={0} | all-to-all | bytes 4456448 | tf_op jit(solution)/shard_map/all_to_all | solution.py:309
  54.1 0.5 collective-permute-start.11
  54.6 7.2 %shard_map.49.refs_0_ = bf16[128,4096]{1,0:T(8,128)(2,1)} custom-call(s32[1]{0:T(128)} %bitcast.block_ref, bf16[128,4096]{1,0:T(8,128)(2,1)S(1)} %copy-done.3, bf16[128,512]{1,0:T(8,128)(2,1)S(1)} %copy-done, bf16[128,512]{1,0:T(8,128)(2,1)S(1)} %copy-done.1, bf16[8,1088,128]{2,1,0:T(8,128)(2,1)S(1)} %all_to_all.10.far_ref), custom_call_target="tpu_custom_call" | custom-call | flops 2415919104 | bytes 4194304 | tf_op jit(solution)/shard_map/pallas_call | solution.py:250
  61.8 7.0 %shard_map.50 = bf16[128,4096]{1,0:T(8,128)(2,1)} custom-call(s32[1]{0:T(128)} %bitcast.block_ref, bf16[128,4096]{1,0:T(8,128)(2,1)S(1)} %copy-done.3, bf16[128,512]{1,0:T(8,128)(2,1)S(1)} %copy-done, bf16[128,512]{1,0:T(8,128)(2,1)S(1)} %copy-done.1, bf16[8,1088,128]{2,1,0:T(8,128)(2,1)S(1)} %collective-permute-done.11.far_ref, ...), custom_call_target="tpu_custom_call", output_to_operand_aliasing={{}: (5, {})} | custom-call | flops 2415919104 | bytes 4194304 | tf_op jit(solution)/shard_map/pallas_call | solution.py:250
  (16 shorter events, 0.1 us)
Async XLA Ops:
  1.0 0.7 copy-start.2
  2.4 1.7 %collective-permute-start = (bf16[544,128]{1,0:T(8,128)(2,1)S(1)}, bf16[544,128]{1,0:T(8,128)(2,1)S(1)}, u32[]{:S(2)}, u32[]{:S(2)}) collective-permute-start(bf16[544,128]{1,0:T(8,128)(2,1)S(1)} %get-tuple-element.8), channel_id=1, source_target_pairs={{0,1},{1,0},{2,3},{3,2},{4,5},{5,4},{6,7},{7,6},{8,9},{9,8},{10,11... | collective-permute-start | bytes 417800 | tf_op jit(solution)/shard_map/ppermute | solution.py:319
  4.2 2.0 %collective-permute-start.1 = (bf16[128,128]{1,0:T(8,128)(2,1)S(1)}, bf16[128,128]{1,0:T(8,128)(2,1)S(1)}, u32[]{:S(2)}, u32[]{:S(2)}) collective-permute-start(bf16[128,128]{1,0:T(8,128)(2,1)S(1)} %get-tuple-element.9), channel_id=1, source_target_pairs={{0,64},{1,17}} | collective-permute-start | bytes 98312 | tf_op jit(solution)/shard_map/ppermute | solution.py:275
  4.9 1.4 %collective-permute-start.2 = (bf16[128,128]{1,0:T(8,128)(2,1)S(1)}, bf16[128,128]{1,0:T(8,128)(2,1)S(1)}, u32[]{:S(2)}, u32[]{:S(2)}) collective-permute-start(bf16[128,128]{1,0:T(8,128)(2,1)S(1)} %get-tuple-element.11), channel_id=1, source_target_pairs={{0,128},{1,33}} | collective-permute-start | bytes 98312 | tf_op jit(solution)/shard_map/ppermute | solution.py:275
  5.5 0.7 %collective-permute-start.3 = (bf16[128,128]{1,0:T(8,128)(2,1)S(1)}, bf16[128,128]{1,0:T(8,128)(2,1)S(1)}, u32[]{:S(2)}, u32[]{:S(2)}) collective-permute-start(bf16[128,128]{1,0:T(8,128)(2,1)S(1)} %get-tuple-element.10), channel_id=1, source_target_pairs={{0,192},{1,49}} | collective-permute-start | bytes 98312 | tf_op jit(solution)/shard_map/ppermute | solution.py:275
  6.3 12.3 %collective-permute-start.4 = (bf16[64,128]{1,0:T(8,128)(2,1)S(1)}, bf16[64,128]{1,0:T(8,128)(2,1)S(1)}, u32[]{:S(2)}, u32[]{:S(2)}) collective-permute-start(bf16[64,128]{1,0:T(8,128)(2,1)S(1)} %slice.38), channel_id=1, source_target_pairs={{0,2},{64,66},{128,130},{192,194},{1,15},{17,31},{33,47},{49,63}} | collective-permute-start | bytes 49160 | tf_op jit(solution)/shard_map/ppermute | solution.py:275
  7.7 23.9 %all-to-all-start = ((bf16[16,64,128]{2,1,0:T(8,128)(2,1)}), bf16[16,64,128]{2,1,0:T(8,128)(2,1)S(1)}, u32[]{:S(2)}, u32[]{:S(2)}) async-start(bf16[16,64,128]{2,1,0:T(8,128)(2,1)} %shard_map.47), calls=%async_computation | async-start | bytes 524288 | tf_op jit(solution)/shard_map/all_to_all | solution.py:309
  18.6 2.6 %collective-permute-start.5 = (bf16[64,128]{1,0:T(8,128)(2,1)S(1)}, bf16[64,128]{1,0:T(8,128)(2,1)S(1)}, u32[]{:S(2)}, u32[]{:S(2)}) collective-permute-start(bf16[64,128]{1,0:T(8,128)(2,1)S(1)} %slice_add_fusion.2), channel_id=1, source_target_pairs={{0,16},{2,18},{64,80},{66,82},{128,144},{130,146},{192,208},{194,2... | collective-permute-start | bytes 49160 | tf_op jit(solution)/shard_map/ppermute | solution.py:275
  19.2 2.0 %collective-permute-start.6 = (bf16[64,128]{1,0:T(8,128)(2,1)S(1)}, bf16[64,128]{1,0:T(8,128)(2,1)S(1)}, u32[]{:S(2)}, u32[]{:S(2)}) collective-permute-start(bf16[64,128]{1,0:T(8,128)(2,1)S(1)} %slice_add_fusion.2), channel_id=1, source_target_pairs={{0,32},{2,34},{64,96},{66,98},{128,160},{130,162},{192,224},{194,2... | collective-permute-start | bytes 49160 | tf_op jit(solution)/shard_map/ppermute | solution.py:275
  19.9 6.9 %collective-permute-start.7 = (bf16[64,128]{1,0:T(8,128)(2,1)S(1)}, bf16[64,128]{1,0:T(8,128)(2,1)S(1)}, u32[]{:S(2)}, u32[]{:S(2)}) collective-permute-start(bf16[64,128]{1,0:T(8,128)(2,1)S(1)} %slice_add_fusion.2), channel_id=1, source_target_pairs={{0,48},{2,50},{64,112},{66,114},{128,176},{130,178},{192,240},{194... | collective-permute-start | bytes 49160 | tf_op jit(solution)/shard_map/ppermute | solution.py:275
  26.8 3.9 %collective-permute-start.10 = (bf16[64,128]{1,0:T(8,128)(2,1)S(1)}, bf16[64,128]{1,0:T(8,128)(2,1)S(1)}, u32[]{:S(2)}, u32[]{:S(2)}) collective-permute-start(bf16[64,128]{1,0:T(8,128)(2,1)S(1)} %add_add_fusion.1), channel_id=1, source_target_pairs={{0,12},{16,28},{32,44},{48,60},{2,14},{18,30},{34,46},{50,62},{64,... | collective-permute-start | bytes 49160 | tf_op jit(solution)/shard_map/ppermute | solution.py:275
  28.1 2.6 %collective-permute-start.8 = (bf16[64,128]{1,0:T(8,128)(2,1)S(1)}, bf16[64,128]{1,0:T(8,128)(2,1)S(1)}, u32[]{:S(2)}, u32[]{:S(2)}) collective-permute-start(bf16[64,128]{1,0:T(8,128)(2,1)S(1)} %add_add_fusion.1), channel_id=1, source_target_pairs={{0,4},{16,20},{32,36},{48,52},{2,6},{18,22},{34,38},{50,54},{64,68... | collective-permute-start | bytes 49160 | tf_op jit(solution)/shard_map/ppermute | solution.py:275
  29.4 2.1 %collective-permute-start.9 = (bf16[64,128]{1,0:T(8,128)(2,1)S(1)}, bf16[64,128]{1,0:T(8,128)(2,1)S(1)}, u32[]{:S(2)}, u32[]{:S(2)}) collective-permute-start(bf16[64,128]{1,0:T(8,128)(2,1)S(1)} %add_add_fusion.1), channel_id=1, source_target_pairs={{0,8},{16,24},{32,40},{48,56},{2,10},{18,26},{34,42},{50,58},{64,7... | collective-permute-start | bytes 49160 | tf_op jit(solution)/shard_map/ppermute | solution.py:275
  31.9 22.7 %copy-start = (bf16[128,512]{1,0:T(8,128)(2,1)S(1)}, bf16[128,512]{1,0:T(8,128)(2,1)}, u32[]{:S(2)}) copy-start(bf16[128,512]{1,0:T(8,128)(2,1)} %k_ref.3) | copy-start | bytes 393220
  31.9 22.6 %copy-start.1 = (bf16[128,512]{1,0:T(8,128)(2,1)S(1)}, bf16[128,512]{1,0:T(8,128)(2,1)}, u32[]{:S(2)}) copy-start(bf16[128,512]{1,0:T(8,128)(2,1)} %v_ref.3) | copy-start | bytes 393220
  32.0 22.6 %copy-start.3 = (bf16[128,4096]{1,0:T(8,128)(2,1)S(1)}, bf16[128,4096]{1,0:T(8,128)(2,1)}, u32[]{:S(2)}) copy-start(bf16[128,4096]{1,0:T(8,128)(2,1)} %q_ref.3) | copy-start | bytes 3145732
  54.1 7.7 %collective-permute-start.11 = (bf16[8,1088,128]{2,1,0:T(8,128)(2,1)S(1)}, bf16[8,1088,128]{2,1,0:T(8,128)(2,1)S(1)}, u32[]{:S(2)}, u32[]{:S(2)}) collective-permute-start(bf16[8,1088,128]{2,1,0:T(8,128)(2,1)S(1)} %all_to_all.10.far_ref), channel_id=1, source_target_pairs={{0,1},{1,0},{2,3},{3,2},{4,5},{5,4},{6,7},{7,6},{8,9},{9,8},{10,11... | collective-permute-start | bytes 6684680 | tf_op jit(solution)/shard_map/ppermute | solution.py:331

commit v7 on v6

--- a/solution.py
+++ b/solution.py
@@ -228,7 +228,7 @@
             finish(unit, buffers[unit % 3])
 
     own_plane = block // (NY * NZ * NC)
-    for low, high in ((0, 1), (1, 2), (2, 4)):
+    for low, high in ((0, 1), (1, 2), (2, 3), (3, 4)):
         here = (own_plane >= low) & (own_plane < high)
         pl.when(here)(functools.partial(run, low, high))
 
@@ -277,7 +277,7 @@
 
 def anchor_over_second(held):
     pieces = held[: 2 * PIECE]
-    for a in range(1, 4):
+    for a in (1, 3, 2):
         pairs = [(device(c, 0, 0, 0, 0), device(c, a, 0, 0, 0)) for c in range(NC)]
         pieces = pieces + send(held[2 * a * PIECE : 2 * (a + 1) * PIECE], pairs)
     pairs = [(device(c, a, 0, 0, 0), device(c, a, 0, 0, 1)) for c in range(NC) for a in range(4)]
@@ -288,7 +288,7 @@
     lines = [(c, a, zl) for c in range(NC) for a in range(4) for zl in range(2)]
     steps = (
         [(device(c, a, 0, 0, zl), device(c, a, u, 0, zl)) for c, a, zl in lines]
-        for u in range(1, 4)
+        for u in (1, 3, 2)
     )
     piece = sum((send(piece, pairs) for pairs in steps), piece)
     steps = (

time: 69.7 us -> 69.3 us (level)
  waiting for transfers between devices: 7.45 us -> 5.58 us
  starting transfers between devices: 21.2 us -> 22.6 us
    ppermute x10, waiting for transfers between devices: 6.44 us -> 4.57 us  [send(): return lax.ppermute(rows, 'd', pairs)]
    ppermute x1, starting transfers between devices: 0.48 us -> 1.74 us  [on_device(): far_other = swap(far)]
  transfers between devices with their start and end apart: 13 -> 13, of which waited for: 3 -> 3; matrix products, arithmetic and copies ran while one was open for 0% -> 0% of each run, Pallas kernels for 12% -> 11%
where the time goes in v7:
time: 69.3 us; the launch traced here: 68.2 us
  starting transfers between devices  22.6 us (33%)
  blocking collectives  22.3 us (32%)
  Pallas kernels  15.8 us (23%)
  waiting for transfers between devices  5.58 us (8%)
  other arithmetic  1.04 us (2%)
  local copies, waits for them, and re-layouts  0.71 us (1%)
    all_to_all x1, blocking collectives, gather(): lax.all_to_all(slots, 'd', 0, 0, tiled=True, axis_index_groups=groups)  22.3 us
    pallas_call x2, Pallas kernels, attend(): pl.pallas_call(functools.partial(attend_kernel, other), grid_spec=pltpu.P...  13.9 us
    all_to_all x1, starting transfers between devices, gather(): lax.all_to_all(slots, 'd', 0, 0, tiled=True, axis_index_groups=groups)  10.9 us
    ppermute x10, starting transfers between devices, send(): return lax.ppermute(rows, 'd', pairs)  9.26 us
    ppermute x10, waiting for transfers between devices, send(): return lax.ppermute(rows, 'd', pairs)  4.57 us
    pallas_call x3, Pallas kernels, small_call(): pl.pallas_call(kernel, in_specs=in_specs, out_specs=tuple((in_vmem for _...  1.85 us
    ppermute x1, starting transfers between devices, on_device(): far_other = swap(far)  1.74 us
  transfers between devices with their start and end apart: 13, of which 3 were waited for; matrix products, arithmetic and copies ran while one was open for 0% of the time, Pallas kernels for 11%

profile of v7, /device:TPU:7, one launch (start us, length us, event | category | flops | bytes accessed | tf_op | source)
XLA Modules:
  0.0 68.2 jit_solution(12254656323652087498)
XLA Ops:
  0.0 1.0 %pad_maximum_fusion.both_ref = bf16[128,1024]{1,0:T(8,128)(2,1)S(1)} fusion(bf16[128,512]{1,0:T(8,128)(2,1)} %v_ref.3, bf16[128,512]{1,0:T(8,128)(2,1)} %k_ref.3), kind=kLoop, calls=%fused_computation | loop fusion | flops 524288 | bytes 524288 | tf_op jit(solution)/shard_map/concatenate | solution.py:314
  1.0 0.0 copy-start.2
  1.0 0.7 copy-done.2
  1.7 0.8 %shard_map.46 = (bf16[544,128]{1,0:T(8,128)(2,1)S(1)}, bf16[544,128]{1,0:T(8,128)(2,1)S(1)}) custom-call(s32[1]{0:T(128)} %bitcast.block_ref, s32[1,4,8]{2,1,0:T(4,128)S(1)} %copy-done.2, bf16[128,1024]{1,0:T(8,128)(2,1)S(1)} %pad_maximum_fusion.both_ref), custom_call_target="tpu_custom_call" | custom-call | tf_op jit(solution)/shard_map/pallas_call | solution.py:116
  2.4 0.7 %collective-permute-start = (bf16[544,128]{1,0:T(8,128)(2,1)S(1)}, bf16[544,128]{1,0:T(8,128)(2,1)S(1)}, u32[]{:S(2)}, u32[]{:S(2)}) collective-permute-start(bf16[544,128]{1,0:T(8,128)(2,1)S(1)} %get-tuple-element.8), channel_id=1, source_target_pairs={{0,1},{1,0},{2,3},{3,2},{4,5},{5,4},{6,7},{7,6},{8,9},{9,8},{10,11... | collective-permute-start | bytes 417800 | tf_op jit(solution)/shard_map/ppermute | solution.py:319
  3.2 1.0 %collective-permute-done.came_ref = bf16[544,128]{1,0:T(8,128)(2,1)S(1)} collective-permute-done((bf16[544,128]{1,0:T(8,128)(2,1)S(1)}, bf16[544,128]{1,0:T(8,128)(2,1)S(1)}, u32[]{:S(2)}, u32[]{:S(2)}) %collective-permute-start) | collective-permute-done | bytes 139296 | tf_op jit(solution)/shard_map/ppermute | solution.py:319
  4.2 0.7 collective-permute-start.1
  4.9 0.7 collective-permute-start.2
  5.5 0.7 collective-permute-start.3
  6.2 0.0 collective-permute-done.1
  6.2 0.0 collective-permute-done.2
  6.3 0.7 collective-permute-start.4
  6.9 0.7 %shard_map.47 = bf16[16,64,128]{2,1,0:T(8,128)(2,1)} custom-call(s32[1]{0:T(128)} %bitcast.block_ref, bf16[544,128]{1,0:T(8,128)(2,1)S(1)} %get-tuple-element.7.mine_ref, bf16[544,128]{1,0:T(8,128)(2,1)S(1)} %collective-permute-done.came_ref), custom_call_target="tpu_custom_call" | custom-call | tf_op jit(solution)/shard_map/pallas_call | solution.py:116
  7.7 10.9 %all-to-all-start = ((bf16[16,64,128]{2,1,0:T(8,128)(2,1)}), bf16[16,64,128]{2,1,0:T(8,128)(2,1)S(1)}, u32[]{:S(2)}, u32[]{:S(2)}) async-start(bf16[16,64,128]{2,1,0:T(8,128)(2,1)} %shard_map.47), calls=%async_computation | async-start | bytes 524288 | tf_op jit(solution)/shard_map/all_to_all | solution.py:309
  18.5 0.0 collective-permute-done.4
  18.6 0.7 collective-permute-start.5
  19.2 1.3 %collective-permute-start.6 = (bf16[64,128]{1,0:T(8,128)(2,1)S(1)}, bf16[64,128]{1,0:T(8,128)(2,1)S(1)}, u32[]{:S(2)}, u32[]{:S(2)}) collective-permute-start(bf16[64,128]{1,0:T(8,128)(2,1)S(1)} %slice_add_fusion.2), channel_id=1, source_target_pairs={{0,48},{2,50},{64,112},{66,114},{128,176},{130,178},{192,240},{194... | collective-permute-start | bytes 49160 | tf_op jit(solution)/shard_map/ppermute | solution.py:275
  20.5 0.7 collective-permute-start.7
  21.2 3.7 %collective-permute-done.6 = bf16[64,128]{1,0:T(8,128)(2,1)S(1)} collective-permute-done((bf16[64,128]{1,0:T(8,128)(2,1)S(1)}, bf16[64,128]{1,0:T(8,128)(2,1)S(1)}, u32[]{:S(2)}, u32[]{:S(2)}) %collective-permute-start.6) | collective-permute-done | bytes 16416 | tf_op jit(solution)/shard_map/ppermute | solution.py:275
  24.9 1.3 %collective-permute-start.10 = (bf16[64,128]{1,0:T(8,128)(2,1)S(1)}, bf16[64,128]{1,0:T(8,128)(2,1)S(1)}, u32[]{:S(2)}, u32[]{:S(2)}) collective-permute-start(bf16[64,128]{1,0:T(8,128)(2,1)S(1)} %add_add_fusion.1), channel_id=1, source_target_pairs={{0,12},{16,28},{32,44},{48,60},{2,14},{18,30},{34,46},{50,62},{64,... | collective-permute-start | bytes 49160 | tf_op jit(solution)/shard_map/ppermute | solution.py:275
  26.2 1.3 %collective-permute-start.8 = (bf16[64,128]{1,0:T(8,128)(2,1)S(1)}, bf16[64,128]{1,0:T(8,128)(2,1)S(1)}, u32[]{:S(2)}, u32[]{:S(2)}) collective-permute-start(bf16[64,128]{1,0:T(8,128)(2,1)S(1)} %add_add_fusion.1), channel_id=1, source_target_pairs={{0,4},{16,20},{32,36},{48,52},{2,6},{18,22},{34,38},{50,54},{64,68... | collective-permute-start | bytes 49160 | tf_op jit(solution)/shard_map/ppermute | solution.py:275
  27.5 1.4 %collective-permute-start.9 = (bf16[64,128]{1,0:T(8,128)(2,1)S(1)}, bf16[64,128]{1,0:T(8,128)(2,1)S(1)}, u32[]{:S(2)}, u32[]{:S(2)}) collective-permute-start(bf16[64,128]{1,0:T(8,128)(2,1)S(1)} %add_add_fusion.1), channel_id=1, source_target_pairs={{0,8},{16,24},{32,40},{48,56},{2,10},{18,26},{34,42},{50,58},{64,7... | collective-permute-start | bytes 49160 | tf_op jit(solution)/shard_map/ppermute | solution.py:275
  29.0 0.0 collective-permute-done.8
  29.0 0.8 %collective-permute-done.9 = bf16[64,128]{1,0:T(8,128)(2,1)S(1)} collective-permute-done((bf16[64,128]{1,0:T(8,128)(2,1)S(1)}, bf16[64,128]{1,0:T(8,128)(2,1)S(1)}, u32[]{:S(2)}, u32[]{:S(2)}) %collective-permute-start.9) | collective-permute-done | bytes 16416 | tf_op jit(solution)/shard_map/ppermute | solution.py:275
  29.8 0.4 shard_map.48
  30.2 0.0 copy-start
  30.2 0.0 copy-start.1
  30.2 0.0 copy-start.3
  30.2 22.3 %all_to_all.10.far_ref = bf16[8,1088,128]{2,1,0:T(8,128)(2,1)S(1)} all-to-all(bf16[8,1088,128]{2,1,0:T(8,128)(2,1)S(1)} %shard_map.48), channel_id=1, replica_groups={{0,2,64,66,128,130,192,194},{4,6,68,70,132,134,196,198},{8,10,72,74,136..., dimensions={0} | all-to-all | bytes 4456448 | tf_op jit(solution)/shard_map/all_to_all | solution.py:309
  52.6 1.7 %collective-permute-start.11 = (bf16[8,1088,128]{2,1,0:T(8,128)(2,1)S(1)}, bf16[8,1088,128]{2,1,0:T(8,128)(2,1)S(1)}, u32[]{:S(2)}, u32[]{:S(2)}) collective-permute-start(bf16[8,1088,128]{2,1,0:T(8,128)(2,1)S(1)} %all_to_all.10.far_ref), channel_id=1, source_target_pairs={{0,1},{1,0},{2,3},{3,2},{4,5},{5,4},{6,7},{7,6},{8,9},{9,8},{10,11... | collective-permute-start | bytes 6684680 | tf_op jit(solution)/shard_map/ppermute | solution.py:331
  54.3 7.1 %shard_map.49.refs_0_ = bf16[128,4096]{1,0:T(8,128)(2,1)} custom-call(s32[1]{0:T(128)} %bitcast.block_ref, bf16[128,4096]{1,0:T(8,128)(2,1)S(1)} %copy-done.3, bf16[128,512]{1,0:T(8,128)(2,1)S(1)} %copy-done, bf16[128,512]{1,0:T(8,128)(2,1)S(1)} %copy-done.1, bf16[8,1088,128]{2,1,0:T(8,128)(2,1)S(1)} %all_to_all.10.far_ref), custom_call_target="tpu_custom_call" | custom-call | flops 2415919104 | bytes 4194304 | tf_op jit(solution)/shard_map/pallas_call | solution.py:250
  61.4 6.8 %shard_map.50 = bf16[128,4096]{1,0:T(8,128)(2,1)} custom-call(s32[1]{0:T(128)} %bitcast.block_ref, bf16[128,4096]{1,0:T(8,128)(2,1)S(1)} %copy-done.3, bf16[128,512]{1,0:T(8,128)(2,1)S(1)} %copy-done, bf16[128,512]{1,0:T(8,128)(2,1)S(1)} %copy-done.1, bf16[8,1088,128]{2,1,0:T(8,128)(2,1)S(1)} %collective-permute-done.11.far_ref, ...), custom_call_target="tpu_custom_call", output_to_operand_aliasing={{}: (5, {})} | custom-call | flops 2415919104 | bytes 4194304 | tf_op jit(solution)/shard_map/pallas_call | solution.py:250
  (16 shorter events, 0.1 us)
Async XLA Ops:
  1.0 0.7 %copy-start.2 = (s32[1,4,8]{2,1,0:T(4,128)S(1)}, s32[1,4,8]{2,1,0:T(4,128)}, u32[]{:S(2)}) copy-start(s32[1,4,8]{2,1,0:T(4,128)} %index_ref.1) | copy-start | bytes 388
  2.4 1.7 %collective-permute-start = (bf16[544,128]{1,0:T(8,128)(2,1)S(1)}, bf16[544,128]{1,0:T(8,128)(2,1)S(1)}, u32[]{:S(2)}, u32[]{:S(2)}) collective-permute-start(bf16[544,128]{1,0:T(8,128)(2,1)S(1)} %get-tuple-element.8), channel_id=1, source_target_pairs={{0,1},{1,0},{2,3},{3,2},{4,5},{5,4},{6,7},{7,6},{8,9},{9,8},{10,11... | collective-permute-start | bytes 417800 | tf_op jit(solution)/shard_map/ppermute | solution.py:319
  4.2 2.0 %collective-permute-start.1 = (bf16[128,128]{1,0:T(8,128)(2,1)S(1)}, bf16[128,128]{1,0:T(8,128)(2,1)S(1)}, u32[]{:S(2)}, u32[]{:S(2)}) collective-permute-start(bf16[128,128]{1,0:T(8,128)(2,1)S(1)} %get-tuple-element.9), channel_id=1, source_target_pairs={{0,64},{1,17}} | collective-permute-start | bytes 98312 | tf_op jit(solution)/shard_map/ppermute | solution.py:275
  4.9 1.4 %collective-permute-start.2 = (bf16[128,128]{1,0:T(8,128)(2,1)S(1)}, bf16[128,128]{1,0:T(8,128)(2,1)S(1)}, u32[]{:S(2)}, u32[]{:S(2)}) collective-permute-start(bf16[128,128]{1,0:T(8,128)(2,1)S(1)} %get-tuple-element.11), channel_id=1, source_target_pairs={{0,192},{1,49}} | collective-permute-start | bytes 98312 | tf_op jit(solution)/shard_map/ppermute | solution.py:275
  5.5 0.7 %collective-permute-start.3 = (bf16[128,128]{1,0:T(8,128)(2,1)S(1)}, bf16[128,128]{1,0:T(8,128)(2,1)S(1)}, u32[]{:S(2)}, u32[]{:S(2)}) collective-permute-start(bf16[128,128]{1,0:T(8,128)(2,1)S(1)} %get-tuple-element.10), channel_id=1, source_target_pairs={{0,128},{1,33}} | collective-permute-start | bytes 98312 | tf_op jit(solution)/shard_map/ppermute | solution.py:275
  6.3 12.3 %collective-permute-start.4 = (bf16[64,128]{1,0:T(8,128)(2,1)S(1)}, bf16[64,128]{1,0:T(8,128)(2,1)S(1)}, u32[]{:S(2)}, u32[]{:S(2)}) collective-permute-start(bf16[64,128]{1,0:T(8,128)(2,1)S(1)} %slice.38), channel_id=1, source_target_pairs={{0,2},{64,66},{128,130},{192,194},{1,15},{17,31},{33,47},{49,63}} | collective-permute-start | bytes 49160 | tf_op jit(solution)/shard_map/ppermute | solution.py:275
  7.7 22.1 %all-to-all-start = ((bf16[16,64,128]{2,1,0:T(8,128)(2,1)}), bf16[16,64,128]{2,1,0:T(8,128)(2,1)S(1)}, u32[]{:S(2)}, u32[]{:S(2)}) async-start(bf16[16,64,128]{2,1,0:T(8,128)(2,1)} %shard_map.47), calls=%async_computation | async-start | bytes 524288 | tf_op jit(solution)/shard_map/all_to_all | solution.py:309
  18.6 2.6 %collective-permute-start.5 = (bf16[64,128]{1,0:T(8,128)(2,1)S(1)}, bf16[64,128]{1,0:T(8,128)(2,1)S(1)}, u32[]{:S(2)}, u32[]{:S(2)}) collective-permute-start(bf16[64,128]{1,0:T(8,128)(2,1)S(1)} %slice_add_fusion.2), channel_id=1, source_target_pairs={{0,16},{2,18},{64,80},{66,82},{128,144},{130,146},{192,208},{194,2... | collective-permute-start | bytes 49160 | tf_op jit(solution)/shard_map/ppermute | solution.py:275
  19.2 5.7 %collective-permute-start.6 = (bf16[64,128]{1,0:T(8,128)(2,1)S(1)}, bf16[64,128]{1,0:T(8,128)(2,1)S(1)}, u32[]{:S(2)}, u32[]{:S(2)}) collective-permute-start(bf16[64,128]{1,0:T(8,128)(2,1)S(1)} %slice_add_fusion.2), channel_id=1, source_target_pairs={{0,48},{2,50},{64,112},{66,114},{128,176},{130,178},{192,240},{194... | collective-permute-start | bytes 49160 | tf_op jit(solution)/shard_map/ppermute | solution.py:275
  20.5 4.4 %collective-permute-start.7 = (bf16[64,128]{1,0:T(8,128)(2,1)S(1)}, bf16[64,128]{1,0:T(8,128)(2,1)S(1)}, u32[]{:S(2)}, u32[]{:S(2)}) collective-permute-start(bf16[64,128]{1,0:T(8,128)(2,1)S(1)} %slice_add_fusion.2), channel_id=1, source_target_pairs={{0,32},{2,34},{64,96},{66,98},{128,160},{130,162},{192,224},{194,2... | collective-permute-start | bytes 49160 | tf_op jit(solution)/shard_map/ppermute | solution.py:275
  24.9 4.0 %collective-permute-start.10 = (bf16[64,128]{1,0:T(8,128)(2,1)S(1)}, bf16[64,128]{1,0:T(8,128)(2,1)S(1)}, u32[]{:S(2)}, u32[]{:S(2)}) collective-permute-start(bf16[64,128]{1,0:T(8,128)(2,1)S(1)} %add_add_fusion.1), channel_id=1, source_target_pairs={{0,12},{16,28},{32,44},{48,60},{2,14},{18,30},{34,46},{50,62},{64,... | collective-permute-start | bytes 49160 | tf_op jit(solution)/shard_map/ppermute | solution.py:275
  26.2 2.7 %collective-permute-start.8 = (bf16[64,128]{1,0:T(8,128)(2,1)S(1)}, bf16[64,128]{1,0:T(8,128)(2,1)S(1)}, u32[]{:S(2)}, u32[]{:S(2)}) collective-permute-start(bf16[64,128]{1,0:T(8,128)(2,1)S(1)} %add_add_fusion.1), channel_id=1, source_target_pairs={{0,4},{16,20},{32,36},{48,52},{2,6},{18,22},{34,38},{50,54},{64,68... | collective-permute-start | bytes 49160 | tf_op jit(solution)/shard_map/ppermute | solution.py:275
  27.5 2.3 %collective-permute-start.9 = (bf16[64,128]{1,0:T(8,128)(2,1)S(1)}, bf16[64,128]{1,0:T(8,128)(2,1)S(1)}, u32[]{:S(2)}, u32[]{:S(2)}) collective-permute-start(bf16[64,128]{1,0:T(8,128)(2,1)S(1)} %add_add_fusion.1), channel_id=1, source_target_pairs={{0,8},{16,24},{32,40},{48,56},{2,10},{18,26},{34,42},{50,58},{64,7... | collective-permute-start | bytes 49160 | tf_op jit(solution)/shard_map/ppermute | solution.py:275
  30.2 24.1 %copy-start = (bf16[128,512]{1,0:T(8,128)(2,1)S(1)}, bf16[128,512]{1,0:T(8,128)(2,1)}, u32[]{:S(2)}) copy-start(bf16[128,512]{1,0:T(8,128)(2,1)} %k_ref.3) | copy-start | bytes 393220
  30.2 24.1 %copy-start.1 = (bf16[128,512]{1,0:T(8,128)(2,1)S(1)}, bf16[128,512]{1,0:T(8,128)(2,1)}, u32[]{:S(2)}) copy-start(bf16[128,512]{1,0:T(8,128)(2,1)} %v_ref.3) | copy-start | bytes 393220
  30.2 24.1 %copy-start.3 = (bf16[128,4096]{1,0:T(8,128)(2,1)S(1)}, bf16[128,4096]{1,0:T(8,128)(2,1)}, u32[]{:S(2)}) copy-start(bf16[128,4096]{1,0:T(8,128)(2,1)} %q_ref.3) | copy-start | bytes 3145732
  52.6 8.8 %collective-permute-start.11 = (bf16[8,1088,128]{2,1,0:T(8,128)(2,1)S(1)}, bf16[8,1088,128]{2,1,0:T(8,128)(2,1)S(1)}, u32[]{:S(2)}, u32[]{:S(2)}) collective-permute-start(bf16[8,1088,128]{2,1,0:T(8,128)(2,1)S(1)} %all_to_all.10.far_ref), channel_id=1, source_target_pairs={{0,1},{1,0},{2,3},{3,2},{4,5},{5,4},{6,7},{7,6},{8,9},{9,8},{10,11... | collective-permute-start | bytes 6684680 | tf_op jit(solution)/shard_map/ppermute | solution.py:331

commit v8 on v7

--- a/solution.py
+++ b/solution.py
@@ -293,7 +293,7 @@
     piece = sum((send(piece, pairs) for pairs in steps), piece)
     steps = (
         [(device(c, a, u, 0, zl), device(c, a, u, zh, zl)) for c, a, zl in lines for u in range(4)]
-        for zh in range(1, 4)
+        for zh in (1, 3, 2)
     )
     return sum((send(piece, pairs) for pairs in steps), piece)
 

time: 69.3 us -> 69.3 us (level)
    ppermute x10, starting transfers between devices: 9.26 us -> 10.5 us  [send(): return lax.ppermute(rows, 'd', pairs)]
    ppermute x1, starting transfers between devices: 1.74 us -> 0.76 us  [on_device(): far_other = swap(far)]
where the time goes in v8:
time: 69.3 us; the launch traced here: 68.3 us
  starting transfers between devices  22.9 us (33%)
  blocking collectives  22.1 us (32%)
  Pallas kernels  15.8 us (23%)
  waiting for transfers between devices  5.58 us (8%)
  other arithmetic  1.04 us (2%)
  local copies, waits for them, and re-layouts  0.71 us (1%)
    all_to_all x1, blocking collectives, gather(): lax.all_to_all(slots, 'd', 0, 0, tiled=True, axis_index_groups=groups)  22.1 us
    pallas_call x2, Pallas kernels, attend(): pl.pallas_call(functools.partial(attend_kernel, other), grid_spec=pltpu.P...  13.9 us
    all_to_all x1, starting transfers between devices, gather(): lax.all_to_all(slots, 'd', 0, 0, tiled=True, axis_index_groups=groups)  10.9 us
    ppermute x10, starting transfers between devices, send(): return lax.ppermute(rows, 'd', pairs)  10.5 us
    ppermute x10, waiting for transfers between devices, send(): return lax.ppermute(rows, 'd', pairs)  4.57 us
    pallas_call x3, Pallas kernels, small_call(): pl.pallas_call(kernel, in_specs=in_specs, out_specs=tuple((in_vmem for _...  1.85 us
  transfers between devices with their start and end apart: 13, of which 3 were waited for; matrix products, arithmetic and copies ran while one was open for 0% of the time, Pallas kernels for 11%

profile of v8, /device:TPU:7, one launch (start us, length us, event | category | flops | bytes accessed | tf_op | source)
XLA Modules:
  0.0 68.3 jit_solution(4313602622723010272)
XLA Ops:
  0.0 1.0 %pad_maximum_fusion.both_ref = bf16[128,1024]{1,0:T(8,128)(2,1)S(1)} fusion(bf16[128,512]{1,0:T(8,128)(2,1)} %v_ref.3, bf16[128,512]{1,0:T(8,128)(2,1)} %k_ref.3), kind=kLoop, calls=%fused_computation | loop fusion | flops 524288 | bytes 524288 | tf_op jit(solution)/shard_map/concatenate | solution.py:314
  1.0 0.0 copy-start.2
  1.0 0.7 copy-done.2
  1.7 0.8 %shard_map.46 = (bf16[544,128]{1,0:T(8,128)(2,1)S(1)}, bf16[544,128]{1,0:T(8,128)(2,1)S(1)}) custom-call(s32[1]{0:T(128)} %bitcast.block_ref, s32[1,4,8]{2,1,0:T(4,128)S(1)} %copy-done.2, bf16[128,1024]{1,0:T(8,128)(2,1)S(1)} %pad_maximum_fusion.both_ref), custom_call_target="tpu_custom_call" | custom-call | tf_op jit(solution)/shard_map/pallas_call | solution.py:116
  2.4 0.7 %collective-permute-start = (bf16[544,128]{1,0:T(8,128)(2,1)S(1)}, bf16[544,128]{1,0:T(8,128)(2,1)S(1)}, u32[]{:S(2)}, u32[]{:S(2)}) collective-permute-start(bf16[544,128]{1,0:T(8,128)(2,1)S(1)} %get-tuple-element.8), channel_id=1, source_target_pairs={{0,1},{1,0},{2,3},{3,2},{4,5},{5,4},{6,7},{7,6},{8,9},{9,8},{10,11... | collective-permute-start | bytes 417800 | tf_op jit(solution)/shard_map/ppermute | solution.py:319
  3.2 1.0 %collective-permute-done.came_ref = bf16[544,128]{1,0:T(8,128)(2,1)S(1)} collective-permute-done((bf16[544,128]{1,0:T(8,128)(2,1)S(1)}, bf16[544,128]{1,0:T(8,128)(2,1)S(1)}, u32[]{:S(2)}, u32[]{:S(2)}) %collective-permute-start) | collective-permute-done | bytes 139296 | tf_op jit(solution)/shard_map/ppermute | solution.py:319
  4.2 0.7 collective-permute-start.1
  4.9 0.7 collective-permute-start.2
  5.5 0.7 collective-permute-start.3
  6.2 0.0 collective-permute-done.1
  6.2 0.0 collective-permute-done.3
  6.3 0.7 collective-permute-start.4
  6.9 0.7 %shard_map.47 = bf16[16,64,128]{2,1,0:T(8,128)(2,1)} custom-call(s32[1]{0:T(128)} %bitcast.block_ref, bf16[544,128]{1,0:T(8,128)(2,1)S(1)} %get-tuple-element.7.mine_ref, bf16[544,128]{1,0:T(8,128)(2,1)S(1)} %collective-permute-done.came_ref), custom_call_target="tpu_custom_call" | custom-call | tf_op jit(solution)/shard_map/pallas_call | solution.py:116
  7.7 10.9 %all-to-all-start = ((bf16[16,64,128]{2,1,0:T(8,128)(2,1)}), bf16[16,64,128]{2,1,0:T(8,128)(2,1)S(1)}, u32[]{:S(2)}, u32[]{:S(2)}) async-start(bf16[16,64,128]{2,1,0:T(8,128)(2,1)} %shard_map.47), calls=%async_computation | async-start | bytes 524288 | tf_op jit(solution)/shard_map/all_to_all | solution.py:309
  18.5 0.0 collective-permute-done.4
  18.6 0.7 collective-permute-start.5
  19.2 1.3 %collective-permute-start.6 = (bf16[64,128]{1,0:T(8,128)(2,1)S(1)}, bf16[64,128]{1,0:T(8,128)(2,1)S(1)}, u32[]{:S(2)}, u32[]{:S(2)}) collective-permute-start(bf16[64,128]{1,0:T(8,128)(2,1)S(1)} %slice_add_fusion.2), channel_id=1, source_target_pairs={{0,48},{2,50},{64,112},{66,114},{128,176},{130,178},{192,240},{194... | collective-permute-start | bytes 49160 | tf_op jit(solution)/shard_map/ppermute | solution.py:275
  20.5 0.7 collective-permute-start.7
  21.2 0.0 collective-permute-done.5
  21.2 3.7 %collective-permute-done.6 = bf16[64,128]{1,0:T(8,128)(2,1)S(1)} collective-permute-done((bf16[64,128]{1,0:T(8,128)(2,1)S(1)}, bf16[64,128]{1,0:T(8,128)(2,1)S(1)}, u32[]{:S(2)}, u32[]{:S(2)}) %collective-permute-start.6) | collective-permute-done | bytes 16416 | tf_op jit(solution)/shard_map/ppermute | solution.py:275
  24.9 2.7 %collective-permute-start.10 = (bf16[64,128]{1,0:T(8,128)(2,1)S(1)}, bf16[64,128]{1,0:T(8,128)(2,1)S(1)}, u32[]{:S(2)}, u32[]{:S(2)}) collective-permute-start(bf16[64,128]{1,0:T(8,128)(2,1)S(1)} %add_add_fusion.1), channel_id=1, source_target_pairs={{0,8},{16,24},{32,40},{48,56},{2,10},{18,26},{34,42},{50,58},{64,7... | collective-permute-start | bytes 49160 | tf_op jit(solution)/shard_map/ppermute | solution.py:275
  27.6 1.3 %collective-permute-start.8 = (bf16[64,128]{1,0:T(8,128)(2,1)S(1)}, bf16[64,128]{1,0:T(8,128)(2,1)S(1)}, u32[]{:S(2)}, u32[]{:S(2)}) collective-permute-start(bf16[64,128]{1,0:T(8,128)(2,1)S(1)} %add_add_fusion.1), channel_id=1, source_target_pairs={{0,4},{16,20},{32,36},{48,52},{2,6},{18,22},{34,38},{50,54},{64,68... | collective-permute-start | bytes 49160 | tf_op jit(solution)/shard_map/ppermute | solution.py:275
  28.9 1.3 %collective-permute-start.9 = (bf16[64,128]{1,0:T(8,128)(2,1)S(1)}, bf16[64,128]{1,0:T(8,128)(2,1)S(1)}, u32[]{:S(2)}, u32[]{:S(2)}) collective-permute-start(bf16[64,128]{1,0:T(8,128)(2,1)S(1)} %add_add_fusion.1), channel_id=1, source_target_pairs={{0,12},{16,28},{32,44},{48,60},{2,14},{18,30},{34,46},{50,62},{64,... | collective-permute-start | bytes 49160 | tf_op jit(solution)/shard_map/ppermute | solution.py:275
  30.2 0.8 %collective-permute-done.9 = bf16[64,128]{1,0:T(8,128)(2,1)S(1)} collective-permute-done((bf16[64,128]{1,0:T(8,128)(2,1)S(1)}, bf16[64,128]{1,0:T(8,128)(2,1)S(1)}, u32[]{:S(2)}, u32[]{:S(2)}) %collective-permute-start.9) | collective-permute-done | bytes 16416 | tf_op jit(solution)/shard_map/ppermute | solution.py:275
  31.1 0.4 shard_map.48
  31.4 0.0 copy-start
  31.5 0.0 copy-start.1
  31.5 0.0 copy-start.3
  31.5 22.1 %all_to_all.10.far_ref = bf16[8,1088,128]{2,1,0:T(8,128)(2,1)S(1)} all-to-all(bf16[8,1088,128]{2,1,0:T(8,128)(2,1)S(1)} %shard_map.48), channel_id=1, replica_groups={{0,2,64,66,128,130,192,194},{4,6,68,70,132,134,196,198},{8,10,72,74,136..., dimensions={0} | all-to-all | bytes 4456448 | tf_op jit(solution)/shard_map/all_to_all | solution.py:309
  53.6 0.8 %collective-permute-start.11 = (bf16[8,1088,128]{2,1,0:T(8,128)(2,1)S(1)}, bf16[8,1088,128]{2,1,0:T(8,128)(2,1)S(1)}, u32[]{:S(2)}, u32[]{:S(2)}) collective-permute-start(bf16[8,1088,128]{2,1,0:T(8,128)(2,1)S(1)} %all_to_all.10.far_ref), channel_id=1, source_target_pairs={{0,1},{1,0},{2,3},{3,2},{4,5},{5,4},{6,7},{7,6},{8,9},{9,8},{10,11... | collective-permute-start | bytes 6684680 | tf_op jit(solution)/shard_map/ppermute | solution.py:331
  54.4 7.1 %shard_map.49.refs_0_ = bf16[128,4096]{1,0:T(8,128)(2,1)} custom-call(s32[1]{0:T(128)} %bitcast.block_ref, bf16[128,4096]{1,0:T(8,128)(2,1)S(1)} %copy-done.3, bf16[128,512]{1,0:T(8,128)(2,1)S(1)} %copy-done, bf16[128,512]{1,0:T(8,128)(2,1)S(1)} %copy-done.1, bf16[8,1088,128]{2,1,0:T(8,128)(2,1)S(1)} %all_to_all.10.far_ref), custom_call_target="tpu_custom_call" | custom-call | flops 2415919104 | bytes 4194304 | tf_op jit(solution)/shard_map/pallas_call | solution.py:250
  61.4 6.8 %shard_map.50 = bf16[128,4096]{1,0:T(8,128)(2,1)} custom-call(s32[1]{0:T(128)} %bitcast.block_ref, bf16[128,4096]{1,0:T(8,128)(2,1)S(1)} %copy-done.3, bf16[128,512]{1,0:T(8,128)(2,1)S(1)} %copy-done, bf16[128,512]{1,0:T(8,128)(2,1)S(1)} %copy-done.1, bf16[8,1088,128]{2,1,0:T(8,128)(2,1)S(1)} %collective-permute-done.11.far_ref, ...), custom_call_target="tpu_custom_call", output_to_operand_aliasing={{}: (5, {})} | custom-call | flops 2415919104 | bytes 4194304 | tf_op jit(solution)/shard_map/pallas_call | solution.py:250
  (16 shorter events, 0.1 us)
Async XLA Ops:
  1.0 0.7 %copy-start.2 = (s32[1,4,8]{2,1,0:T(4,128)S(1)}, s32[1,4,8]{2,1,0:T(4,128)}, u32[]{:S(2)}) copy-start(s32[1,4,8]{2,1,0:T(4,128)} %index_ref.1) | copy-start | bytes 388
  2.4 1.7 %collective-permute-start = (bf16[544,128]{1,0:T(8,128)(2,1)S(1)}, bf16[544,128]{1,0:T(8,128)(2,1)S(1)}, u32[]{:S(2)}, u32[]{:S(2)}) collective-permute-start(bf16[544,128]{1,0:T(8,128)(2,1)S(1)} %get-tuple-element.8), channel_id=1, source_target_pairs={{0,1},{1,0},{2,3},{3,2},{4,5},{5,4},{6,7},{7,6},{8,9},{9,8},{10,11... | collective-permute-start | bytes 417800 | tf_op jit(solution)/shard_map/ppermute | solution.py:319
  4.2 2.0 %collective-permute-start.1 = (bf16[128,128]{1,0:T(8,128)(2,1)S(1)}, bf16[128,128]{1,0:T(8,128)(2,1)S(1)}, u32[]{:S(2)}, u32[]{:S(2)}) collective-permute-start(bf16[128,128]{1,0:T(8,128)(2,1)S(1)} %get-tuple-element.9), channel_id=1, source_target_pairs={{0,64},{1,17}} | collective-permute-start | bytes 98312 | tf_op jit(solution)/shard_map/ppermute | solution.py:275
  4.9 1.4 %collective-permute-start.2 = (bf16[128,128]{1,0:T(8,128)(2,1)S(1)}, bf16[128,128]{1,0:T(8,128)(2,1)S(1)}, u32[]{:S(2)}, u32[]{:S(2)}) collective-permute-start(bf16[128,128]{1,0:T(8,128)(2,1)S(1)} %get-tuple-element.11), channel_id=1, source_target_pairs={{0,192},{1,49}} | collective-permute-start | bytes 98312 | tf_op jit(solution)/shard_map/ppermute | solution.py:275
  5.5 0.7 %collective-permute-start.3 = (bf16[128,128]{1,0:T(8,128)(2,1)S(1)}, bf16[128,128]{1,0:T(8,128)(2,1)S(1)}, u32[]{:S(2)}, u32[]{:S(2)}) collective-permute-start(bf16[128,128]{1,0:T(8,128)(2,1)S(1)} %get-tuple-element.10), channel_id=1, source_target_pairs={{0,128},{1,33}} | collective-permute-start | bytes 98312 | tf_op jit(solution)/shard_map/ppermute | solution.py:275
  6.3 12.3 %collective-permute-start.4 = (bf16[64,128]{1,0:T(8,128)(2,1)S(1)}, bf16[64,128]{1,0:T(8,128)(2,1)S(1)}, u32[]{:S(2)}, u32[]{:S(2)}) collective-permute-start(bf16[64,128]{1,0:T(8,128)(2,1)S(1)} %slice.38), channel_id=1, source_target_pairs={{0,2},{64,66},{128,130},{192,194},{1,15},{17,31},{33,47},{49,63}} | collective-permute-start | bytes 49160 | tf_op jit(solution)/shard_map/ppermute | solution.py:275
  7.7 23.4 %all-to-all-start = ((bf16[16,64,128]{2,1,0:T(8,128)(2,1)}), bf16[16,64,128]{2,1,0:T(8,128)(2,1)S(1)}, u32[]{:S(2)}, u32[]{:S(2)}) async-start(bf16[16,64,128]{2,1,0:T(8,128)(2,1)} %shard_map.47), calls=%async_computation | async-start | bytes 524288 | tf_op jit(solution)/shard_map/all_to_all | solution.py:309
  18.6 2.6 %collective-permute-start.5 = (bf16[64,128]{1,0:T(8,128)(2,1)S(1)}, bf16[64,128]{1,0:T(8,128)(2,1)S(1)}, u32[]{:S(2)}, u32[]{:S(2)}) collective-permute-start(bf16[64,128]{1,0:T(8,128)(2,1)S(1)} %slice_add_fusion.2), channel_id=1, source_target_pairs={{0,16},{2,18},{64,80},{66,82},{128,144},{130,146},{192,208},{194,2... | collective-permute-start | bytes 49160 | tf_op jit(solution)/shard_map/ppermute | solution.py:275
  19.2 5.7 %collective-permute-start.6 = (bf16[64,128]{1,0:T(8,128)(2,1)S(1)}, bf16[64,128]{1,0:T(8,128)(2,1)S(1)}, u32[]{:S(2)}, u32[]{:S(2)}) collective-permute-start(bf16[64,128]{1,0:T(8,128)(2,1)S(1)} %slice_add_fusion.2), channel_id=1, source_target_pairs={{0,48},{2,50},{64,112},{66,114},{128,176},{130,178},{192,240},{194... | collective-permute-start | bytes 49160 | tf_op jit(solution)/shard_map/ppermute | solution.py:275
  20.5 4.4 %collective-permute-start.7 = (bf16[64,128]{1,0:T(8,128)(2,1)S(1)}, bf16[64,128]{1,0:T(8,128)(2,1)S(1)}, u32[]{:S(2)}, u32[]{:S(2)}) collective-permute-start(bf16[64,128]{1,0:T(8,128)(2,1)S(1)} %slice_add_fusion.2), channel_id=1, source_target_pairs={{0,32},{2,34},{64,96},{66,98},{128,160},{130,162},{192,224},{194,2... | collective-permute-start | bytes 49160 | tf_op jit(solution)/shard_map/ppermute | solution.py:275
  24.9 5.3 %collective-permute-start.10 = (bf16[64,128]{1,0:T(8,128)(2,1)S(1)}, bf16[64,128]{1,0:T(8,128)(2,1)S(1)}, u32[]{:S(2)}, u32[]{:S(2)}) collective-permute-start(bf16[64,128]{1,0:T(8,128)(2,1)S(1)} %add_add_fusion.1), channel_id=1, source_target_pairs={{0,8},{16,24},{32,40},{48,56},{2,10},{18,26},{34,42},{50,58},{64,7... | collective-permute-start | bytes 49160 | tf_op jit(solution)/shard_map/ppermute | solution.py:275
  27.6 2.6 %collective-permute-start.8 = (bf16[64,128]{1,0:T(8,128)(2,1)S(1)}, bf16[64,128]{1,0:T(8,128)(2,1)S(1)}, u32[]{:S(2)}, u32[]{:S(2)}) collective-permute-start(bf16[64,128]{1,0:T(8,128)(2,1)S(1)} %add_add_fusion.1), channel_id=1, source_target_pairs={{0,4},{16,20},{32,36},{48,52},{2,6},{18,22},{34,38},{50,54},{64,68... | collective-permute-start | bytes 49160 | tf_op jit(solution)/shard_map/ppermute | solution.py:275
  28.9 2.1 %collective-permute-start.9 = (bf16[64,128]{1,0:T(8,128)(2,1)S(1)}, bf16[64,128]{1,0:T(8,128)(2,1)S(1)}, u32[]{:S(2)}, u32[]{:S(2)}) collective-permute-start(bf16[64,128]{1,0:T(8,128)(2,1)S(1)} %add_add_fusion.1), channel_id=1, source_target_pairs={{0,12},{16,28},{32,44},{48,60},{2,14},{18,30},{34,46},{50,62},{64,... | collective-permute-start | bytes 49160 | tf_op jit(solution)/shard_map/ppermute | solution.py:275
  31.4 22.9 %copy-start = (bf16[128,512]{1,0:T(8,128)(2,1)S(1)}, bf16[128,512]{1,0:T(8,128)(2,1)}, u32[]{:S(2)}) copy-start(bf16[128,512]{1,0:T(8,128)(2,1)} %k_ref.3) | copy-start | bytes 393220
  31.5 22.9 %copy-start.1 = (bf16[128,512]{1,0:T(8,128)(2,1)S(1)}, bf16[128,512]{1,0:T(8,128)(2,1)}, u32[]{:S(2)}) copy-start(bf16[128,512]{1,0:T(8,128)(2,1)} %v_ref.3) | copy-start | bytes 393220
  31.5 22.9 %copy-start.3 = (bf16[128,4096]{1,0:T(8,128)(2,1)S(1)}, bf16[128,4096]{1,0:T(8,128)(2,1)}, u32[]{:S(2)}) copy-start(bf16[128,4096]{1,0:T(8,128)(2,1)} %q_ref.3) | copy-start | bytes 3145732
  53.6 7.8 %collective-permute-start.11 = (bf16[8,1088,128]{2,1,0:T(8,128)(2,1)S(1)}, bf16[8,1088,128]{2,1,0:T(8,128)(2,1)S(1)}, u32[]{:S(2)}, u32[]{:S(2)}) collective-permute-start(bf16[8,1088,128]{2,1,0:T(8,128)(2,1)S(1)} %all_to_all.10.far_ref), channel_id=1, source_target_pairs={{0,1},{1,0},{2,3},{3,2},{4,5},{5,4},{6,7},{7,6},{8,9},{9,8},{10,11... | collective-permute-start | bytes 6684680 | tf_op jit(solution)/shard_map/ppermute | solution.py:331
